TPU v7x, 32 devices: a whole 2x2x4 slice. The times are simulated.
32 devices in a mesh: reader: 4 (over y, x), blk: 8 (over z, core).
Axes of the slice: x: 2, y: 2, z: 4, core: 2. Of those that a mesh axis runs over, the one named last changes fastest.
Arguments:
- features: bfloat16 [4096, 512], P(('reader', 'blk')), may hold values from -40 to 40
- cotangent: bfloat16 [4096, 512], P(('reader', 'blk')), may hold values from -6 to 6
- w_query: bfloat16 [512, 512], replicated, may hold values from -0.25 to 0.25
- w_key: bfloat16 [512, 512], replicated, may hold values from -0.25 to 0.25
- w_value: bfloat16 [512, 512], replicated, may hold values from -0.25 to 0.25
- tile_coords: int32 [4, 8, 8, 3], P('reader', 'blk'), may hold values from 0 to 239, as said below
- tile_count: int32 [4, 8], P('reader', 'blk'), may hold values from 1 to 8, as said below
- mask_table: int32 [240, 128, 4], replicated, may hold values from -2147483648 to 2147483647, as said below
Outputs:
- attn_out: bfloat16 [4096, 512], P(('reader', 'blk'))
- grad_features: bfloat16 [4096, 512], P(('reader', 'blk'))
Inputs may be any that keep to these rules, and one draw needn't show every extreme that they name: `tile_coords`: for every r and b the 8 slots name distinct (qb, kb) pairs with qb < 8, kb < 4, p < 240; the first 1 slots are the tiles in which the nodes of segment r * 8 + b meet themselves. `tile_count`: some pair (r, b) uses all 8 slots, and some pair uses the fewest. `mask_table`: each word packs 32 edge bits as a signed int32; each bit is set with probability 1/32.
All inputs are finite; a program needn't handle non-finite values.
Results may differ from a plain program's by a relative error of at most 0.01265.
The roundings to bfloat16 on the way count: a program that leaves them out, or rounds other values in their place, can miss the bound.
Values may be sent and summed in bfloat16 or wider, within the bound.
No kernel may reach another device: no remote copies, remote signals or barrier semaphores. Data moves between devices by JAX's collectives and lax.ppermute only.
A program may use at most 128 MiB of HBM per device.

v0:
```python
import functools

import jax
import jax.numpy as jnp
from jax import lax
from jax.experimental import pallas as pl
from jax.experimental.pallas import tpu as pltpu
from jax.sharding import PartitionSpec as P

HEADS = 8
NEG_FILL = -1e30
NT = (((1,), (1,)), ((), ()))
NN = (((1,), (0,)), ((), ()))
TILES = 2
LIST_ROWS = 16
VMEM_SOME = 40 * 1024 * 1024
VMEM_MOST = 58 * 1024 * 1024


def dot(a, b, dims=NN):
    return lax.dot_general(a, b, dims, preferred_element_type=jnp.float32)


def pair_stack(rows):
    lane = lax.broadcasted_iota(jnp.int32, rows.shape, 1)
    half = rows.shape[1] // 2
    zero = jnp.zeros_like(rows)
    return jnp.concatenate([jnp.where(lane < half, rows, zero), jnp.where(lane >= half, rows, zero)], 0)


def tile_bias(words, pattern, diag):
    count, size = words.shape
    keys = lax.broadcasted_iota(jnp.int32, (size, size), 0)
    queries = lax.broadcasted_iota(jnp.int32, (size, size), 1)
    spread = jnp.concatenate(
        [jnp.broadcast_to(words[g : g + 1], (size // count, size)) for g in range(count)], 0
    )
    bits = jnp.right_shift(spread, keys & 31) & 1
    same = keys - queries == jnp.where(diag, 0, 2 * size)
    return jnp.where((bits == 1) | same, jnp.where(pattern < 0, NEG_FILL, 0.0), NEG_FILL)


class Layout:
    def __init__(self, readers, blks, cap):
        self.readers, self.blks, self.cap = readers, blks, cap
        self.reader, self.blk = lax.axis_index("reader"), lax.axis_index("blk")
        self.me = self.reader * blks + self.blk

    def apart(self, device):
        far = jnp.bitwise_xor(device, self.me)
        reader, blk = far // self.blks, lax.rem(far, self.blks)
        return reader, blk // 2, blk & 1

    def row_place(self, device):
        reader, line, core = self.apart(device)
        near = line == 0
        group = jnp.where(near, 0, reader) + self.readers * core
        index = jnp.where(reader == 0, self.readers, 0) + line - 1
        return group, jnp.where(near, reader, index)

    def half_place(self, bit, device):
        reader, line, core = self.apart(device)
        first = jnp.right_shift(reader, bit) & 1
        top = (self.blks // 2 - 1).bit_length() - 1
        line = sum((jnp.right_shift(line, top - at) & 1) << at for at in range(top + 1))
        low = reader & ((1 << bit) - 1)
        rest = low + (jnp.right_shift(reader, bit + 1) << bit)
        return rest + self.readers // 2 * core, 2 * line + first


def start_copy(place, refs, make):
    group, where = place
    for g, ref in enumerate(refs):

        @pl.when(group == g)
        def _():
            make(ref.at[where]).start()


def pack_kernel(own_hbm, coords_hbm, count_hbm, out_ref, coords_ref, count_ref, sems):
    block = own_hbm.shape[0]
    cap = coords_ref.shape[3]
    copies = [
        pltpu.make_async_copy(coords_hbm, coords_ref, sems.at[0]),
        pltpu.make_async_copy(count_hbm, count_ref, sems.at[1]),
        pltpu.make_async_copy(own_hbm, out_ref.at[0, pl.ds(0, block)], sems.at[2]),
    ]
    for copy in copies:
        copy.start()
    copies[0].wait()
    copies[1].wait()
    lane = lax.broadcasted_iota(jnp.int32, (LIST_ROWS, out_ref.shape[2]), 1)
    row = jnp.zeros(lane.shape, jnp.int32)
    for column in range(3):
        for slot in range(cap):
            row = jnp.where(lane == column * cap + slot, coords_ref[0, column, 0, slot], row)
    row = jnp.where(lane == 3 * cap, count_ref[0, 0], row)
    out_ref[0, block:] = row.astype(jnp.float32).astype(jnp.bfloat16)
    copies[2].wait()


def scan_list(lists_ref, cap, row, column, wanted, found, out_ref, block_of):
    def one_slot(slot, found):
        out_ref[2 * found + 1] = block_of(lists_ref[row, (1 - column) * cap + slot])
        out_ref[2 * found + 2] = lists_ref[row, 2 * cap + slot]
        return found + jnp.where(lists_ref[row, column * cap + slot] == wanted, 1, 0)

    return lax.fori_loop(0, lists_ref[row, 3 * cap], one_slot, found)


def close_work(found, out_ref):
    out_ref[2 * found + 1] = out_ref[2 * found - 1]
    out_ref[2 * found + 2] = -1
    out_ref[0] = (found + 1) // 2


def query_work_kernel(sizes, lists_hbm, work_ref, lists_ref, sem):
    readers, blks, cap = sizes
    layout = Layout(*sizes)
    copy = pltpu.make_async_copy(lists_hbm, lists_ref, sem)
    copy.start()
    copy.wait()

    def one(k, found):
        blk = jnp.bitwise_xor(k, layout.blk)
        row = k // 2 + (k & 1) * (blks // 2)
        put = lambda other: other * blks + blk
        return scan_list(lists_ref, cap, row, 0, layout.blk, found, work_ref, put)

    close_work(lax.fori_loop(0, blks, one, 0), work_ref)


def key_work_kernel(sizes, lists_hbm, work_ref, lists_ref, sem):
    readers, blks, cap = sizes
    layout = Layout(*sizes)
    copy = pltpu.make_async_copy(lists_hbm, lists_ref, sem)
    copy.start()
    copy.wait()

    def one(k, found):
        reader = jnp.bitwise_xor(k, layout.reader)
        put = lambda other: reader * blks + other
        return scan_list(lists_ref, cap, k, 1, layout.reader, found, work_ref, put)

    close_work(lax.fori_loop(0, readers, one, 0), work_ref)


def load(pairs, sems, first=0):
    copies = [pltpu.make_async_copy(src, into, sems.at[first + k]) for k, (src, into) in enumerate(pairs)]
    for copy in copies:
        copy.start()
    return copies


def prepare_kernel(
    own_hbm, cot_hbm, wq_hbm, wk_hbm, wv_hbm,
    query_stack_ref, cot_stack_ref, key_ref, value_ref, wqt_ref, wkt_ref, wvt_ref,
    own_ref, cot_ref, wq_ref, wk_ref, wv_ref, sems,
):
    loads = load((
        (own_hbm, own_ref), (wq_hbm, wq_ref), (wk_hbm, wk_ref), (wv_hbm, wv_ref), (cot_hbm, cot_ref),
    ), sems)
    for copy in loads:
        copy.wait()
    head = own_ref.shape[1] // HEADS
    queries = dot(own_ref[...], wq_ref[...]).astype(jnp.bfloat16) * jnp.bfloat16(head**-0.5)
    for p in range(HEADS // 2):
        pair = slice(2 * head * p, 2 * head * (p + 1))
        query_stack_ref[p] = pair_stack(queries[:, pair]).T
        cot_stack_ref[p] = pair_stack(cot_ref[:, pair]).T
    key_ref[...] = dot(own_ref[...], wk_ref[...]).astype(jnp.bfloat16)
    value_ref[...] = dot(own_ref[...], wv_ref[...]).astype(jnp.bfloat16)
    wqt_ref[...] = wq_ref[...].T
    wkt_ref[...] = wk_ref[...].T
    wvt_ref[...] = wv_ref[...].T


def step_entry(work_ref, index):
    at = 1 + 2 * TILES * index
    return [work_ref[at + 2 * t] for t in range(TILES)], [work_ref[at + 2 * t + 1] for t in range(TILES)]


def run_steps(work_ref, start, wait, body):
    total = work_ref[0]

    def step(index, carry):
        @pl.when(index + 1 < total)
        def _():
            start(lax.rem(index + 1, 2), *step_entry(work_ref, index + 1))

        slot = lax.rem(index, 2)
        wait(slot)
        body(slot, *step_entry(work_ref, index), index)
        return carry

    lax.fori_loop(0, total, step, 0)


def first_step(work_ref, start):
    start(0, *step_entry(work_ref, 0))


class Rows:
    def __init__(self, layout, groups, mask_ref, buf, words, sems, block):
        self.layout, self.groups, self.mask_ref = layout, groups, mask_ref
        self.buf, self.words, self.sems, self.block = buf, words, sems, block

    def rows(self, slot, t):
        into = self.buf.at[slot, pl.ds(t * self.block, self.block)]
        return lambda src: pltpu.make_async_copy(src, into, self.sems.at[slot, t, 0])

    def mask(self, slot, t, pattern):
        return pltpu.make_async_copy(self.mask_ref.at[pattern], self.words.at[slot, t], self.sems.at[slot, t, 1])

    def start(self, slot, blocks, patterns):
        for t in range(TILES):
            start_copy(self.layout.row_place(blocks[t]), self.groups, self.rows(slot, t))
            self.mask(slot, t, jnp.maximum(patterns[t], 0)).start()

    def wait(self, slot):
        for t in range(TILES):
            self.rows(slot, t)(self.groups[0].at[0]).wait()
            self.mask(slot, t, 0).wait()

    def bias(self, slot, blocks, patterns):
        parts = [
            tile_bias(self.words[slot, t], patterns[t], blocks[t] == self.layout.me) for t in range(TILES)
        ]
        return jnp.concatenate(parts, 0)


def forward_kernel(sizes, work_ref, stack_ref, cot_ref, wk_ref, wvt_ref, mask_ref, *refs):
    count = 2 * sizes[0]
    groups, refs = refs[:count], refs[count:]
    out_ref, sent_ref, stats_ref, buf, words, bias_ref, max_ref, sum_ref, acc_ref, score_ref, sems = refs
    layout = Layout(*sizes)
    block, width = cot_ref.shape
    head = width // HEADS
    rows_in = Rows(layout, groups, mask_ref, buf, words, sems, block)
    first_step(work_ref, rows_in.start)
    max_ref[...] = jnp.full(max_ref.shape, NEG_FILL, jnp.float32)
    sum_ref[...] = jnp.zeros(sum_ref.shape, jnp.float32)
    acc_ref[...] = jnp.zeros(acc_ref.shape, jnp.float32)

    def tiles(slot, blocks, patterns, index):
        rows = buf[slot]
        keys = dot(rows, wk_ref[...]).astype(jnp.bfloat16)
        values = dot(wvt_ref[...], rows, NT).astype(jnp.bfloat16)
        bias_ref[...] = rows_in.bias(slot, blocks, patterns)
        for p in range(HEADS // 2):
            scores = dot(keys[:, 2 * head * p : 2 * head * (p + 1)], stack_ref[p])
            for e in range(2):
                score_ref[2 * p + e] = scores[:, block * e : block * (e + 1)] + bias_ref[...]
        for h in range(HEADS):
            s = score_ref[h]
            old = max_ref[h : h + 1]
            new = jnp.maximum(old, jnp.max(s, axis=0, keepdims=True))
            fade = jnp.exp(old - new)
            expo = jnp.exp(s - new)
            max_ref[h : h + 1] = new
            sum_ref[h : h + 1] = sum_ref[h : h + 1] * fade + jnp.sum(expo, axis=0, keepdims=True)
            at = slice(head * h, head * (h + 1))
            acc_ref[at] = acc_ref[at] * fade + dot(values[at], expo.astype(jnp.bfloat16))

    run_steps(work_ref, rows_in.start, rows_in.wait, tiles)
    inverse = 1.0 / sum_ref[...]
    cot = cot_ref[...].astype(jnp.float32).T
    stats_ref[0:HEADS] = max_ref[...] + jnp.log(sum_ref[...])
    for h in range(HEADS):
        at = slice(head * h, head * (h + 1))
        outputs = acc_ref[at] * inverse[h : h + 1]
        acc_ref[at] = outputs
        stats_ref[HEADS + h : HEADS + h + 1] = jnp.sum(outputs * cot[at], axis=0, keepdims=True)
    sent_ref[...] = jnp.broadcast_to(stats_ref[...], sent_ref.shape)
    out_ref[...] = acc_ref[...].T.astype(out_ref.dtype)


def tile_grads(scores, d_probs, lse, delta):
    prob = jnp.exp(scores - lse)
    return prob.astype(jnp.bfloat16), (prob * (d_probs - delta)).astype(jnp.bfloat16)


def query_grad_kernel(
    sizes, work_ref, stack_hbm, cot_stack_hbm, stats_hbm, wqt_hbm, wk_hbm, wkt_hbm, wv_hbm, mask_ref, *refs
):
    count = 2 * sizes[0]
    groups, refs = refs[:count], refs[count:]
    part_ref, stack_ref, cot_stack_ref, stats_ref, wqt_ref, wk_ref, wkt_ref, wv_ref = refs[:8]
    buf, words, bias_ref, acc_ref, score_ref, d_prob_ref, sems, w_sems = refs[8:]
    layout = Layout(*sizes)
    block, width = part_ref.shape
    head = width // HEADS
    rows_in = Rows(layout, groups, mask_ref, buf, words, sems, block)
    first_step(work_ref, rows_in.start)
    loads = load((
        (wk_hbm, wk_ref), (stack_hbm, stack_ref), (wv_hbm, wv_ref), (cot_stack_hbm, cot_stack_ref),
        (wkt_hbm, wkt_ref), (stats_hbm.at[0], stats_ref), (wqt_hbm, wqt_ref),
    ), w_sems)
    acc_ref[...] = jnp.zeros(acc_ref.shape, jnp.float32)
    for copy in loads[:6]:
        copy.wait()

    def tiles(slot, blocks, patterns, index):
        rows = buf[slot]
        keys = dot(rows, wk_ref[...]).astype(jnp.bfloat16)
        values = dot(rows, wv_ref[...]).astype(jnp.bfloat16)
        keys_t = dot(wkt_ref[...], rows, NT).astype(jnp.bfloat16)
        bias_ref[...] = rows_in.bias(slot, blocks, patterns)
        for p in range(HEADS // 2):
            pair = slice(2 * head * p, 2 * head * (p + 1))
            scores = dot(keys[:, pair], stack_ref[p])
            d_probs = dot(values[:, pair], cot_stack_ref[p])
            for e in range(2):
                of = slice(block * e, block * (e + 1))
                score_ref[2 * p + e] = scores[:, of] + bias_ref[...]
                d_prob_ref[2 * p + e] = d_probs[:, of]
        for h in range(HEADS):
            _, d_scores = tile_grads(
                score_ref[h], d_prob_ref[h], stats_ref[h : h + 1], stats_ref[HEADS + h : HEADS + h + 1]
            )
            at = slice(head * h, head * (h + 1))
            acc_ref[at] += dot(keys_t[at], d_scores)

    run_steps(work_ref, rows_in.start, rows_in.wait, tiles)
    loads[6].wait()
    grad = (acc_ref[...].T * (head**-0.5)).astype(jnp.bfloat16)
    part_ref[...] = dot(grad, wqt_ref[...])


def key_grad_kernel(
    sizes, bits, work_ref, key_hbm, value_hbm, wq_hbm, wkt_hbm, wvt_hbm, part_hbm, mask_ref, stats_all_ref, *refs
):
    readers = sizes[0]
    count = 2 * readers
    groups, refs = refs[:count], refs[count:]
    halves, refs = (refs[:readers], refs[readers : 2 * readers]), refs[2 * readers :]
    out_ref, key_ref, value_ref, part_ref, wq_ref, wkt_ref, wvt_ref, buf, words, cot_buf, stats, bias_ref = refs[:12]
    query_stack_ref, cot_stack_ref, score_ref, d_prob_ref, key_acc, value_acc, sems, c_sems, w_sems = refs[12:]
    layout = Layout(*sizes)
    block, width = out_ref.shape
    head = width // HEADS
    rows_in = Rows(layout, groups, mask_ref, buf, words, sems, block)

    def half_copy(slot, t, k):
        into = cot_buf.at[slot, pl.ds(t * block + block // 2 * k, block // 2)]
        return lambda src: pltpu.make_async_copy(src, into, c_sems.at[slot, t, k])

    def stats_copy(slot, t, query):
        return pltpu.make_async_copy(stats_all_ref.at[query], stats.at[slot, t], c_sems.at[slot, t, 2])

    def start(slot, blocks, patterns):
        rows_in.start(slot, blocks, patterns)
        for t in range(TILES):
            stats_copy(slot, t, blocks[t]).start()
            for k in range(2):
                start_copy(layout.half_place(bits[k], blocks[t]), halves[k], half_copy(slot, t, k))

    def wait(slot):
        rows_in.wait(slot)
        for t in range(TILES):
            stats_copy(slot, t, 0).wait()
            for k in range(2):
                half_copy(slot, t, k)(halves[k][0].at[0]).wait()

    first_step(work_ref, start)
    loads = load(((wq_hbm, wq_ref), (key_hbm, key_ref), (value_hbm, value_ref)), w_sems)
    key_acc[...] = jnp.zeros(key_acc.shape, jnp.float32)
    value_acc[...] = jnp.zeros(value_acc.shape, jnp.float32)
    for copy in loads:
        copy.wait()
    loads = load(((wkt_hbm, wkt_ref), (wvt_hbm, wvt_ref), (part_hbm, part_ref)), w_sems, 3)

    def tiles(slot, blocks, patterns, index):
        queries = dot(buf[slot], wq_ref[...]).astype(jnp.bfloat16) * jnp.bfloat16(head**-0.5)
        bias_ref[...] = rows_in.bias(slot, blocks, patterns)
        cots = cot_buf[slot]
        pairs = [slice(2 * head * p, 2 * head * (p + 1)) for p in range(HEADS // 2)]
        of_tile = [slice(block * t, block * (t + 1)) for t in range(TILES)]
        for p, pair in enumerate(pairs):
            query_stack_ref[p] = jnp.concatenate([pair_stack(queries[of, pair]) for of in of_tile], 0)
            cot_stack_ref[p] = jnp.concatenate([pair_stack(cots[of, pair]) for of in of_tile], 0)
            score_ref[p] = dot(key_ref[:, pair], query_stack_ref[p], NT)
            d_prob_ref[p] = dot(value_ref[:, pair], cot_stack_ref[p], NT)
        for p, pair in enumerate(pairs):
            probs, d_scores = [], []
            for t in range(TILES):
                for e in range(2):
                    h = 2 * p + e
                    of = slice(block * (2 * t + e), block * (2 * t + e + 1))
                    prob, d_score = tile_grads(
                        score_ref[p, :, of] + bias_ref[of_tile[t]], d_prob_ref[p, :, of], stats[slot, t, h : h + 1],
                        stats[slot, t, HEADS + h : HEADS + h + 1],
                    )
                    probs.append(prob)
                    d_scores.append(d_score)
            value_acc[:, pair] += dot(jnp.concatenate(probs, 1), cot_stack_ref[p])
            key_acc[:, pair] += dot(jnp.concatenate(d_scores, 1), query_stack_ref[p])

    run_steps(work_ref, start, wait, tiles)
    for copy in loads:
        copy.wait()
    grad = part_ref[...] + dot(key_acc[...].astype(jnp.bfloat16), wkt_ref[...])
    grad = grad + dot(value_acc[...].astype(jnp.bfloat16), wvt_ref[...])
    out_ref[...] = grad.astype(out_ref.dtype)


VMEM = pl.BlockSpec(memory_space=pltpu.VMEM)
SMEM = pl.BlockSpec(memory_space=pltpu.SMEM)
HBM = pl.BlockSpec(memory_space=pltpu.HBM)


def swap(block, mask):
    axes = ("reader", "blk")
    count = lax.axis_size("reader") * lax.axis_size("blk")
    return lax.ppermute(block, axes, [(i, i ^ mask) for i in range(count)])


def after(value, *others):
    return lax.optimization_barrier((value, *others))[0]


def local(features, cotangent, w_query, w_key, w_value, tile_coords, tile_count, mask_table):
    block, width = features.shape
    readers, blks, cap = lax.axis_size("reader"), lax.axis_size("blk"), tile_coords.shape[2]
    assert block == mask_table.shape[1] and 3 * cap < 128
    sizes = (readers, blks, cap)
    devices, lines = readers * blks, blks // 2
    f32, bf16, i32 = jnp.float32, jnp.bfloat16, jnp.int32
    shape = jax.ShapeDtypeStruct
    masks = mask_table.transpose(0, 2, 1)
    words = masks.shape[1]
    head = width // HEADS
    half = block // 2
    some = pltpu.CompilerParams(vmem_limit_bytes=VMEM_SOME)
    most = pltpu.CompilerParams(vmem_limit_bytes=VMEM_MOST)
    axes = ("reader", "blk")

    def cost(tiles):
        return pl.CostEstimate(flops=tiles * 200_000_000, bytes_accessed=4_000_000, transcendentals=tiles * 131072)

    packed = pl.pallas_call(
        pack_kernel,
        out_shape=shape((1, block + LIST_ROWS, width), bf16),
        in_specs=[HBM, HBM, HBM],
        out_specs=VMEM,
        scratch_shapes=[
            pltpu.SMEM((1, 3, 1, cap), i32), pltpu.SMEM((1, 1), i32), pltpu.SemaphoreType.DMA((3,)),
        ],
        compiler_params=most,
        name="pack",
    )(features, tile_coords.transpose(0, 3, 1, 2), tile_count)
    lined = [packed] + [swap(packed, 2 * k) for k in range(1, lines)]

    nearest_first = sorted(range(1, readers), key=lambda k: (k.bit_count(), k))

    def to_readers(block):
        there = {k: swap(block, blks * k) for k in nearest_first}
        return [there[k] for k in range(1, readers)]

    columns = [packed] + to_readers(packed)

    bits = (0, (readers - 1).bit_length() - 1)
    cot_parts = [cotangent[None, half * k : half * (k + 1)] for k in range(2)]
    cot_other = [swap(part, blks << bit) for part, bit in zip(cot_parts, bits)]

    column_lists = jnp.concatenate([entry[:, block:, :128] for entry in columns], 0)

    def work(kernel, lists, count, name):
        return pl.pallas_call(
            functools.partial(kernel, sizes),
            out_shape=shape((2 * count * cap + 5,), i32),
            in_specs=[HBM],
            out_specs=SMEM,
            scratch_shapes=[pltpu.SMEM((count, 128), i32), pltpu.SemaphoreType.DMA],
            compiler_params=some,
            cost_estimate=cost(1),
            name=name,
        )(lists[:, 0].astype(i32))

    key_work = work(key_work_kernel, column_lists, readers, "key_work")

    stacks = shape((HEADS // 2, 2 * head, 2 * block), bf16)
    own = shape((block, width), bf16)
    square = shape((width, width), bf16)
    weight = pltpu.VMEM((width, width), bf16)
    rows_low, rows_wide = pltpu.VMEM((block, width), bf16), pltpu.VMEM((block, width), f32)
    prepared = pl.pallas_call(
        prepare_kernel,
        out_shape=(stacks, stacks, own, own, square, square, square),
        in_specs=[HBM] * 5,
        out_specs=(VMEM,) * 7,
        scratch_shapes=[rows_low, rows_low, weight, weight, weight, pltpu.SemaphoreType.DMA((5,))],
        compiler_params=most,
        cost_estimate=cost(2),
        name="prepare",
    )(after(features, columns), cotangent, w_query, w_key, w_value)
    query_stack, cot_stack, keys, values, w_query_t, w_key_t, w_value_t = prepared

    line = jnp.concatenate([entry[:, :block] for entry in lined[1:]], 0)
    line = after(line, columns, cot_other)
    there = to_readers(line)
    near = jnp.concatenate([entry[:, :block] for entry in columns] + [line], 0)

    pairs = [part for k in range(2) for part in (cot_parts[k], cot_other[k])]
    pieces = [after(jnp.concatenate(pairs, 0), near)]
    done_first = (key_work, prepared)
    mask = blks // 2
    while mask > 1:
        pieces += [swap(after(piece, done_first) if at else piece, mask) for at, piece in enumerate(pieces)]
        mask //= 2

    line_lists = jnp.concatenate([entry[:, block:, :128] for entry in lined], 0)
    line_lists = after(line_lists, pieces[lines // 2])
    row_lists = jnp.concatenate([line_lists, swap(line_lists, 1)], 0)
    query_work = work(query_work_kernel, row_lists, blks, "query_work")
    here = [near] + there
    rows_all = here + [swap(group, 1) for group in here]

    cots_here = []
    for k in range(2):
        part = jnp.concatenate([piece[2 * k : 2 * k + 2] for piece in pieces], 0)
        masks_left = [m for m in range(1, readers) if not m >> bits[k] & 1]
        cots_here.append((part, [swap(after(part, here), blks * m) for m in masks_left]))

    stack_space = pltpu.VMEM(stacks.shape, bf16)
    buffer = pltpu.VMEM((2, TILES * block, width), bf16)
    word_buffer = pltpu.VMEM((2, TILES, words, block), i32)
    bias = pltpu.VMEM((TILES * block, block), f32)
    turned = pltpu.VMEM((width, block), f32)
    per_head = pltpu.VMEM((HEADS, block), f32)
    own_stats = pltpu.VMEM((2 * HEADS, block), f32)
    met = pltpu.VMEM((HEADS, TILES * block, block), f32)
    pair_met = pltpu.VMEM((HEADS // 2, block, 2 * TILES * block), f32)
    pair_rows = pltpu.VMEM((HEADS // 2, 2 * TILES * block, 2 * head), bf16)
    row_sems = pltpu.SemaphoreType.DMA((2, TILES, 2))

    attn_out, stats = pl.pallas_call(
        functools.partial(forward_kernel, sizes),
        out_shape=(own, shape((devices, 2 * HEADS, block), f32)),
        in_specs=[SMEM] + [VMEM] * 4 + [HBM] * (1 + 2 * readers),
        out_specs=(VMEM, VMEM),
        scratch_shapes=[own_stats, buffer, word_buffer, bias, per_head, per_head, turned, met, row_sems],
        compiler_params=some,
        cost_estimate=cost(5),
        name="forward",
    )(query_work, query_stack, cotangent, w_key, w_value_t, masks, *rows_all)

    stats_all = lax.all_to_all(stats, axes, 0, 0, tiled=True)

    query_part = pl.pallas_call(
        functools.partial(query_grad_kernel, sizes),
        out_shape=shape((block, width), f32),
        in_specs=[SMEM] + [HBM] * (8 + 2 * readers),
        out_specs=VMEM,
        scratch_shapes=[
            stack_space, stack_space, own_stats, weight, weight, weight, weight, buffer, word_buffer, bias, turned,
            met, met, row_sems, pltpu.SemaphoreType.DMA((7,)),
        ],
        compiler_params=most,
        cost_estimate=cost(5),
        name="query_grad",
    )(query_work, query_stack, cot_stack, stats, w_query_t, w_key, w_key_t, w_value, masks, *rows_all)

    cots_all = []
    for first, rest in cots_here:
        cots_all += [first, *rest, swap(after(first, stats), 1)]
        cots_all += [swap(after(part, stats_all, query_part), 1) for part in rest]

    grad_features = pl.pallas_call(
        functools.partial(key_grad_kernel, sizes, bits),
        out_shape=own,
        in_specs=[SMEM] + [HBM] * (8 + 4 * readers),
        out_specs=VMEM,
        scratch_shapes=[
            rows_low, rows_low, rows_wide, weight, weight, weight,
            buffer, word_buffer, buffer, pltpu.VMEM((2, TILES, 2 * HEADS, block), f32), bias,
            pair_rows, pair_rows, pair_met, pair_met, rows_wide, rows_wide,
            row_sems, pltpu.SemaphoreType.DMA((2, TILES, 3)), pltpu.SemaphoreType.DMA((6,)),
        ],
        compiler_params=most,
        cost_estimate=cost(5),
        name="key_grad",
    )(key_work, keys, values, w_query, w_key_t, w_value_t, query_part, masks, stats_all, *rows_all, *cots_all)
    return attn_out, grad_features


def solution(mesh):
    return jax.shard_map(
        local,
        mesh=mesh,
        in_specs=(
            P(("reader", "blk"), None),
            P(("reader", "blk"), None),
            P(),
            P(),
            P(),
            P("reader", "blk", None, None),
            P("reader", "blk"),
            P(),
        ),
        out_specs=(P(("reader", "blk"), None), P(("reader", "blk"), None)),
        check_vma=False,
    )
```

profile of v0, /device:TPU:0, one launch (start us, length us, event | category | flops | bytes accessed | tf_op | source)
XLA Modules:
  0.0 79.5 jit_solution(7320809569862572642)
XLA Ops:
  1.3 0.0 copy-start.11
  1.3 1.6 %pack.1 = bf16[1,144,512]{2,1,0:T(8,128)(2,1)} custom-call(bf16[128,512]{1,0:T(8,128)(2,1)} %own_hbm.2, s32[1,3,1,8]{3,2,1,0:T(1,128)} %bitcast.13, s32[1,1]{1,0:T(1,128)S(6)} %copy.14.count_hbm), custom_call_target="tpu_custom_call" | custom-call | tf_op jit(solution)/shard_map/pack/pallas_call | solution.py:441
  2.9 5.1 %collective-permute-start.2 = (bf16[1,144,512]{2,1,0:T(8,128)(2,1)}, bf16[1,144,512]{2,1,0:T(8,128)(2,1)S(1)}, u32[]{:S(2)}, u32[]{:S(2)}) collective-permute-start(bf16[1,144,512]{2,1,0:T(8,128)(2,1)} %pack.1), channel_id=1, source_target_pairs={{0,6},{1,7},{2,4},{3,5},{4,2},{5,3},{6,0},{7,1},{8,14},{9,15},{10,... | collective-permute-start | bytes 442376 | tf_op jit(solution)/shard_map/ppermute | solution.py:415
  8.0 0.6 collective-permute-start
  8.7 1.7 %collective-permute-start.3 = (bf16[1,64,512]{2,1,0:T(8,128)(2,1)S(1)}, bf16[1,64,512]{2,1,0:T(8,128)(2,1)S(1)}, u32[]{:S(2)}, u32[]{:S(2)}) collective-permute-start(bf16[1,64,512]{2,1,0:T(8,128)(2,1)S(1)} %get-tuple-element.50), channel_id=1, source_target_pairs={{0,8},{1,9},{2,10},{3,11},{4,12},{5,13},{6,14},{7,15},{8,0},{9,1},... | collective-permute-start | bytes 196616 | tf_op jit(solution)/shard_map/ppermute | solution.py:415
  10.4 1.5 %collective-permute-start.4 = (bf16[1,64,512]{2,1,0:T(8,128)(2,1)S(1)}, bf16[1,64,512]{2,1,0:T(8,128)(2,1)S(1)}, u32[]{:S(2)}, u32[]{:S(2)}) collective-permute-start(bf16[1,64,512]{2,1,0:T(8,128)(2,1)S(1)} %get-tuple-element.51), channel_id=1, source_target_pairs={{0,16},{1,17},{2,18},{3,19},{4,20},{5,21},{6,22},{7,23},{8,24},{9,... | collective-permute-start | bytes 196616 | tf_op jit(solution)/shard_map/ppermute | solution.py:415
  12.0 1.1 %collective-permute-done.3 = bf16[1,64,512]{2,1,0:T(8,128)(2,1)S(1)} collective-permute-done((bf16[1,64,512]{2,1,0:T(8,128)(2,1)S(1)}, bf16[1,64,512]{2,1,0:T(8,128)(2,1)S(1)}, u32[]{:S(2)}, u32[]{:S(2)}) %collective-permute-start.3) | collective-permute-done | bytes 65568 | tf_op jit(solution)/shard_map/ppermute | solution.py:415
  13.0 2.6 %collective-permute-start.7 = (bf16[1,144,512]{2,1,0:T(8,128)(2,1)S(1)}, bf16[1,144,512]{2,1,0:T(8,128)(2,1)S(1)}, u32[]{:S(2)}, u32[]{:S(2)}) collective-permute-start(bf16[1,144,512]{2,1,0:T(8,128)(2,1)S(1)} %copy-done.19), channel_id=1, source_target_pairs={{0,24},{1,25},{2,26},{3,27},{4,28},{5,29},{6,30},{7,31},{8,16},{9,... | collective-permute-start | bytes 442376 | tf_op jit(solution)/shard_map/ppermute | solution.py:415
  15.6 0.6 collective-permute-start.6
  16.2 0.0 collective-permute-done.2
  16.2 0.5 collective-permute-start.5
  16.8 0.1 copy-done.24
  16.9 3.9 %collective-permute-done.1 = bf16[1,144,512]{2,1,0:T(8,128)(2,1)S(1)} collective-permute-done((bf16[1,144,512]{2,1,0:T(8,128)(2,1)}, bf16[1,144,512]{2,1,0:T(8,128)(2,1)S(1)}, u32[]{:S(2)}, u32[]{:S(2)}) %collective-permute-start.1) | collective-permute-done | bytes 147488 | tf_op jit(solution)/shard_map/ppermute | solution.py:415
  20.7 0.0 slice-start
  20.8 0.9 %slice-done = bf16[1,128,512]{2,1,0:T(8,128)(2,1)S(1)} async-done(((bf16[1,144,512]{2,1,0:T(8,128)(2,1)}), bf16[1,128,512]{2,1,0:T(8,128)(2,1)S(1)}, s32[]{:S(2)}) %slice-start) | async-done | bytes 131096 | tf_op jit(solution)/shard_map/slice | solution.py:499
  21.7 0.0 collective-permute-done.7
  21.7 2.5 %collective-permute-start.12 = (bf16[3,128,512]{2,1,0:T(8,128)(2,1)S(1)}, bf16[3,128,512]{2,1,0:T(8,128)(2,1)S(1)}, u32[]{:S(2)}, u32[]{:S(2)}) collective-permute-start(bf16[3,128,512]{2,1,0:T(8,128)(2,1)S(1)} %pad_maximum_fusion.2), channel_id=1, source_target_pairs={{0,24},{1,25},{2,26},{3,27},{4,28},{5,29},{6,30},{7,31},{8,16},{9,... | collective-permute-start | bytes 1179656 | tf_op jit(solution)/shard_map/ppermute | solution.py:415
  24.2 0.5 collective-permute-start.11
  24.8 0.5 collective-permute-start.10
  25.4 4.6 %collective-permute-start.17 = (bf16[4,64,512]{2,1,0:T(8,128)(2,1)S(1)}, bf16[4,64,512]{2,1,0:T(8,128)(2,1)S(1)}, u32[]{:S(2)}, u32[]{:S(2)}) collective-permute-start(bf16[4,64,512]{2,1,0:T(8,128)(2,1)S(1)} %pad_maximum_fusion.3), channel_id=1, source_target_pairs={{0,4},{1,5},{2,6},{3,7},{4,0},{5,1},{6,2},{7,3},{8,12},{9,13},{10,... | collective-permute-start | bytes 786440 | tf_op jit(solution)/shard_map/ppermute | solution.py:415
  30.0 0.0 collective-permute-start.8
  30.1 3.3 %prepare.1 = (bf16[4,128,256]{2,1,0:T(8,128)(2,1)}, bf16[4,128,256]{2,1,0:T(8,128)(2,1)}, bf16[128,512]{1,0:T(8,128)(2,1)}, bf16[128,512]{1,0:T(8,128)(2,1)}, bf...) custom-call(bf16[128,512]{1,0:T(8,128)(2,1)} %own_hbm.2, bf16[128,512]{1,0:T(8,128)(2,1)} %cot_ref.1, ...), custom_call_target="tpu_custom_call" | custom-call | flops 400000000 | bytes 4000000 | tf_op jit(solution)/shard_map/prepare/pallas_call | solution.py:487
  33.4 1.4 %key_work.1.work_ref = s32[69]{0:T(128)S(1)} custom-call(s32[4,128]{1,0:T(4,128)S(1)} %bitcast.12), custom_call_target="tpu_custom_call" | custom-call | flops 200000000 | bytes 4000000 | tf_op jit(solution)/shard_map/key_work/pallas_call | solution.py:469
  34.9 0.5 copy-done.15
  35.4 4.0 %collective-permute-done.8 = bf16[4,64,512]{2,1,0:T(8,128)(2,1)S(1)} collective-permute-done((bf16[4,64,512]{2,1,0:T(8,128)(2,1)S(1)}, bf16[4,64,512]{2,1,0:T(8,128)(2,1)S(1)}, u32[]{:S(2)}, u32[]{:S(2)}) %collective-permute-start.8) | collective-permute-done | bytes 262176 | tf_op jit(solution)/shard_map/ppermute | solution.py:415
  39.3 0.0 collective-permute-start.13
  39.3 0.0 collective-permute-done.17
  39.4 0.5 collective-permute-start.9
  39.9 2.0 %collective-permute-done.9 = bf16[4,16,128]{2,1,0:T(8,128)(2,1)S(1)} collective-permute-done((bf16[4,16,128]{2,1,0:T(8,128)(2,1)S(1)}, bf16[4,16,128]{2,1,0:T(8,128)(2,1)S(1)}, u32[]{:S(2)}, u32[]{:S(2)}) %collective-permute-start.9) | collective-permute-done | bytes 16416 | tf_op jit(solution)/shard_map/ppermute | solution.py:415
  41.8 0.0 collective-permute-start.18
  41.9 1.6 %query_work.1.work_ref = s32[133]{0:T(256)S(1)} custom-call(s32[8,128]{1,0:T(8,128)S(1)} %bitcast.11), custom_call_target="tpu_custom_call" | custom-call | flops 200000000 | bytes 4000000 | tf_op jit(solution)/shard_map/query_work/pallas_call | solution.py:469
  43.5 0.0 copy-start.14
  43.5 0.2 collective-permute-start.16
  43.7 0.0 collective-permute-done.11.refs_2_
  43.7 0.4 collective-permute-start.15
  44.1 0.0 collective-permute-done.10.refs_1_
  44.1 0.1 collective-permute-start.14
  44.3 5.9 %collective-permute-done.18 = bf16[4,64,512]{2,1,0:T(8,128)(2,1)S(1)} collective-permute-done((bf16[4,64,512]{2,1,0:T(8,128)(2,1)S(1)}, bf16[4,64,512]{2,1,0:T(8,128)(2,1)S(1)}, u32[]{:S(2)}, u32[]{:S(2)}) %collective-permute-start.18) | collective-permute-done | bytes 262176 | tf_op jit(solution)/shard_map/ppermute | solution.py:415
  50.2 0.0 copy-start.12
  50.2 0.1 pad_maximum_fusion.1.refs_12_
  50.3 0.0 copy-start.2
  50.3 0.0 copy-start.3
  50.4 0.1 pad_maximum_fusion.refs_8_
  50.4 1.8 %collective-permute-start.19 = (bf16[8,64,512]{2,1,0:T(8,128)(2,1)S(1)}, bf16[8,64,512]{2,1,0:T(8,128)(2,1)}, u32[]{:S(2)}, u32[]{:S(2)}) collective-permute-start(bf16[8,64,512]{2,1,0:T(8,128)(2,1)S(1)} %pad_maximum_fusion.refs_8_), channel_id=1, source_target_pairs={{0,16},{1,17},{2,18},{3,19},{4,20},{5,21},{6,22},{7,23},{8,24},{9,... | collective-permute-start | bytes 1572872 | tf_op jit(solution)/shard_map/ppermute | solution.py:415
  52.2 0.0 collective-permute-done.16.refs_7_
  52.3 1.5 %collective-permute-start.22 = (bf16[8,64,512]{2,1,0:T(8,128)(2,1)S(1)}, bf16[8,64,512]{2,1,0:T(8,128)(2,1)}, u32[]{:S(2)}, u32[]{:S(2)}) collective-permute-start(bf16[8,64,512]{2,1,0:T(8,128)(2,1)S(1)} %pad_maximum_fusion.1.refs_12_), channel_id=1, source_target_pairs={{0,8},{1,9},{2,10},{3,11},{4,12},{5,13},{6,14},{7,15},{8,0},{9,1},... | collective-permute-start | bytes 1572872 | tf_op jit(solution)/shard_map/ppermute | solution.py:415
  53.8 0.0 collective-permute-done.15.refs_6_
  53.8 0.0 collective-permute-done.14.refs_5_
  53.9 2.9 %forward.1 = (bf16[128,512]{1,0:T(8,128)(2,1)}, f32[32,16,128]{2,1,0:T(8,128)}) custom-call(s32[133]{0:T(256)S(1)} %query_work.1.work_ref, bf16[4,128,256]{2,1,0:T(8,128)(2,1)S(1)} %copy-done.13, bf16[128,512]{1,0:T(8,128)(2,1)S(1)} %copy-done.12, bf16[512,512]{1,0:T(8,128)(2,1)S(1)} %copy-done.2, bf16[512,512]{1,0:T(8,128)(2,1)S(1)} %copy-done.10, ...), custom_call_target="tpu_custom_call" | custom-call | flops 1000000000 | bytes 4000000 | tf_op jit(solution)/shard_map/forward/pallas_call | solution.py:537
  56.9 2.7 %all-to-all-start = ((f32[32,16,128]{2,1,0:T(8,128)}), f32[32,16,128]{2,1,0:T(8,128)S(1)}, u32[]{:S(2)}, u32[]{:S(2)}) async-start(f32[32,16,128]{2,1,0:T(8,128)} %get-tuple-element.33.stats_hbm), calls=%async_computation | async-start | bytes 524288 | tf_op jit(solution)/shard_map/all_to_all | solution.py:548
  59.6 0.3 collective-permute-start.20
  59.9 0.3 collective-permute-start.23
  60.2 4.5 %query_grad.1.part_hbm = f32[128,512]{1,0:T(8,128)} custom-call(s32[133]{0:T(256)} %copy-done.14, bf16[4,128,256]{2,1,0:T(8,128)(2,1)} %get-tuple-element.26.stack_ref.stack_hbm, bf16[4,128,256]{2,1,0:T(8,128)(2,1)} %get-tuple-element.32.cot_stack_hbm, f32[32,16,128]{2,1,0:T(8,128)} %get-tuple-element.33.stats_hbm, ...), custom_call_target="tpu_custom_call" | custom-call | flops 1000000000 | bytes 4000000 | tf_op jit(solution)/shard_map/query_grad/pallas_call | solution.py:550
  64.7 0.0 collective-permute-done.19.refs_9_
  64.7 5.3 %all-to-all-done.stats_all_ref = f32[32,16,128]{2,1,0:T(8,128)S(1)} async-done(((f32[32,16,128]{2,1,0:T(8,128)}), f32[32,16,128]{2,1,0:T(8,128)S(1)}, u32[]{:S(2)}, u32[]{:S(2)}) %all-to-all-start) | async-done | bytes 262176 | tf_op jit(solution)/shard_map/all_to_all | solution.py:548
  70.0 0.4 collective-permute-start.21
  70.3 0.0 collective-permute-done.22.refs_13_
  70.3 0.1 collective-permute-start.24
  70.5 0.0 collective-permute-done.20.refs_10_
  70.5 1.6 %collective-permute-done.21.refs_11_ = bf16[8,64,512]{2,1,0:T(8,128)(2,1)S(1)} collective-permute-done((bf16[8,64,512]{2,1,0:T(8,128)(2,1)}, bf16[8,64,512]{2,1,0:T(8,128)(2,1)S(1)}, u32[]{:S(2)}, u32[]{:S(2)}) %collective-permute-start.21) | collective-permute-done | bytes 524320 | tf_op jit(solution)/shard_map/ppermute | solution.py:415
  72.1 0.7 collective-permute-done.24.refs_15_
  72.8 0.0 copy-done.22
  72.9 0.8 copy-done.23
  73.7 5.8 %key_grad.1 = bf16[128,512]{1,0:T(8,128)(2,1)} custom-call(s32[69]{0:T(128)} %copy-done.15, bf16[128,512]{1,0:T(8,128)(2,1)} %get-tuple-element.29.key_hbm, bf16[128,512]{1,0:T(8,128)(2,1)} %get-tuple-element.30.value_hbm, bf16[512,512]{1,0:T(8,128)(2,1)} %wq_hbm.3, bf16[512,512]{1,0:T(8,128)(2,1)} %get-tuple-element.31.wkt_hbm, ...), custom_call_target="tpu_custom_call" | custom-call | flops 1000000000 | bytes 4000000 | tf_op jit(solution)/shard_map/key_grad/pallas_call | solution.py:569
  (75 shorter events, 0.4 us)
Async XLA Ops:
  1.3 7.4 %copy-start.11 = (bf16[128,512]{1,0:T(8,128)(2,1)S(1)}, bf16[128,512]{1,0:T(8,128)(2,1)}, u32[]{:S(2)}) copy-start(bf16[128,512]{1,0:T(8,128)(2,1)} %cot_ref.1) | copy-start | bytes 393220
  2.9 9.0 %copy-start.19 = (bf16[1,144,512]{2,1,0:T(8,128)(2,1)S(1)}, bf16[1,144,512]{2,1,0:T(8,128)(2,1)}, u32[]{:S(2)}) copy-start(bf16[1,144,512]{2,1,0:T(8,128)(2,1)} %pack.1) | copy-start | bytes 442372
  2.9 13.3 %collective-permute-start.2 = (bf16[1,144,512]{2,1,0:T(8,128)(2,1)}, bf16[1,144,512]{2,1,0:T(8,128)(2,1)S(1)}, u32[]{:S(2)}, u32[]{:S(2)}) collective-permute-start(bf16[1,144,512]{2,1,0:T(8,128)(2,1)} %pack.1), channel_id=1, source_target_pairs={{0,6},{1,7},{2,4},{3,5},{4,2},{5,3},{6,0},{7,1},{8,14},{9,15},{10,... | collective-permute-start | bytes 442376 | tf_op jit(solution)/shard_map/ppermute | solution.py:415
  8.0 12.7 %collective-permute-start.1 = (bf16[1,144,512]{2,1,0:T(8,128)(2,1)}, bf16[1,144,512]{2,1,0:T(8,128)(2,1)S(1)}, u32[]{:S(2)}, u32[]{:S(2)}) collective-permute-start(bf16[1,144,512]{2,1,0:T(8,128)(2,1)} %pack.1), channel_id=1, source_target_pairs={{0,4},{1,5},{2,6},{3,7},{4,0},{5,1},{6,2},{7,3},{8,12},{9,13},{10,... | collective-permute-start | bytes 442376 | tf_op jit(solution)/shard_map/ppermute | solution.py:415
  8.0 12.7 %collective-permute-start = (bf16[1,144,512]{2,1,0:T(8,128)(2,1)}, bf16[1,144,512]{2,1,0:T(8,128)(2,1)S(1)}, u32[]{:S(2)}, u32[]{:S(2)}) collective-permute-start(bf16[1,144,512]{2,1,0:T(8,128)(2,1)} %pack.1), channel_id=1, source_target_pairs={{0,2},{1,3},{2,0},{3,1},{4,6},{5,7},{6,4},{7,5},{8,10},{9,11},{10,... | collective-permute-start | bytes 442376 | tf_op jit(solution)/shard_map/ppermute | solution.py:415
  8.7 4.3 %collective-permute-start.3 = (bf16[1,64,512]{2,1,0:T(8,128)(2,1)S(1)}, bf16[1,64,512]{2,1,0:T(8,128)(2,1)S(1)}, u32[]{:S(2)}, u32[]{:S(2)}) collective-permute-start(bf16[1,64,512]{2,1,0:T(8,128)(2,1)S(1)} %get-tuple-element.50), channel_id=1, source_target_pairs={{0,8},{1,9},{2,10},{3,11},{4,12},{5,13},{6,14},{7,15},{8,0},{9,1},... | collective-permute-start | bytes 196616 | tf_op jit(solution)/shard_map/ppermute | solution.py:415
  10.4 5.2 %collective-permute-start.4 = (bf16[1,64,512]{2,1,0:T(8,128)(2,1)S(1)}, bf16[1,64,512]{2,1,0:T(8,128)(2,1)S(1)}, u32[]{:S(2)}, u32[]{:S(2)}) collective-permute-start(bf16[1,64,512]{2,1,0:T(8,128)(2,1)S(1)} %get-tuple-element.51), channel_id=1, source_target_pairs={{0,16},{1,17},{2,18},{3,19},{4,20},{5,21},{6,22},{7,23},{8,24},{9,... | collective-permute-start | bytes 196616 | tf_op jit(solution)/shard_map/ppermute | solution.py:415
  13.0 8.7 %collective-permute-start.7 = (bf16[1,144,512]{2,1,0:T(8,128)(2,1)S(1)}, bf16[1,144,512]{2,1,0:T(8,128)(2,1)S(1)}, u32[]{:S(2)}, u32[]{:S(2)}) collective-permute-start(bf16[1,144,512]{2,1,0:T(8,128)(2,1)S(1)} %copy-done.19), channel_id=1, source_target_pairs={{0,24},{1,25},{2,26},{3,27},{4,28},{5,29},{6,30},{7,31},{8,16},{9,... | collective-permute-start | bytes 442376 | tf_op jit(solution)/shard_map/ppermute | solution.py:415
  15.6 6.1 %collective-permute-start.6 = (bf16[1,144,512]{2,1,0:T(8,128)(2,1)S(1)}, bf16[1,144,512]{2,1,0:T(8,128)(2,1)S(1)}, u32[]{:S(2)}, u32[]{:S(2)}) collective-permute-start(bf16[1,144,512]{2,1,0:T(8,128)(2,1)S(1)} %copy-done.19), channel_id=1, source_target_pairs={{0,16},{1,17},{2,18},{3,19},{4,20},{5,21},{6,22},{7,23},{8,24},{9,... | collective-permute-start | bytes 442376 | tf_op jit(solution)/shard_map/ppermute | solution.py:415
  16.2 0.7 copy-start.24
  16.2 5.5 %collective-permute-start.5 = (bf16[1,144,512]{2,1,0:T(8,128)(2,1)S(1)}, bf16[1,144,512]{2,1,0:T(8,128)(2,1)S(1)}, u32[]{:S(2)}, u32[]{:S(2)}) collective-permute-start(bf16[1,144,512]{2,1,0:T(8,128)(2,1)S(1)} %copy-done.19), channel_id=1, source_target_pairs={{0,8},{1,9},{2,10},{3,11},{4,12},{5,13},{6,14},{7,15},{8,0},{9,1},... | collective-permute-start | bytes 442376 | tf_op jit(solution)/shard_map/ppermute | solution.py:415
  20.7 0.9 %slice-start = ((bf16[1,144,512]{2,1,0:T(8,128)(2,1)}), bf16[1,128,512]{2,1,0:T(8,128)(2,1)S(1)}, s32[]{:S(2)}) async-start(bf16[1,144,512]{2,1,0:T(8,128)(2,1)} %copy-done.24), calls=%async_computation.1 | async-start | bytes 262144 | tf_op jit(solution)/shard_map/slice | solution.py:499
  21.7 21.8 %collective-permute-start.12 = (bf16[3,128,512]{2,1,0:T(8,128)(2,1)S(1)}, bf16[3,128,512]{2,1,0:T(8,128)(2,1)S(1)}, u32[]{:S(2)}, u32[]{:S(2)}) collective-permute-start(bf16[3,128,512]{2,1,0:T(8,128)(2,1)S(1)} %pad_maximum_fusion.2), channel_id=1, source_target_pairs={{0,24},{1,25},{2,26},{3,27},{4,28},{5,29},{6,30},{7,31},{8,16},{9,... | collective-permute-start | bytes 1179656 | tf_op jit(solution)/shard_map/ppermute | solution.py:415
  24.2 19.5 %collective-permute-start.11 = (bf16[3,128,512]{2,1,0:T(8,128)(2,1)S(1)}, bf16[3,128,512]{2,1,0:T(8,128)(2,1)S(1)}, u32[]{:S(2)}, u32[]{:S(2)}) collective-permute-start(bf16[3,128,512]{2,1,0:T(8,128)(2,1)S(1)} %pad_maximum_fusion.2), channel_id=1, source_target_pairs={{0,16},{1,17},{2,18},{3,19},{4,20},{5,21},{6,22},{7,23},{8,24},{9,... | collective-permute-start | bytes 1179656 | tf_op jit(solution)/shard_map/ppermute | solution.py:415
  24.8 19.4 %collective-permute-start.10 = (bf16[3,128,512]{2,1,0:T(8,128)(2,1)S(1)}, bf16[3,128,512]{2,1,0:T(8,128)(2,1)S(1)}, u32[]{:S(2)}, u32[]{:S(2)}) collective-permute-start(bf16[3,128,512]{2,1,0:T(8,128)(2,1)S(1)} %pad_maximum_fusion.2), channel_id=1, source_target_pairs={{0,8},{1,9},{2,10},{3,11},{4,12},{5,13},{6,14},{7,15},{8,0},{9,1},... | collective-permute-start | bytes 1179656 | tf_op jit(solution)/shard_map/ppermute | solution.py:415
  25.3 4.7 %copy-start.25 = (bf16[1,144,512]{2,1,0:T(8,128)(2,1)S(1)}, bf16[1,144,512]{2,1,0:T(8,128)(2,1)}, u32[]{:S(2)}) copy-start(bf16[1,144,512]{2,1,0:T(8,128)(2,1)} %copy-done.24) | copy-start | bytes 442372
  25.4 28.4 %copy-start = (bf16[7,128,512]{2,1,0:T(8,128)(2,1)}, bf16[7,128,512]{2,1,0:T(8,128)(2,1)S(1)}, u32[]{:S(2)}) copy-start(bf16[7,128,512]{2,1,0:T(8,128)(2,1)S(1)} %constant_dynamic-update-slice_fusion.refs_0_) | copy-start | bytes 2752516
  25.4 14.0 %collective-permute-start.17 = (bf16[4,64,512]{2,1,0:T(8,128)(2,1)S(1)}, bf16[4,64,512]{2,1,0:T(8,128)(2,1)S(1)}, u32[]{:S(2)}, u32[]{:S(2)}) collective-permute-start(bf16[4,64,512]{2,1,0:T(8,128)(2,1)S(1)} %pad_maximum_fusion.3), channel_id=1, source_target_pairs={{0,4},{1,5},{2,6},{3,7},{4,0},{5,1},{6,2},{7,3},{8,12},{9,13},{10,... | collective-permute-start | bytes 786440 | tf_op jit(solution)/shard_map/ppermute | solution.py:415
  30.0 9.3 %collective-permute-start.8 = (bf16[4,64,512]{2,1,0:T(8,128)(2,1)S(1)}, bf16[4,64,512]{2,1,0:T(8,128)(2,1)S(1)}, u32[]{:S(2)}, u32[]{:S(2)}) collective-permute-start(bf16[4,64,512]{2,1,0:T(8,128)(2,1)S(1)} %pad_maximum_fusion.3), channel_id=1, source_target_pairs={{0,2},{1,3},{2,0},{3,1},{4,6},{5,7},{6,4},{7,5},{8,10},{9,11},{10,... | collective-permute-start | bytes 786440 | tf_op jit(solution)/shard_map/ppermute | solution.py:415
  34.8 0.5 copy-start.15
  39.3 14.4 %collective-permute-start.13 = (bf16[7,128,512]{2,1,0:T(8,128)(2,1)S(1)}, bf16[7,128,512]{2,1,0:T(8,128)(2,1)S(1)}, u32[]{:S(2)}, u32[]{:S(2)}) collective-permute-start(bf16[7,128,512]{2,1,0:T(8,128)(2,1)S(1)} %constant_dynamic-update-slice_fusion.refs_0_), channel_id=1, source_target_pairs={{0,1},{1,0},{2,3},{3,2},{4,5},{5,4},{6,7},{7,6},{8,9},{9,8},{10,11... | collective-permute-start | bytes 2752520 | tf_op jit(solution)/shard_map/ppermute | solution.py:415
  39.4 2.5 %collective-permute-start.9 = (bf16[4,16,128]{2,1,0:T(8,128)(2,1)S(1)}, bf16[4,16,128]{2,1,0:T(8,128)(2,1)S(1)}, u32[]{:S(2)}, u32[]{:S(2)}) collective-permute-start(bf16[4,16,128]{2,1,0:T(8,128)(2,1)S(1)} %pad_maximum_fusion.4), channel_id=1, source_target_pairs={{0,1},{1,0},{2,3},{3,2},{4,5},{5,4},{6,7},{7,6},{8,9},{9,8},{10,11... | collective-permute-start | bytes 49160 | tf_op jit(solution)/shard_map/ppermute | solution.py:415
  41.8 8.3 %collective-permute-start.18 = (bf16[4,64,512]{2,1,0:T(8,128)(2,1)S(1)}, bf16[4,64,512]{2,1,0:T(8,128)(2,1)S(1)}, u32[]{:S(2)}, u32[]{:S(2)}) collective-permute-start(bf16[4,64,512]{2,1,0:T(8,128)(2,1)S(1)} %collective-permute-done.17), channel_id=1, source_target_pairs={{0,2},{1,3},{2,0},{3,1},{4,6},{5,7},{6,4},{7,5},{8,10},{9,11},{10,... | collective-permute-start | bytes 786440 | tf_op jit(solution)/shard_map/ppermute | solution.py:415
  43.5 10.3 %copy-start.14 = (s32[133]{0:T(256)}, s32[133]{0:T(256)S(1)}, u32[]{:S(2)}) copy-start(s32[133]{0:T(256)S(1)} %query_work.1.work_ref) | copy-start | bytes 1600
  43.5 10.3 %copy-start.4 = (bf16[3,128,512]{2,1,0:T(8,128)(2,1)}, bf16[3,128,512]{2,1,0:T(8,128)(2,1)S(1)}, u32[]{:S(2)}) copy-start(bf16[3,128,512]{2,1,0:T(8,128)(2,1)S(1)} %collective-permute-done.12.refs_3_) | copy-start | bytes 1179652
  43.5 8.7 %collective-permute-start.16 = (bf16[3,128,512]{2,1,0:T(8,128)(2,1)S(1)}, bf16[3,128,512]{2,1,0:T(8,128)(2,1)S(1)}, u32[]{:S(2)}, u32[]{:S(2)}) collective-permute-start(bf16[3,128,512]{2,1,0:T(8,128)(2,1)S(1)} %collective-permute-done.12.refs_3_), channel_id=1, source_target_pairs={{0,1},{1,0},{2,3},{3,2},{4,5},{5,4},{6,7},{7,6},{8,9},{9,8},{10,11... | collective-permute-start | bytes 1179656 | tf_op jit(solution)/shard_map/ppermute | solution.py:415
  43.7 10.1 %copy-start.5 = (bf16[3,128,512]{2,1,0:T(8,128)(2,1)}, bf16[3,128,512]{2,1,0:T(8,128)(2,1)S(1)}, u32[]{:S(2)}) copy-start(bf16[3,128,512]{2,1,0:T(8,128)(2,1)S(1)} %collective-permute-done.11.refs_2_) | copy-start | bytes 1179652
  43.7 10.0 %collective-permute-start.15 = (bf16[3,128,512]{2,1,0:T(8,128)(2,1)S(1)}, bf16[3,128,512]{2,1,0:T(8,128)(2,1)S(1)}, u32[]{:S(2)}, u32[]{:S(2)}) collective-permute-start(bf16[3,128,512]{2,1,0:T(8,128)(2,1)S(1)} %collective-permute-done.11.refs_2_), channel_id=1, source_target_pairs={{0,1},{1,0},{2,3},{3,2},{4,5},{5,4},{6,7},{7,6},{8,9},{9,8},{10,11... | collective-permute-start | bytes 1179656 | tf_op jit(solution)/shard_map/ppermute | solution.py:415
  44.1 9.7 %copy-start.6 = (bf16[3,128,512]{2,1,0:T(8,128)(2,1)}, bf16[3,128,512]{2,1,0:T(8,128)(2,1)S(1)}, u32[]{:S(2)}) copy-start(bf16[3,128,512]{2,1,0:T(8,128)(2,1)S(1)} %collective-permute-done.10.refs_1_) | copy-start | bytes 1179652
  44.1 9.7 %collective-permute-start.14 = (bf16[3,128,512]{2,1,0:T(8,128)(2,1)S(1)}, bf16[3,128,512]{2,1,0:T(8,128)(2,1)S(1)}, u32[]{:S(2)}, u32[]{:S(2)}) collective-permute-start(bf16[3,128,512]{2,1,0:T(8,128)(2,1)S(1)} %collective-permute-done.10.refs_1_), channel_id=1, source_target_pairs={{0,1},{1,0},{2,3},{3,2},{4,5},{5,4},{6,7},{7,6},{8,9},{9,8},{10,11... | collective-permute-start | bytes 1179656 | tf_op jit(solution)/shard_map/ppermute | solution.py:415
  50.2 3.6 %copy-start.10 = (bf16[512,512]{1,0:T(8,128)(2,1)S(1)}, bf16[512,512]{1,0:T(8,128)(2,1)}, u32[]{:S(2)}) copy-start(bf16[512,512]{1,0:T(8,128)(2,1)} %get-tuple-element.27.wvt_ref.wvt_hbm) | copy-start | bytes 1572868
  50.2 3.6 %copy-start.12 = (bf16[128,512]{1,0:T(8,128)(2,1)S(1)}, bf16[128,512]{1,0:T(8,128)(2,1)}, u32[]{:S(2)}) copy-start(bf16[128,512]{1,0:T(8,128)(2,1)} %cot_ref.1) | copy-start | bytes 393220
  50.2 3.6 %copy-start.13 = (bf16[4,128,256]{2,1,0:T(8,128)(2,1)S(1)}, bf16[4,128,256]{2,1,0:T(8,128)(2,1)}, u32[]{:S(2)}) copy-start(bf16[4,128,256]{2,1,0:T(8,128)(2,1)} %get-tuple-element.26.stack_ref.stack_hbm) | copy-start | bytes 786436
  50.3 9.6 %copy-start.16 = (bf16[8,64,512]{2,1,0:T(8,128)(2,1)}, bf16[8,64,512]{2,1,0:T(8,128)(2,1)S(1)}, u32[]{:S(2)}) copy-start(bf16[8,64,512]{2,1,0:T(8,128)(2,1)S(1)} %pad_maximum_fusion.1.refs_12_) | copy-start | bytes 1572868
  50.3 3.6 %copy-start.2 = (bf16[512,512]{1,0:T(8,128)(2,1)S(1)}, bf16[512,512]{1,0:T(8,128)(2,1)}, u32[]{:S(2)}) copy-start(bf16[512,512]{1,0:T(8,128)(2,1)} %wk_hbm.3) | copy-start | bytes 1572868
  50.3 3.6 %copy-start.3 = (s32[240,128,4]{1,2,0:T(4,128)S(1)}, s32[240,128,4]{1,2,0:T(4,128)}, u32[]{:S(2)}) copy-start(s32[240,128,4]{1,2,0:T(4,128)} %param.15) | copy-start | bytes 1474564
  50.4 9.1 %copy-start.17 = (bf16[8,64,512]{2,1,0:T(8,128)(2,1)}, bf16[8,64,512]{2,1,0:T(8,128)(2,1)S(1)}, u32[]{:S(2)}) copy-start(bf16[8,64,512]{2,1,0:T(8,128)(2,1)S(1)} %pad_maximum_fusion.refs_8_) | copy-start | bytes 1572868
  50.4 14.2 %collective-permute-start.19 = (bf16[8,64,512]{2,1,0:T(8,128)(2,1)S(1)}, bf16[8,64,512]{2,1,0:T(8,128)(2,1)}, u32[]{:S(2)}, u32[]{:S(2)}) collective-permute-start(bf16[8,64,512]{2,1,0:T(8,128)(2,1)S(1)} %pad_maximum_fusion.refs_8_), channel_id=1, source_target_pairs={{0,16},{1,17},{2,18},{3,19},{4,20},{5,21},{6,22},{7,23},{8,24},{9,... | collective-permute-start | bytes 1572872 | tf_op jit(solution)/shard_map/ppermute | solution.py:415
  52.3 4.6 %copy-start.7 = (bf16[3,128,512]{2,1,0:T(8,128)(2,1)}, bf16[3,128,512]{2,1,0:T(8,128)(2,1)S(1)}, u32[]{:S(2)}) copy-start(bf16[3,128,512]{2,1,0:T(8,128)(2,1)S(1)} %collective-permute-done.16.refs_7_) | copy-start | bytes 1179652
  52.3 18.1 %collective-permute-start.22 = (bf16[8,64,512]{2,1,0:T(8,128)(2,1)S(1)}, bf16[8,64,512]{2,1,0:T(8,128)(2,1)}, u32[]{:S(2)}, u32[]{:S(2)}) collective-permute-start(bf16[8,64,512]{2,1,0:T(8,128)(2,1)S(1)} %pad_maximum_fusion.1.refs_12_), channel_id=1, source_target_pairs={{0,8},{1,9},{2,10},{3,11},{4,12},{5,13},{6,14},{7,15},{8,0},{9,1},... | collective-permute-start | bytes 1572872 | tf_op jit(solution)/shard_map/ppermute | solution.py:415
  53.8 3.1 %copy-start.8 = (bf16[3,128,512]{2,1,0:T(8,128)(2,1)}, bf16[3,128,512]{2,1,0:T(8,128)(2,1)S(1)}, u32[]{:S(2)}) copy-start(bf16[3,128,512]{2,1,0:T(8,128)(2,1)S(1)} %collective-permute-done.15.refs_6_) | copy-start | bytes 1179652
  53.8 3.1 %copy-start.9 = (bf16[3,128,512]{2,1,0:T(8,128)(2,1)}, bf16[3,128,512]{2,1,0:T(8,128)(2,1)S(1)}, u32[]{:S(2)}) copy-start(bf16[3,128,512]{2,1,0:T(8,128)(2,1)S(1)} %collective-permute-done.14.refs_5_) | copy-start | bytes 1179652
  53.8 3.0 %copy-start.1 = (bf16[7,128,512]{2,1,0:T(8,128)(2,1)}, bf16[7,128,512]{2,1,0:T(8,128)(2,1)S(1)}, u32[]{:S(2)}) copy-start(bf16[7,128,512]{2,1,0:T(8,128)(2,1)S(1)} %collective-permute-done.13.refs_4_) | copy-start | bytes 2752516
  56.9 13.1 %all-to-all-start = ((f32[32,16,128]{2,1,0:T(8,128)}), f32[32,16,128]{2,1,0:T(8,128)S(1)}, u32[]{:S(2)}, u32[]{:S(2)}) async-start(f32[32,16,128]{2,1,0:T(8,128)} %get-tuple-element.33.stats_hbm), calls=%async_computation | async-start | bytes 524288 | tf_op jit(solution)/shard_map/all_to_all | solution.py:548
  59.6 10.9 %collective-permute-start.20 = (bf16[8,64,512]{2,1,0:T(8,128)(2,1)S(1)}, bf16[8,64,512]{2,1,0:T(8,128)(2,1)S(1)}, u32[]{:S(2)}, u32[]{:S(2)}) collective-permute-start(bf16[8,64,512]{2,1,0:T(8,128)(2,1)S(1)} %pad_maximum_fusion.refs_8_), channel_id=1, source_target_pairs={{0,1},{1,0},{2,3},{3,2},{4,5},{5,4},{6,7},{7,6},{8,9},{9,8},{10,11... | collective-permute-start | bytes 1572872 | tf_op jit(solution)/shard_map/ppermute | solution.py:415
  59.9 10.6 %collective-permute-start.23 = (bf16[8,64,512]{2,1,0:T(8,128)(2,1)S(1)}, bf16[8,64,512]{2,1,0:T(8,128)(2,1)S(1)}, u32[]{:S(2)}, u32[]{:S(2)}) collective-permute-start(bf16[8,64,512]{2,1,0:T(8,128)(2,1)S(1)} %pad_maximum_fusion.1.refs_12_), channel_id=1, source_target_pairs={{0,1},{1,0},{2,3},{3,2},{4,5},{5,4},{6,7},{7,6},{8,9},{9,8},{10,11... | collective-permute-start | bytes 1572872 | tf_op jit(solution)/shard_map/ppermute | solution.py:415
  70.0 2.9 %copy-start.18 = (f32[32,16,128]{2,1,0:T(8,128)}, f32[32,16,128]{2,1,0:T(8,128)S(1)}, u32[]{:S(2)}) copy-start(f32[32,16,128]{2,1,0:T(8,128)S(1)} %all-to-all-done.stats_all_ref) | copy-start | bytes 786436
  70.0 2.1 %collective-permute-start.21 = (bf16[8,64,512]{2,1,0:T(8,128)(2,1)}, bf16[8,64,512]{2,1,0:T(8,128)(2,1)S(1)}, u32[]{:S(2)}, u32[]{:S(2)}) collective-permute-start(bf16[8,64,512]{2,1,0:T(8,128)(2,1)} %collective-permute-done.19.refs_9_), channel_id=1, source_target_pairs={{0,1},{1,0},{2,3},{3,2},{4,5},{5,4},{6,7},{7,6},{8,9},{9,8},{10,11... | collective-permute-start | bytes 1572872 | tf_op jit(solution)/shard_map/ppermute | solution.py:415
  70.3 2.5 %collective-permute-start.24 = (bf16[8,64,512]{2,1,0:T(8,128)(2,1)}, bf16[8,64,512]{2,1,0:T(8,128)(2,1)S(1)}, u32[]{:S(2)}, u32[]{:S(2)}) collective-permute-start(bf16[8,64,512]{2,1,0:T(8,128)(2,1)} %collective-permute-done.22.refs_13_), channel_id=1, source_target_pairs={{0,1},{1,0},{2,3},{3,2},{4,5},{5,4},{6,7},{7,6},{8,9},{9,8},{10,11... | collective-permute-start | bytes 1572872 | tf_op jit(solution)/shard_map/ppermute | solution.py:415
  70.5 2.4 %copy-start.20 = (bf16[8,64,512]{2,1,0:T(8,128)(2,1)}, bf16[8,64,512]{2,1,0:T(8,128)(2,1)S(1)}, u32[]{:S(2)}) copy-start(bf16[8,64,512]{2,1,0:T(8,128)(2,1)S(1)} %collective-permute-done.20.refs_10_) | copy-start | bytes 1572868
  70.5 2.4 %copy-start.21 = (bf16[8,64,512]{2,1,0:T(8,128)(2,1)}, bf16[8,64,512]{2,1,0:T(8,128)(2,1)S(1)}, u32[]{:S(2)}) copy-start(bf16[8,64,512]{2,1,0:T(8,128)(2,1)S(1)} %collective-permute-done.23.refs_14_) | copy-start | bytes 1572868
  72.1 0.8 %copy-start.22 = (bf16[8,64,512]{2,1,0:T(8,128)(2,1)}, bf16[8,64,512]{2,1,0:T(8,128)(2,1)S(1)}, u32[]{:S(2)}) copy-start(bf16[8,64,512]{2,1,0:T(8,128)(2,1)S(1)} %collective-permute-done.21.refs_11_) | copy-start | bytes 1572868
  72.9 0.8 copy-start.23
where the time goes:
time: 79.4 us; the launch traced here: 79.5 us
  starting transfers between devices  29.2 us (37%)
  waiting for transfers between devices  24.4 us (31%)
  Pallas kernels  21.2 us (27%)
  local copies, waits for them, and re-layouts  2.59 us (3%)
  between operations  1.84 us (2%)
    ppermute x25, starting transfers between devices, swap(): return lax.ppermute(block, axes, [(i, i ^ mask) for i in range(count)])  26.4 us
    ppermute x25, waiting for transfers between devices, swap(): return lax.ppermute(block, axes, [(i, i ^ mask) for i in range(count)])  19.2 us
    pallas_call x1, Pallas kernels, local(): pl.pallas_call(functools.partial(key_grad_kernel, sizes, bits), out_shape...  5.79 us
    all_to_all x1, waiting for transfers between devices, local(): stats_all = lax.all_to_all(stats, axes, 0, 0, tiled=True)  5.26 us
    pallas_call x1, Pallas kernels, local(): pl.pallas_call(functools.partial(query_grad_kernel, sizes), out_shape=sha...  4.52 us
    pallas_call x1, Pallas kernels, local(): pl.pallas_call(prepare_kernel, out_shape=(stacks, stacks, own, own, squar...  3.32 us
    pallas_call x2, Pallas kernels, work(): pl.pallas_call(functools.partial(kernel, sizes), out_shape=shape((2 * cou...  3.04 us
    pallas_call x1, Pallas kernels, local(): pl.pallas_call(functools.partial(forward_kernel, sizes), out_shape=(own,...  2.9 us
  transfers between devices with their start and end apart: 26, of which 8 were waited for; matrix products, arithmetic and copies ran while one was open for 1% of the time, Pallas kernels for 17%

commit v1 on v0

--- a/solution.py
+++ b/solution.py
@@ -514,13 +514,7 @@
     row_lists = jnp.concatenate([line_lists, swap(line_lists, 1)], 0)
     query_work = work(query_work_kernel, row_lists, blks, "query_work")
     here = [near] + there
-    rows_all = here + [swap(group, 1) for group in here]
-
-    cots_here = []
-    for k in range(2):
-        part = jnp.concatenate([piece[2 * k : 2 * k + 2] for piece in pieces], 0)
-        masks_left = [m for m in range(1, readers) if not m >> bits[k] & 1]
-        cots_here.append((part, [swap(after(part, here), blks * m) for m in masks_left]))
+    rows_all = here + [swap(after(near, pieces[lines // 2]), 1)] + [swap(group, 1) for group in there]
 
     stack_space = pltpu.VMEM(stacks.shape, bf16)
     buffer = pltpu.VMEM((2, TILES * block, width), bf16)
@@ -544,6 +538,13 @@
         cost_estimate=cost(5),
         name="forward",
     )(query_work, query_stack, cotangent, w_key, w_value_t, masks, *rows_all)
+
+    pieces[-1] = after(pieces[-1], stats)
+    cots_here = []
+    for k in range(2):
+        part = jnp.concatenate([piece[2 * k : 2 * k + 2] for piece in pieces], 0)
+        masks_left = [m for m in range(1, readers) if not m >> bits[k] & 1]
+        cots_here.append((part, [swap(part, blks * m) for m in masks_left]))
 
     stats_all = lax.all_to_all(stats, axes, 0, 0, tiled=True)
 

time: 79.4 us -> 77.9 us (0.981)
  starting transfers between devices: 29.2 us -> 28.1 us
    ppermute x25, waiting for transfers between devices: 19.2 us -> 17.2 us  [swap(): return lax.ppermute(block, axes, [(i, i ^ mask) for i in range(count)])]
    all_to_all x1, waiting for transfers between devices: 5.26 us -> 7.02 us  [local(): stats_all = lax.all_to_all(stats, axes, 0, 0, tiled=True)]
    ppermute x25, starting transfers between devices: 26.4 us -> 25.5 us  [swap(): return lax.ppermute(block, axes, [(i, i ^ mask) for i in range(count)])]
  transfers between devices with their start and end apart: 26 -> 26, of which waited for: 8 -> 9; matrix products, arithmetic and copies ran while one was open for 1% -> 0% of each run, Pallas kernels for 17% -> 18%
where the time goes in v1:
time: 77.9 us; the launch traced here: 78.2 us
  starting transfers between devices  28.1 us (36%)
  waiting for transfers between devices  24.2 us (31%)
  Pallas kernels  21.1 us (27%)
  local copies, waits for them, and re-layouts  2.56 us (3%)
  between operations  1.88 us (2%)
    ppermute x25, starting transfers between devices, swap(): return lax.ppermute(block, axes, [(i, i ^ mask) for i in range(count)])  25.5 us
    ppermute x25, waiting for transfers between devices, swap(): return lax.ppermute(block, axes, [(i, i ^ mask) for i in range(count)])  17.2 us
    all_to_all x1, waiting for transfers between devices, local(): stats_all = lax.all_to_all(stats, axes, 0, 0, tiled=True)  7.02 us
    pallas_call x1, Pallas kernels, local(): pl.pallas_call(functools.partial(key_grad_kernel, sizes, bits), out_shape...  5.8 us
    pallas_call x1, Pallas kernels, local(): pl.pallas_call(functools.partial(query_grad_kernel, sizes), out_shape=sha...  4.52 us
    pallas_call x1, Pallas kernels, local(): pl.pallas_call(prepare_kernel, out_shape=(stacks, stacks, own, own, squar...  3.36 us
    pallas_call x2, Pallas kernels, work(): pl.pallas_call(functools.partial(kernel, sizes), out_shape=shape((2 * cou...  2.93 us
    pallas_call x1, Pallas kernels, local(): pl.pallas_call(functools.partial(forward_kernel, sizes), out_shape=(own,...  2.9 us
  transfers between devices with their start and end apart: 26, of which 9 were waited for; matrix products, arithmetic and copies ran while one was open for 0% of the time, Pallas kernels for 18%

profile of v1, /device:TPU:0, one launch (start us, length us, event | category | flops | bytes accessed | tf_op | source)
XLA Modules:
  0.0 78.2 jit_solution(9409595627272648680)
XLA Ops:
  1.3 0.0 copy-start.11
  1.3 1.6 %pack.1 = bf16[1,144,512]{2,1,0:T(8,128)(2,1)} custom-call(bf16[128,512]{1,0:T(8,128)(2,1)} %own_hbm.2, s32[1,3,1,8]{3,2,1,0:T(1,128)} %bitcast.13, s32[1,1]{1,0:T(1,128)S(6)} %copy.14.count_hbm), custom_call_target="tpu_custom_call" | custom-call | tf_op jit(solution)/shard_map/pack/pallas_call | solution.py:441
  2.9 5.1 %collective-permute-start.2 = (bf16[1,144,512]{2,1,0:T(8,128)(2,1)}, bf16[1,144,512]{2,1,0:T(8,128)(2,1)S(1)}, u32[]{:S(2)}, u32[]{:S(2)}) collective-permute-start(bf16[1,144,512]{2,1,0:T(8,128)(2,1)} %pack.1), channel_id=1, source_target_pairs={{0,6},{1,7},{2,4},{3,5},{4,2},{5,3},{6,0},{7,1},{8,14},{9,15},{10,... | collective-permute-start | bytes 442376 | tf_op jit(solution)/shard_map/ppermute | solution.py:415
  8.1 0.0 collective-permute-start.1
  8.1 0.6 collective-permute-start
  8.7 1.7 %collective-permute-start.3 = (bf16[1,64,512]{2,1,0:T(8,128)(2,1)S(1)}, bf16[1,64,512]{2,1,0:T(8,128)(2,1)S(1)}, u32[]{:S(2)}, u32[]{:S(2)}) collective-permute-start(bf16[1,64,512]{2,1,0:T(8,128)(2,1)S(1)} %get-tuple-element.50), channel_id=1, source_target_pairs={{0,8},{1,9},{2,10},{3,11},{4,12},{5,13},{6,14},{7,15},{8,0},{9,1},... | collective-permute-start | bytes 196616 | tf_op jit(solution)/shard_map/ppermute | solution.py:415
  10.4 1.5 %collective-permute-start.4 = (bf16[1,64,512]{2,1,0:T(8,128)(2,1)S(1)}, bf16[1,64,512]{2,1,0:T(8,128)(2,1)S(1)}, u32[]{:S(2)}, u32[]{:S(2)}) collective-permute-start(bf16[1,64,512]{2,1,0:T(8,128)(2,1)S(1)} %get-tuple-element.51), channel_id=1, source_target_pairs={{0,16},{1,17},{2,18},{3,19},{4,20},{5,21},{6,22},{7,23},{8,24},{9,... | collective-permute-start | bytes 196616 | tf_op jit(solution)/shard_map/ppermute | solution.py:415
  11.9 1.1 %collective-permute-done.3 = bf16[1,64,512]{2,1,0:T(8,128)(2,1)S(1)} collective-permute-done((bf16[1,64,512]{2,1,0:T(8,128)(2,1)S(1)}, bf16[1,64,512]{2,1,0:T(8,128)(2,1)S(1)}, u32[]{:S(2)}, u32[]{:S(2)}) %collective-permute-start.3) | collective-permute-done | bytes 65568 | tf_op jit(solution)/shard_map/ppermute | solution.py:415
  13.0 2.6 %collective-permute-start.7 = (bf16[1,144,512]{2,1,0:T(8,128)(2,1)S(1)}, bf16[1,144,512]{2,1,0:T(8,128)(2,1)S(1)}, u32[]{:S(2)}, u32[]{:S(2)}) collective-permute-start(bf16[1,144,512]{2,1,0:T(8,128)(2,1)S(1)} %copy-done.19), channel_id=1, source_target_pairs={{0,24},{1,25},{2,26},{3,27},{4,28},{5,29},{6,30},{7,31},{8,16},{9,... | collective-permute-start | bytes 442376 | tf_op jit(solution)/shard_map/ppermute | solution.py:415
  15.6 0.0 collective-permute-done.4
  15.6 0.6 collective-permute-start.6
  16.2 0.0 collective-permute-done.2
  16.2 0.5 collective-permute-start.5
  16.8 0.1 copy-done.26
  16.9 3.9 %collective-permute-done.1 = bf16[1,144,512]{2,1,0:T(8,128)(2,1)S(1)} collective-permute-done((bf16[1,144,512]{2,1,0:T(8,128)(2,1)}, bf16[1,144,512]{2,1,0:T(8,128)(2,1)S(1)}, u32[]{:S(2)}, u32[]{:S(2)}) %collective-permute-start.1) | collective-permute-done | bytes 147488 | tf_op jit(solution)/shard_map/ppermute | solution.py:415
  20.8 0.0 slice-start
  20.8 0.0 collective-permute-done
  20.8 0.9 %slice-done = bf16[1,128,512]{2,1,0:T(8,128)(2,1)S(1)} async-done(((bf16[1,144,512]{2,1,0:T(8,128)(2,1)}), bf16[1,128,512]{2,1,0:T(8,128)(2,1)S(1)}, s32[]{:S(2)}) %slice-start) | async-done | bytes 131096 | tf_op jit(solution)/shard_map/slice | solution.py:499
  21.7 0.0 collective-permute-done.6
  21.7 0.0 collective-permute-done.5
  21.9 2.6 %collective-permute-start.8 = (bf16[4,64,512]{2,1,0:T(8,128)(2,1)S(1)}, bf16[4,64,512]{2,1,0:T(8,128)(2,1)S(1)}, u32[]{:S(2)}, u32[]{:S(2)}) collective-permute-start(bf16[4,64,512]{2,1,0:T(8,128)(2,1)S(1)} %pad_maximum_fusion.3), channel_id=1, source_target_pairs={{0,2},{1,3},{2,0},{3,1},{4,6},{5,7},{6,4},{7,5},{8,10},{9,11},{10,... | collective-permute-start | bytes 786440 | tf_op jit(solution)/shard_map/ppermute | solution.py:415
  24.4 2.4 %collective-permute-start.12 = (bf16[3,128,512]{2,1,0:T(8,128)(2,1)S(1)}, bf16[3,128,512]{2,1,0:T(8,128)(2,1)S(1)}, u32[]{:S(2)}, u32[]{:S(2)}) collective-permute-start(bf16[3,128,512]{2,1,0:T(8,128)(2,1)S(1)} %pad_maximum_fusion.2), channel_id=1, source_target_pairs={{0,24},{1,25},{2,26},{3,27},{4,28},{5,29},{6,30},{7,31},{8,16},{9,... | collective-permute-start | bytes 1179656 | tf_op jit(solution)/shard_map/ppermute | solution.py:415
  26.9 0.5 collective-permute-start.11
  27.4 0.5 collective-permute-start.10
  27.9 1.5 %collective-permute-start.17 = (bf16[4,64,512]{2,1,0:T(8,128)(2,1)S(1)}, bf16[4,64,512]{2,1,0:T(8,128)(2,1)S(1)}, u32[]{:S(2)}, u32[]{:S(2)}) collective-permute-start(bf16[4,64,512]{2,1,0:T(8,128)(2,1)S(1)} %pad_maximum_fusion.3), channel_id=1, source_target_pairs={{0,4},{1,5},{2,6},{3,7},{4,0},{5,1},{6,2},{7,3},{8,12},{9,13},{10,... | collective-permute-start | bytes 786440 | tf_op jit(solution)/shard_map/ppermute | solution.py:415
  29.4 0.8 collective-permute-done.8
  30.2 3.4 %prepare.1 = (bf16[4,128,256]{2,1,0:T(8,128)(2,1)}, bf16[4,128,256]{2,1,0:T(8,128)(2,1)}, bf16[128,512]{1,0:T(8,128)(2,1)}, bf16[128,512]{1,0:T(8,128)(2,1)}, bf...) custom-call(bf16[128,512]{1,0:T(8,128)(2,1)} %own_hbm.2, bf16[128,512]{1,0:T(8,128)(2,1)} %cot_ref.1, ...), custom_call_target="tpu_custom_call" | custom-call | flops 400000000 | bytes 4000000 | tf_op jit(solution)/shard_map/prepare/pallas_call | solution.py:487
  33.6 1.3 %key_work.1.work_ref = s32[69]{0:T(128)S(1)} custom-call(s32[4,128]{1,0:T(4,128)S(1)} %bitcast.12), custom_call_target="tpu_custom_call" | custom-call | flops 200000000 | bytes 4000000 | tf_op jit(solution)/shard_map/key_work/pallas_call | solution.py:469
  35.0 0.5 copy-done.15
  35.4 4.1 %collective-permute-done.17 = bf16[4,64,512]{2,1,0:T(8,128)(2,1)S(1)} collective-permute-done((bf16[4,64,512]{2,1,0:T(8,128)(2,1)S(1)}, bf16[4,64,512]{2,1,0:T(8,128)(2,1)S(1)}, u32[]{:S(2)}, u32[]{:S(2)}) %collective-permute-start.17) | collective-permute-done | bytes 262176 | tf_op jit(solution)/shard_map/ppermute | solution.py:415
  39.5 0.0 collective-permute-start.9
  39.5 0.5 collective-permute-start.16
  40.0 2.5 %collective-permute-done.11.refs_2_ = bf16[3,128,512]{2,1,0:T(8,128)(2,1)S(1)} collective-permute-done((bf16[3,128,512]{2,1,0:T(8,128)(2,1)S(1)}, bf16[3,128,512]{2,1,0:T(8,128)(2,1)S(1)}, u32[]{:S(2)}, u32[]{:S(2)}) %collective-permute-start.11) | collective-permute-done | bytes 393248 | tf_op jit(solution)/shard_map/ppermute | solution.py:415
  42.5 0.0 collective-permute-start.15
  42.5 0.0 collective-permute-done.10.refs_1_
  42.5 0.5 collective-permute-start.14
  43.0 0.0 copy-start.2
  43.0 0.8 collective-permute-start.18
  43.8 0.0 copy-start.3
  43.8 0.0 copy-start.12
  43.9 1.6 %query_work.1.work_ref = s32[133]{0:T(256)S(1)} custom-call(s32[8,128]{1,0:T(8,128)S(1)} %bitcast.11), custom_call_target="tpu_custom_call" | custom-call | flops 200000000 | bytes 4000000 | tf_op jit(solution)/shard_map/query_work/pallas_call | solution.py:469
  45.5 0.0 copy-start.14
  45.5 0.0 collective-permute-done.16.refs_7_
  45.5 0.0 collective-permute-done.14.refs_5_
  45.5 0.0 collective-permute-done.13.refs_4_
  45.6 2.9 %forward.1 = (bf16[128,512]{1,0:T(8,128)(2,1)}, f32[32,16,128]{2,1,0:T(8,128)}) custom-call(s32[133]{0:T(256)S(1)} %query_work.1.work_ref, bf16[4,128,256]{2,1,0:T(8,128)(2,1)S(1)} %copy-done.13, bf16[128,512]{1,0:T(8,128)(2,1)S(1)} %copy-done.12, bf16[512,512]{1,0:T(8,128)(2,1)S(1)} %copy-done.2, bf16[512,512]{1,0:T(8,128)(2,1)S(1)} %copy-done.10, ...), custom_call_target="tpu_custom_call" | custom-call | flops 1000000000 | bytes 4000000 | tf_op jit(solution)/shard_map/forward/pallas_call | solution.py:531
  48.6 2.8 %collective-permute-done.18 = bf16[4,64,512]{2,1,0:T(8,128)(2,1)S(1)} collective-permute-done((bf16[4,64,512]{2,1,0:T(8,128)(2,1)S(1)}, bf16[4,64,512]{2,1,0:T(8,128)(2,1)S(1)}, u32[]{:S(2)}, u32[]{:S(2)}) %collective-permute-start.18) | collective-permute-done | bytes 262176 | tf_op jit(solution)/shard_map/ppermute | solution.py:415
  51.4 0.1 pad_maximum_fusion.refs_8_
  51.5 0.9 %collective-permute-start.19 = (bf16[8,64,512]{2,1,0:T(8,128)(2,1)S(1)}, bf16[8,64,512]{2,1,0:T(8,128)(2,1)S(1)}, u32[]{:S(2)}, u32[]{:S(2)}) collective-permute-start(bf16[8,64,512]{2,1,0:T(8,128)(2,1)S(1)} %pad_maximum_fusion.refs_8_), channel_id=1, source_target_pairs={{0,16},{1,17},{2,18},{3,19},{4,20},{5,21},{6,22},{7,23},{8,24},{9,... | collective-permute-start | bytes 1572872 | tf_op jit(solution)/shard_map/ppermute | solution.py:415
  52.4 0.1 pad_maximum_fusion.1.refs_12_
  52.5 1.5 %collective-permute-start.22 = (bf16[8,64,512]{2,1,0:T(8,128)(2,1)S(1)}, bf16[8,64,512]{2,1,0:T(8,128)(2,1)S(1)}, u32[]{:S(2)}, u32[]{:S(2)}) collective-permute-start(bf16[8,64,512]{2,1,0:T(8,128)(2,1)S(1)} %pad_maximum_fusion.1.refs_12_), channel_id=1, source_target_pairs={{0,8},{1,9},{2,10},{3,11},{4,12},{5,13},{6,14},{7,15},{8,0},{9,1},... | collective-permute-start | bytes 1572872 | tf_op jit(solution)/shard_map/ppermute | solution.py:415
  54.0 2.6 %all-to-all-start = ((f32[32,16,128]{2,1,0:T(8,128)}), f32[32,16,128]{2,1,0:T(8,128)S(1)}, u32[]{:S(2)}, u32[]{:S(2)}) async-start(f32[32,16,128]{2,1,0:T(8,128)} %get-tuple-element.34.stats_hbm), calls=%async_computation | async-start | bytes 524288 | tf_op jit(solution)/shard_map/all_to_all | solution.py:549
  56.6 0.3 collective-permute-start.20
  57.0 0.3 collective-permute-start.23
  57.2 4.5 %query_grad.1.part_hbm = f32[128,512]{1,0:T(8,128)} custom-call(s32[133]{0:T(256)} %copy-done.14, bf16[4,128,256]{2,1,0:T(8,128)(2,1)} %get-tuple-element.26.stack_ref.stack_hbm, bf16[4,128,256]{2,1,0:T(8,128)(2,1)} %get-tuple-element.33.cot_stack_hbm, f32[32,16,128]{2,1,0:T(8,128)} %get-tuple-element.34.stats_hbm, ...), custom_call_target="tpu_custom_call" | custom-call | flops 1000000000 | bytes 4000000 | tf_op jit(solution)/shard_map/query_grad/pallas_call | solution.py:551
  61.8 7.0 %all-to-all-done.stats_all_ref = f32[32,16,128]{2,1,0:T(8,128)S(1)} async-done(((f32[32,16,128]{2,1,0:T(8,128)}), f32[32,16,128]{2,1,0:T(8,128)S(1)}, u32[]{:S(2)}, u32[]{:S(2)}) %all-to-all-start) | async-done | bytes 262176 | tf_op jit(solution)/shard_map/all_to_all | solution.py:549
  68.8 0.0 collective-permute-done.19.refs_9_
  68.8 0.1 collective-permute-start.21
  68.9 0.5 collective-permute-start.24
  69.4 1.4 %collective-permute-done.21.refs_11_ = bf16[8,64,512]{2,1,0:T(8,128)(2,1)S(1)} collective-permute-done((bf16[8,64,512]{2,1,0:T(8,128)(2,1)S(1)}, bf16[8,64,512]{2,1,0:T(8,128)(2,1)S(1)}, u32[]{:S(2)}, u32[]{:S(2)}) %collective-permute-start.21) | collective-permute-done | bytes 524320 | tf_op jit(solution)/shard_map/ppermute | solution.py:415
  70.8 0.7 collective-permute-done.24.refs_15_
  71.5 0.0 copy-done.24
  71.6 0.8 %copy-done.25 = bf16[8,64,512]{2,1,0:T(8,128)(2,1)} copy-done((bf16[8,64,512]{2,1,0:T(8,128)(2,1)}, bf16[8,64,512]{2,1,0:T(8,128)(2,1)S(1)}, u32[]{:S(2)}) %copy-start.25) | copy-done | bytes 524312
  72.4 5.8 %key_grad.1 = bf16[128,512]{1,0:T(8,128)(2,1)} custom-call(s32[69]{0:T(128)} %copy-done.15, bf16[128,512]{1,0:T(8,128)(2,1)} %get-tuple-element.30.key_hbm, bf16[128,512]{1,0:T(8,128)(2,1)} %get-tuple-element.31.value_hbm, bf16[512,512]{1,0:T(8,128)(2,1)} %wq_hbm.3, bf16[512,512]{1,0:T(8,128)(2,1)} %get-tuple-element.32.wkt_hbm, ...), custom_call_target="tpu_custom_call" | custom-call | flops 1000000000 | bytes 4000000 | tf_op jit(solution)/shard_map/key_grad/pallas_call | solution.py:570
  (79 shorter events, 0.4 us)
Async XLA Ops:
  1.3 7.4 %copy-start.11 = (bf16[128,512]{1,0:T(8,128)(2,1)S(1)}, bf16[128,512]{1,0:T(8,128)(2,1)}, u32[]{:S(2)}) copy-start(bf16[128,512]{1,0:T(8,128)(2,1)} %cot_ref.1) | copy-start | bytes 393220
  2.9 9.0 %copy-start.19 = (bf16[1,144,512]{2,1,0:T(8,128)(2,1)S(1)}, bf16[1,144,512]{2,1,0:T(8,128)(2,1)}, u32[]{:S(2)}) copy-start(bf16[1,144,512]{2,1,0:T(8,128)(2,1)} %pack.1) | copy-start | bytes 442372
  2.9 13.3 %collective-permute-start.2 = (bf16[1,144,512]{2,1,0:T(8,128)(2,1)}, bf16[1,144,512]{2,1,0:T(8,128)(2,1)S(1)}, u32[]{:S(2)}, u32[]{:S(2)}) collective-permute-start(bf16[1,144,512]{2,1,0:T(8,128)(2,1)} %pack.1), channel_id=1, source_target_pairs={{0,6},{1,7},{2,4},{3,5},{4,2},{5,3},{6,0},{7,1},{8,14},{9,15},{10,... | collective-permute-start | bytes 442376 | tf_op jit(solution)/shard_map/ppermute | solution.py:415
  8.1 12.7 %collective-permute-start.1 = (bf16[1,144,512]{2,1,0:T(8,128)(2,1)}, bf16[1,144,512]{2,1,0:T(8,128)(2,1)S(1)}, u32[]{:S(2)}, u32[]{:S(2)}) collective-permute-start(bf16[1,144,512]{2,1,0:T(8,128)(2,1)} %pack.1), channel_id=1, source_target_pairs={{0,4},{1,5},{2,6},{3,7},{4,0},{5,1},{6,2},{7,3},{8,12},{9,13},{10,... | collective-permute-start | bytes 442376 | tf_op jit(solution)/shard_map/ppermute | solution.py:415
  8.1 12.7 %collective-permute-start = (bf16[1,144,512]{2,1,0:T(8,128)(2,1)}, bf16[1,144,512]{2,1,0:T(8,128)(2,1)S(1)}, u32[]{:S(2)}, u32[]{:S(2)}) collective-permute-start(bf16[1,144,512]{2,1,0:T(8,128)(2,1)} %pack.1), channel_id=1, source_target_pairs={{0,2},{1,3},{2,0},{3,1},{4,6},{5,7},{6,4},{7,5},{8,10},{9,11},{10,... | collective-permute-start | bytes 442376 | tf_op jit(solution)/shard_map/ppermute | solution.py:415
  8.7 4.3 %collective-permute-start.3 = (bf16[1,64,512]{2,1,0:T(8,128)(2,1)S(1)}, bf16[1,64,512]{2,1,0:T(8,128)(2,1)S(1)}, u32[]{:S(2)}, u32[]{:S(2)}) collective-permute-start(bf16[1,64,512]{2,1,0:T(8,128)(2,1)S(1)} %get-tuple-element.50), channel_id=1, source_target_pairs={{0,8},{1,9},{2,10},{3,11},{4,12},{5,13},{6,14},{7,15},{8,0},{9,1},... | collective-permute-start | bytes 196616 | tf_op jit(solution)/shard_map/ppermute | solution.py:415
  10.4 5.2 %collective-permute-start.4 = (bf16[1,64,512]{2,1,0:T(8,128)(2,1)S(1)}, bf16[1,64,512]{2,1,0:T(8,128)(2,1)S(1)}, u32[]{:S(2)}, u32[]{:S(2)}) collective-permute-start(bf16[1,64,512]{2,1,0:T(8,128)(2,1)S(1)} %get-tuple-element.51), channel_id=1, source_target_pairs={{0,16},{1,17},{2,18},{3,19},{4,20},{5,21},{6,22},{7,23},{8,24},{9,... | collective-permute-start | bytes 196616 | tf_op jit(solution)/shard_map/ppermute | solution.py:415
  13.0 8.7 %collective-permute-start.7 = (bf16[1,144,512]{2,1,0:T(8,128)(2,1)S(1)}, bf16[1,144,512]{2,1,0:T(8,128)(2,1)S(1)}, u32[]{:S(2)}, u32[]{:S(2)}) collective-permute-start(bf16[1,144,512]{2,1,0:T(8,128)(2,1)S(1)} %copy-done.19), channel_id=1, source_target_pairs={{0,24},{1,25},{2,26},{3,27},{4,28},{5,29},{6,30},{7,31},{8,16},{9,... | collective-permute-start | bytes 442376 | tf_op jit(solution)/shard_map/ppermute | solution.py:415
  15.6 6.1 %collective-permute-start.6 = (bf16[1,144,512]{2,1,0:T(8,128)(2,1)S(1)}, bf16[1,144,512]{2,1,0:T(8,128)(2,1)S(1)}, u32[]{:S(2)}, u32[]{:S(2)}) collective-permute-start(bf16[1,144,512]{2,1,0:T(8,128)(2,1)S(1)} %copy-done.19), channel_id=1, source_target_pairs={{0,16},{1,17},{2,18},{3,19},{4,20},{5,21},{6,22},{7,23},{8,24},{9,... | collective-permute-start | bytes 442376 | tf_op jit(solution)/shard_map/ppermute | solution.py:415
  16.2 0.7 copy-start.26
  16.2 5.5 %collective-permute-start.5 = (bf16[1,144,512]{2,1,0:T(8,128)(2,1)S(1)}, bf16[1,144,512]{2,1,0:T(8,128)(2,1)S(1)}, u32[]{:S(2)}, u32[]{:S(2)}) collective-permute-start(bf16[1,144,512]{2,1,0:T(8,128)(2,1)S(1)} %copy-done.19), channel_id=1, source_target_pairs={{0,8},{1,9},{2,10},{3,11},{4,12},{5,13},{6,14},{7,15},{8,0},{9,1},... | collective-permute-start | bytes 442376 | tf_op jit(solution)/shard_map/ppermute | solution.py:415
  20.8 0.9 %slice-start = ((bf16[1,144,512]{2,1,0:T(8,128)(2,1)}), bf16[1,128,512]{2,1,0:T(8,128)(2,1)S(1)}, s32[]{:S(2)}) async-start(bf16[1,144,512]{2,1,0:T(8,128)(2,1)} %copy-done.26), calls=%async_computation.1 | async-start | bytes 262144 | tf_op jit(solution)/shard_map/slice | solution.py:499
  21.8 7.6 %copy-start.27 = (bf16[1,144,512]{2,1,0:T(8,128)(2,1)S(1)}, bf16[1,144,512]{2,1,0:T(8,128)(2,1)}, u32[]{:S(2)}) copy-start(bf16[1,144,512]{2,1,0:T(8,128)(2,1)} %copy-done.26) | copy-start | bytes 442372
  21.8 23.7 %copy-start = (bf16[7,128,512]{2,1,0:T(8,128)(2,1)}, bf16[7,128,512]{2,1,0:T(8,128)(2,1)S(1)}, u32[]{:S(2)}) copy-start(bf16[7,128,512]{2,1,0:T(8,128)(2,1)S(1)} %constant_dynamic-update-slice_fusion.refs_0_) | copy-start | bytes 2752516
  21.9 8.3 %collective-permute-start.8 = (bf16[4,64,512]{2,1,0:T(8,128)(2,1)S(1)}, bf16[4,64,512]{2,1,0:T(8,128)(2,1)S(1)}, u32[]{:S(2)}, u32[]{:S(2)}) collective-permute-start(bf16[4,64,512]{2,1,0:T(8,128)(2,1)S(1)} %pad_maximum_fusion.3), channel_id=1, source_target_pairs={{0,2},{1,3},{2,0},{3,1},{4,6},{5,7},{6,4},{7,5},{8,10},{9,11},{10,... | collective-permute-start | bytes 786440 | tf_op jit(solution)/shard_map/ppermute | solution.py:415
  24.4 15.1 %collective-permute-start.12 = (bf16[3,128,512]{2,1,0:T(8,128)(2,1)S(1)}, bf16[3,128,512]{2,1,0:T(8,128)(2,1)S(1)}, u32[]{:S(2)}, u32[]{:S(2)}) collective-permute-start(bf16[3,128,512]{2,1,0:T(8,128)(2,1)S(1)} %pad_maximum_fusion.2), channel_id=1, source_target_pairs={{0,24},{1,25},{2,26},{3,27},{4,28},{5,29},{6,30},{7,31},{8,16},{9,... | collective-permute-start | bytes 1179656 | tf_op jit(solution)/shard_map/ppermute | solution.py:415
  26.9 15.6 %collective-permute-start.11 = (bf16[3,128,512]{2,1,0:T(8,128)(2,1)S(1)}, bf16[3,128,512]{2,1,0:T(8,128)(2,1)S(1)}, u32[]{:S(2)}, u32[]{:S(2)}) collective-permute-start(bf16[3,128,512]{2,1,0:T(8,128)(2,1)S(1)} %pad_maximum_fusion.2), channel_id=1, source_target_pairs={{0,16},{1,17},{2,18},{3,19},{4,20},{5,21},{6,22},{7,23},{8,24},{9,... | collective-permute-start | bytes 1179656 | tf_op jit(solution)/shard_map/ppermute | solution.py:415
  27.4 15.1 %collective-permute-start.10 = (bf16[3,128,512]{2,1,0:T(8,128)(2,1)S(1)}, bf16[3,128,512]{2,1,0:T(8,128)(2,1)S(1)}, u32[]{:S(2)}, u32[]{:S(2)}) collective-permute-start(bf16[3,128,512]{2,1,0:T(8,128)(2,1)S(1)} %pad_maximum_fusion.2), channel_id=1, source_target_pairs={{0,8},{1,9},{2,10},{3,11},{4,12},{5,13},{6,14},{7,15},{8,0},{9,1},... | collective-permute-start | bytes 1179656 | tf_op jit(solution)/shard_map/ppermute | solution.py:415
  27.9 11.6 %collective-permute-start.17 = (bf16[4,64,512]{2,1,0:T(8,128)(2,1)S(1)}, bf16[4,64,512]{2,1,0:T(8,128)(2,1)S(1)}, u32[]{:S(2)}, u32[]{:S(2)}) collective-permute-start(bf16[4,64,512]{2,1,0:T(8,128)(2,1)S(1)} %pad_maximum_fusion.3), channel_id=1, source_target_pairs={{0,4},{1,5},{2,6},{3,7},{4,0},{5,1},{6,2},{7,3},{8,12},{9,13},{10,... | collective-permute-start | bytes 786440 | tf_op jit(solution)/shard_map/ppermute | solution.py:415
  30.2 15.3 %collective-permute-start.13 = (bf16[7,128,512]{2,1,0:T(8,128)(2,1)S(1)}, bf16[7,128,512]{2,1,0:T(8,128)(2,1)S(1)}, u32[]{:S(2)}, u32[]{:S(2)}) collective-permute-start(bf16[7,128,512]{2,1,0:T(8,128)(2,1)S(1)} %constant_dynamic-update-slice_fusion.refs_0_), channel_id=1, source_target_pairs={{0,1},{1,0},{2,3},{3,2},{4,5},{5,4},{6,7},{7,6},{8,9},{9,8},{10,11... | collective-permute-start | bytes 2752520 | tf_op jit(solution)/shard_map/ppermute | solution.py:415
  34.9 0.5 copy-start.15
  34.9 10.7 %copy-start.13 = (bf16[4,128,256]{2,1,0:T(8,128)(2,1)S(1)}, bf16[4,128,256]{2,1,0:T(8,128)(2,1)}, u32[]{:S(2)}) copy-start(bf16[4,128,256]{2,1,0:T(8,128)(2,1)} %get-tuple-element.26.stack_ref.stack_hbm) | copy-start | bytes 786436
  39.5 3.5 %collective-permute-start.9 = (bf16[4,16,128]{2,1,0:T(8,128)(2,1)S(1)}, bf16[4,16,128]{2,1,0:T(8,128)(2,1)S(1)}, u32[]{:S(2)}, u32[]{:S(2)}) collective-permute-start(bf16[4,16,128]{2,1,0:T(8,128)(2,1)S(1)} %pad_maximum_fusion.4), channel_id=1, source_target_pairs={{0,1},{1,0},{2,3},{3,2},{4,5},{5,4},{6,7},{7,6},{8,9},{9,8},{10,11... | collective-permute-start | bytes 49160 | tf_op jit(solution)/shard_map/ppermute | solution.py:415
  39.5 6.1 %copy-start.4 = (bf16[3,128,512]{2,1,0:T(8,128)(2,1)}, bf16[3,128,512]{2,1,0:T(8,128)(2,1)S(1)}, u32[]{:S(2)}) copy-start(bf16[3,128,512]{2,1,0:T(8,128)(2,1)S(1)} %collective-permute-done.12.refs_3_) | copy-start | bytes 1179652
  39.5 6.0 %collective-permute-start.16 = (bf16[3,128,512]{2,1,0:T(8,128)(2,1)S(1)}, bf16[3,128,512]{2,1,0:T(8,128)(2,1)S(1)}, u32[]{:S(2)}, u32[]{:S(2)}) collective-permute-start(bf16[3,128,512]{2,1,0:T(8,128)(2,1)S(1)} %collective-permute-done.12.refs_3_), channel_id=1, source_target_pairs={{0,1},{1,0},{2,3},{3,2},{4,5},{5,4},{6,7},{7,6},{8,9},{9,8},{10,11... | collective-permute-start | bytes 1179656 | tf_op jit(solution)/shard_map/ppermute | solution.py:415
  42.5 3.1 %copy-start.5 = (bf16[3,128,512]{2,1,0:T(8,128)(2,1)}, bf16[3,128,512]{2,1,0:T(8,128)(2,1)S(1)}, u32[]{:S(2)}) copy-start(bf16[3,128,512]{2,1,0:T(8,128)(2,1)S(1)} %collective-permute-done.11.refs_2_) | copy-start | bytes 1179652
  42.5 3.0 %collective-permute-start.15 = (bf16[3,128,512]{2,1,0:T(8,128)(2,1)S(1)}, bf16[3,128,512]{2,1,0:T(8,128)(2,1)S(1)}, u32[]{:S(2)}, u32[]{:S(2)}) collective-permute-start(bf16[3,128,512]{2,1,0:T(8,128)(2,1)S(1)} %collective-permute-done.11.refs_2_), channel_id=1, source_target_pairs={{0,1},{1,0},{2,3},{3,2},{4,5},{5,4},{6,7},{7,6},{8,9},{9,8},{10,11... | collective-permute-start | bytes 1179656 | tf_op jit(solution)/shard_map/ppermute | solution.py:415
  42.5 3.1 %copy-start.6 = (bf16[3,128,512]{2,1,0:T(8,128)(2,1)}, bf16[3,128,512]{2,1,0:T(8,128)(2,1)S(1)}, u32[]{:S(2)}) copy-start(bf16[3,128,512]{2,1,0:T(8,128)(2,1)S(1)} %collective-permute-done.10.refs_1_) | copy-start | bytes 1179652
  42.5 3.0 %collective-permute-start.14 = (bf16[3,128,512]{2,1,0:T(8,128)(2,1)S(1)}, bf16[3,128,512]{2,1,0:T(8,128)(2,1)S(1)}, u32[]{:S(2)}, u32[]{:S(2)}) collective-permute-start(bf16[3,128,512]{2,1,0:T(8,128)(2,1)S(1)} %collective-permute-done.10.refs_1_), channel_id=1, source_target_pairs={{0,1},{1,0},{2,3},{3,2},{4,5},{5,4},{6,7},{7,6},{8,9},{9,8},{10,11... | collective-permute-start | bytes 1179656 | tf_op jit(solution)/shard_map/ppermute | solution.py:415
  43.0 2.6 %copy-start.10 = (bf16[512,512]{1,0:T(8,128)(2,1)S(1)}, bf16[512,512]{1,0:T(8,128)(2,1)}, u32[]{:S(2)}) copy-start(bf16[512,512]{1,0:T(8,128)(2,1)} %get-tuple-element.27.wvt_ref.wvt_hbm) | copy-start | bytes 1572868
  43.0 2.6 %copy-start.2 = (bf16[512,512]{1,0:T(8,128)(2,1)S(1)}, bf16[512,512]{1,0:T(8,128)(2,1)}, u32[]{:S(2)}) copy-start(bf16[512,512]{1,0:T(8,128)(2,1)} %wk_hbm.3) | copy-start | bytes 1572868
  43.0 8.4 %collective-permute-start.18 = (bf16[4,64,512]{2,1,0:T(8,128)(2,1)S(1)}, bf16[4,64,512]{2,1,0:T(8,128)(2,1)S(1)}, u32[]{:S(2)}, u32[]{:S(2)}) collective-permute-start(bf16[4,64,512]{2,1,0:T(8,128)(2,1)S(1)} %collective-permute-done.17), channel_id=1, source_target_pairs={{0,2},{1,3},{2,0},{3,1},{4,6},{5,7},{6,4},{7,5},{8,10},{9,11},{10,... | collective-permute-start | bytes 786440 | tf_op jit(solution)/shard_map/ppermute | solution.py:415
  43.8 1.8 %copy-start.3 = (s32[240,128,4]{1,2,0:T(4,128)S(1)}, s32[240,128,4]{1,2,0:T(4,128)}, u32[]{:S(2)}) copy-start(s32[240,128,4]{1,2,0:T(4,128)} %param.15) | copy-start | bytes 1474564
  43.8 1.8 %copy-start.12 = (bf16[128,512]{1,0:T(8,128)(2,1)S(1)}, bf16[128,512]{1,0:T(8,128)(2,1)}, u32[]{:S(2)}) copy-start(bf16[128,512]{1,0:T(8,128)(2,1)} %cot_ref.1) | copy-start | bytes 393220
  45.5 3.1 %copy-start.14 = (s32[133]{0:T(256)}, s32[133]{0:T(256)S(1)}, u32[]{:S(2)}) copy-start(s32[133]{0:T(256)S(1)} %query_work.1.work_ref) | copy-start | bytes 1600
  45.5 3.1 %copy-start.7 = (bf16[3,128,512]{2,1,0:T(8,128)(2,1)}, bf16[3,128,512]{2,1,0:T(8,128)(2,1)S(1)}, u32[]{:S(2)}) copy-start(bf16[3,128,512]{2,1,0:T(8,128)(2,1)S(1)} %collective-permute-done.16.refs_7_) | copy-start | bytes 1179652
  45.5 3.1 %copy-start.8 = (bf16[3,128,512]{2,1,0:T(8,128)(2,1)}, bf16[3,128,512]{2,1,0:T(8,128)(2,1)S(1)}, u32[]{:S(2)}) copy-start(bf16[3,128,512]{2,1,0:T(8,128)(2,1)S(1)} %collective-permute-done.15.refs_6_) | copy-start | bytes 1179652
  45.5 3.1 %copy-start.9 = (bf16[3,128,512]{2,1,0:T(8,128)(2,1)}, bf16[3,128,512]{2,1,0:T(8,128)(2,1)S(1)}, u32[]{:S(2)}) copy-start(bf16[3,128,512]{2,1,0:T(8,128)(2,1)S(1)} %collective-permute-done.14.refs_5_) | copy-start | bytes 1179652
  45.5 3.0 %copy-start.1 = (bf16[7,128,512]{2,1,0:T(8,128)(2,1)}, bf16[7,128,512]{2,1,0:T(8,128)(2,1)S(1)}, u32[]{:S(2)}) copy-start(bf16[7,128,512]{2,1,0:T(8,128)(2,1)S(1)} %collective-permute-done.13.refs_4_) | copy-start | bytes 2752516
  51.5 5.1 %copy-start.16 = (bf16[8,64,512]{2,1,0:T(8,128)(2,1)}, bf16[8,64,512]{2,1,0:T(8,128)(2,1)S(1)}, u32[]{:S(2)}) copy-start(bf16[8,64,512]{2,1,0:T(8,128)(2,1)S(1)} %pad_maximum_fusion.refs_8_) | copy-start | bytes 1572868
  51.5 17.3 %collective-permute-start.19 = (bf16[8,64,512]{2,1,0:T(8,128)(2,1)S(1)}, bf16[8,64,512]{2,1,0:T(8,128)(2,1)S(1)}, u32[]{:S(2)}, u32[]{:S(2)}) collective-permute-start(bf16[8,64,512]{2,1,0:T(8,128)(2,1)S(1)} %pad_maximum_fusion.refs_8_), channel_id=1, source_target_pairs={{0,16},{1,17},{2,18},{3,19},{4,20},{5,21},{6,22},{7,23},{8,24},{9,... | collective-permute-start | bytes 1572872 | tf_op jit(solution)/shard_map/ppermute | solution.py:415
  52.5 9.2 %copy-start.17 = (bf16[8,64,512]{2,1,0:T(8,128)(2,1)}, bf16[8,64,512]{2,1,0:T(8,128)(2,1)S(1)}, u32[]{:S(2)}) copy-start(bf16[8,64,512]{2,1,0:T(8,128)(2,1)S(1)} %pad_maximum_fusion.1.refs_12_) | copy-start | bytes 1572868
  52.5 16.3 %collective-permute-start.22 = (bf16[8,64,512]{2,1,0:T(8,128)(2,1)S(1)}, bf16[8,64,512]{2,1,0:T(8,128)(2,1)S(1)}, u32[]{:S(2)}, u32[]{:S(2)}) collective-permute-start(bf16[8,64,512]{2,1,0:T(8,128)(2,1)S(1)} %pad_maximum_fusion.1.refs_12_), channel_id=1, source_target_pairs={{0,8},{1,9},{2,10},{3,11},{4,12},{5,13},{6,14},{7,15},{8,0},{9,1},... | collective-permute-start | bytes 1572872 | tf_op jit(solution)/shard_map/ppermute | solution.py:415
  54.0 14.7 %all-to-all-start = ((f32[32,16,128]{2,1,0:T(8,128)}), f32[32,16,128]{2,1,0:T(8,128)S(1)}, u32[]{:S(2)}, u32[]{:S(2)}) async-start(f32[32,16,128]{2,1,0:T(8,128)} %get-tuple-element.34.stats_hbm), calls=%async_computation | async-start | bytes 524288 | tf_op jit(solution)/shard_map/all_to_all | solution.py:549
  56.6 12.7 %collective-permute-start.20 = (bf16[8,64,512]{2,1,0:T(8,128)(2,1)S(1)}, bf16[8,64,512]{2,1,0:T(8,128)(2,1)S(1)}, u32[]{:S(2)}, u32[]{:S(2)}) collective-permute-start(bf16[8,64,512]{2,1,0:T(8,128)(2,1)S(1)} %pad_maximum_fusion.refs_8_), channel_id=1, source_target_pairs={{0,1},{1,0},{2,3},{3,2},{4,5},{5,4},{6,7},{7,6},{8,9},{9,8},{10,11... | collective-permute-start | bytes 1572872 | tf_op jit(solution)/shard_map/ppermute | solution.py:415
  57.0 12.4 %collective-permute-start.23 = (bf16[8,64,512]{2,1,0:T(8,128)(2,1)S(1)}, bf16[8,64,512]{2,1,0:T(8,128)(2,1)S(1)}, u32[]{:S(2)}, u32[]{:S(2)}) collective-permute-start(bf16[8,64,512]{2,1,0:T(8,128)(2,1)S(1)} %pad_maximum_fusion.1.refs_12_), channel_id=1, source_target_pairs={{0,1},{1,0},{2,3},{3,2},{4,5},{5,4},{6,7},{7,6},{8,9},{9,8},{10,11... | collective-permute-start | bytes 1572872 | tf_op jit(solution)/shard_map/ppermute | solution.py:415
  68.8 2.7 %copy-start.18 = (f32[32,16,128]{2,1,0:T(8,128)}, f32[32,16,128]{2,1,0:T(8,128)S(1)}, u32[]{:S(2)}) copy-start(f32[32,16,128]{2,1,0:T(8,128)S(1)} %all-to-all-done.stats_all_ref) | copy-start | bytes 786436
  68.8 2.7 %copy-start.20 = (bf16[8,64,512]{2,1,0:T(8,128)(2,1)}, bf16[8,64,512]{2,1,0:T(8,128)(2,1)S(1)}, u32[]{:S(2)}) copy-start(bf16[8,64,512]{2,1,0:T(8,128)(2,1)S(1)} %collective-permute-done.19.refs_9_) | copy-start | bytes 1572868
  68.8 2.0 %collective-permute-start.21 = (bf16[8,64,512]{2,1,0:T(8,128)(2,1)S(1)}, bf16[8,64,512]{2,1,0:T(8,128)(2,1)S(1)}, u32[]{:S(2)}, u32[]{:S(2)}) collective-permute-start(bf16[8,64,512]{2,1,0:T(8,128)(2,1)S(1)} %collective-permute-done.19.refs_9_), channel_id=1, source_target_pairs={{0,1},{1,0},{2,3},{3,2},{4,5},{5,4},{6,7},{7,6},{8,9},{9,8},{10,11... | collective-permute-start | bytes 1572872 | tf_op jit(solution)/shard_map/ppermute | solution.py:415
  68.9 2.6 %copy-start.21 = (bf16[8,64,512]{2,1,0:T(8,128)(2,1)}, bf16[8,64,512]{2,1,0:T(8,128)(2,1)S(1)}, u32[]{:S(2)}) copy-start(bf16[8,64,512]{2,1,0:T(8,128)(2,1)S(1)} %collective-permute-done.22.refs_13_) | copy-start | bytes 1572868
  68.9 2.6 %collective-permute-start.24 = (bf16[8,64,512]{2,1,0:T(8,128)(2,1)S(1)}, bf16[8,64,512]{2,1,0:T(8,128)(2,1)S(1)}, u32[]{:S(2)}, u32[]{:S(2)}) collective-permute-start(bf16[8,64,512]{2,1,0:T(8,128)(2,1)S(1)} %collective-permute-done.22.refs_13_), channel_id=1, source_target_pairs={{0,1},{1,0},{2,3},{3,2},{4,5},{5,4},{6,7},{7,6},{8,9},{9,8},{10,11... | collective-permute-start | bytes 1572872 | tf_op jit(solution)/shard_map/ppermute | solution.py:415
  69.4 2.2 %copy-start.22 = (bf16[8,64,512]{2,1,0:T(8,128)(2,1)}, bf16[8,64,512]{2,1,0:T(8,128)(2,1)S(1)}, u32[]{:S(2)}) copy-start(bf16[8,64,512]{2,1,0:T(8,128)(2,1)S(1)} %collective-permute-done.20.refs_10_) | copy-start | bytes 1572868
  69.4 2.2 %copy-start.23 = (bf16[8,64,512]{2,1,0:T(8,128)(2,1)}, bf16[8,64,512]{2,1,0:T(8,128)(2,1)S(1)}, u32[]{:S(2)}) copy-start(bf16[8,64,512]{2,1,0:T(8,128)(2,1)S(1)} %collective-permute-done.23.refs_14_) | copy-start | bytes 1572868
  70.8 0.8 %copy-start.24 = (bf16[8,64,512]{2,1,0:T(8,128)(2,1)}, bf16[8,64,512]{2,1,0:T(8,128)(2,1)S(1)}, u32[]{:S(2)}) copy-start(bf16[8,64,512]{2,1,0:T(8,128)(2,1)S(1)} %collective-permute-done.21.refs_11_) | copy-start | bytes 1572868
  71.6 0.8 %copy-start.25 = (bf16[8,64,512]{2,1,0:T(8,128)(2,1)}, bf16[8,64,512]{2,1,0:T(8,128)(2,1)S(1)}, u32[]{:S(2)}) copy-start(bf16[8,64,512]{2,1,0:T(8,128)(2,1)S(1)} %collective-permute-done.24.refs_15_) | copy-start | bytes 1572868

commit v2 on v0

--- a/solution.py
+++ b/solution.py
@@ -232,7 +232,7 @@
 def forward_kernel(sizes, work_ref, stack_ref, cot_ref, wk_ref, wvt_ref, mask_ref, *refs):
     count = 2 * sizes[0]
     groups, refs = refs[:count], refs[count:]
-    out_ref, sent_ref, stats_ref, buf, words, bias_ref, max_ref, sum_ref, acc_ref, score_ref, sems = refs
+    out_ref, sent_ref, stats_ref, buf, words, bias_ref, max_ref, sum_ref, acc_ref, score_ref, expo_ref, sems = refs
     layout = Layout(*sizes)
     block, width = cot_ref.shape
     head = width // HEADS
@@ -251,16 +251,20 @@
             scores = dot(keys[:, 2 * head * p : 2 * head * (p + 1)], stack_ref[p])
             for e in range(2):
                 score_ref[2 * p + e] = scores[:, block * e : block * (e + 1)] + bias_ref[...]
+        old = max_ref[...]
+        tops = [jnp.max(score_ref[h], axis=0, keepdims=True) for h in range(HEADS)]
+        new = jnp.maximum(old, jnp.concatenate(tops, 0))
+        fade = jnp.exp(old - new)
+        max_ref[...] = new
+        sums = []
         for h in range(HEADS):
-            s = score_ref[h]
-            old = max_ref[h : h + 1]
-            new = jnp.maximum(old, jnp.max(s, axis=0, keepdims=True))
-            fade = jnp.exp(old - new)
-            expo = jnp.exp(s - new)
-            max_ref[h : h + 1] = new
-            sum_ref[h : h + 1] = sum_ref[h : h + 1] * fade + jnp.sum(expo, axis=0, keepdims=True)
+            expo = jnp.exp(score_ref[h] - new[h : h + 1])
+            sums.append(jnp.sum(expo, axis=0, keepdims=True))
+            expo_ref[h] = expo.astype(jnp.bfloat16)
+        sum_ref[...] = sum_ref[...] * fade + jnp.concatenate(sums, 0)
+        for h in range(HEADS):
             at = slice(head * h, head * (h + 1))
-            acc_ref[at] = acc_ref[at] * fade + dot(values[at], expo.astype(jnp.bfloat16))
+            acc_ref[at] = acc_ref[at] * fade[h : h + 1] + dot(values[at], expo_ref[h])
 
     run_steps(work_ref, rows_in.start, rows_in.wait, tiles)
     inverse = 1.0 / sum_ref[...]
@@ -335,7 +339,8 @@
     groups, refs = refs[:count], refs[count:]
     halves, refs = (refs[:readers], refs[readers : 2 * readers]), refs[2 * readers :]
     out_ref, key_ref, value_ref, part_ref, wq_ref, wkt_ref, wvt_ref, buf, words, cot_buf, stats, bias_ref = refs[:12]
-    query_stack_ref, cot_stack_ref, score_ref, d_prob_ref, key_acc, value_acc, sems, c_sems, w_sems = refs[12:]
+    query_stack_ref, cot_stack_ref, score_ref, d_prob_ref, prob_ref, d_score_ref = refs[12:18]
+    key_acc, value_acc, sems, c_sems, w_sems = refs[18:]
     layout = Layout(*sizes)
     block, width = out_ref.shape
     head = width // HEADS
@@ -381,20 +386,18 @@
             cot_stack_ref[p] = jnp.concatenate([pair_stack(cots[of, pair]) for of in of_tile], 0)
             score_ref[p] = dot(key_ref[:, pair], query_stack_ref[p], NT)
             d_prob_ref[p] = dot(value_ref[:, pair], cot_stack_ref[p], NT)
-        for p, pair in enumerate(pairs):
-            probs, d_scores = [], []
+        for p in range(HEADS // 2):
             for t in range(TILES):
                 for e in range(2):
                     h = 2 * p + e
                     of = slice(block * (2 * t + e), block * (2 * t + e + 1))
-                    prob, d_score = tile_grads(
+                    prob_ref[p, :, of], d_score_ref[p, :, of] = tile_grads(
                         score_ref[p, :, of] + bias_ref[of_tile[t]], d_prob_ref[p, :, of], stats[slot, t, h : h + 1],
                         stats[slot, t, HEADS + h : HEADS + h + 1],
                     )
-                    probs.append(prob)
-                    d_scores.append(d_score)
-            value_acc[:, pair] += dot(jnp.concatenate(probs, 1), cot_stack_ref[p])
-            key_acc[:, pair] += dot(jnp.concatenate(d_scores, 1), query_stack_ref[p])
+        for p, pair in enumerate(pairs):
+            value_acc[:, pair] += dot(prob_ref[p], cot_stack_ref[p])
+            key_acc[:, pair] += dot(d_score_ref[p], query_stack_ref[p])
 
     run_steps(work_ref, start, wait, tiles)
     for copy in loads:
@@ -502,7 +505,7 @@
     near = jnp.concatenate([entry[:, :block] for entry in columns] + [line], 0)
 
     pairs = [part for k in range(2) for part in (cot_parts[k], cot_other[k])]
-    pieces = [after(jnp.concatenate(pairs, 0), near)]
+    pieces = [after(jnp.concatenate(pairs, 0), line)]
     done_first = (key_work, prepared)
     mask = blks // 2
     while mask > 1:
@@ -510,11 +513,11 @@
         mask //= 2
 
     line_lists = jnp.concatenate([entry[:, block:, :128] for entry in lined], 0)
-    line_lists = after(line_lists, pieces[lines // 2])
+    line_lists = after(line_lists, there[-1])
     row_lists = jnp.concatenate([line_lists, swap(line_lists, 1)], 0)
     query_work = work(query_work_kernel, row_lists, blks, "query_work")
     here = [near] + there
-    rows_all = here + [swap(group, 1) for group in here]
+    rows_all = here + [swap(after(near, there[-1]), 1)] + [swap(group, 1) for group in there]
 
     cots_here = []
     for k in range(2):
@@ -530,6 +533,8 @@
     per_head = pltpu.VMEM((HEADS, block), f32)
     own_stats = pltpu.VMEM((2 * HEADS, block), f32)
     met = pltpu.VMEM((HEADS, TILES * block, block), f32)
+    met_low = pltpu.VMEM((HEADS, TILES * block, block), bf16)
+    pair_low = pltpu.VMEM((HEADS // 2, block, 2 * TILES * block), bf16)
     pair_met = pltpu.VMEM((HEADS // 2, block, 2 * TILES * block), f32)
     pair_rows = pltpu.VMEM((HEADS // 2, 2 * TILES * block, 2 * head), bf16)
     row_sems = pltpu.SemaphoreType.DMA((2, TILES, 2))
@@ -539,7 +544,9 @@
         out_shape=(own, shape((devices, 2 * HEADS, block), f32)),
         in_specs=[SMEM] + [VMEM] * 4 + [HBM] * (1 + 2 * readers),
         out_specs=(VMEM, VMEM),
-        scratch_shapes=[own_stats, buffer, word_buffer, bias, per_head, per_head, turned, met, row_sems],
+        scratch_shapes=[
+            own_stats, buffer, word_buffer, bias, per_head, per_head, turned, met, met_low, row_sems,
+        ],
         compiler_params=some,
         cost_estimate=cost(5),
         name="forward",
@@ -574,7 +581,7 @@
         scratch_shapes=[
             rows_low, rows_low, rows_wide, weight, weight, weight,
             buffer, word_buffer, buffer, pltpu.VMEM((2, TILES, 2 * HEADS, block), f32), bias,
-            pair_rows, pair_rows, pair_met, pair_met, rows_wide, rows_wide,
+            pair_rows, pair_rows, pair_met, pair_met, pair_low, pair_low, rows_wide, rows_wide,
             row_sems, pltpu.SemaphoreType.DMA((2, TILES, 3)), pltpu.SemaphoreType.DMA((6,)),
         ],
         compiler_params=most,

time: 79.4 us -> 79.9 us (level)
  waiting for transfers between devices: 24.4 us -> 20.7 us
  Pallas kernels: 21.2 us -> 24.1 us
    ppermute x25, waiting for transfers between devices: 19.2 us -> 16.5 us  [swap(): return lax.ppermute(block, axes, [(i, i ^ mask) for i in range(count)])]
    pallas_call x1, Pallas kernels: 2.9 us -> 4.59 us  [local(): pl.pallas_call(functools.partial(forward_kernel, sizes), out_shape=(own,...]
    all_to_all x1, waiting for transfers between devices: 5.26 us -> 4.22 us  [local(): stats_all = lax.all_to_all(stats, axes, 0, 0, tiled=True)]
    pallas_call x1, Pallas kernels: 4.52 us -> 5.55 us  [local(): pl.pallas_call(functools.partial(query_grad_kernel, sizes), out_shape=sha...]
    unnamed x56 -> x60, local copies, waits for them, and re-layouts: 1.58 us -> 1.91 us
  transfers between devices with their start and end apart: 26 -> 26, of which waited for: 8 -> 8; matrix products, arithmetic and copies ran while one was open for 1% -> 1% of each run, Pallas kernels for 17% -> 21%
where the time goes in v2:
time: 79.9 us; the launch traced here: 79.4 us
  starting transfers between devices  29.6 us (37%)
  Pallas kernels  24.1 us (30%)
  waiting for transfers between devices  20.7 us (26%)
  local copies, waits for them, and re-layouts  2.93 us (4%)
  between operations  1.87 us (2%)
    ppermute x25, starting transfers between devices, swap(): return lax.ppermute(block, axes, [(i, i ^ mask) for i in range(count)])  26.2 us
    ppermute x25, waiting for transfers between devices, swap(): return lax.ppermute(block, axes, [(i, i ^ mask) for i in range(count)])  16.5 us
    pallas_call x1, Pallas kernels, local(): pl.pallas_call(functools.partial(key_grad_kernel, sizes, bits), out_shape...  5.87 us
    pallas_call x1, Pallas kernels, local(): pl.pallas_call(functools.partial(query_grad_kernel, sizes), out_shape=sha...  5.55 us
    pallas_call x1, Pallas kernels, local(): pl.pallas_call(functools.partial(forward_kernel, sizes), out_shape=(own,...  4.59 us
    all_to_all x1, waiting for transfers between devices, local(): stats_all = lax.all_to_all(stats, axes, 0, 0, tiled=True)  4.22 us
    pallas_call x1, Pallas kernels, local(): pl.pallas_call(prepare_kernel, out_shape=(stacks, stacks, own, own, squar...  3.59 us
    all_to_all x1, starting transfers between devices, local(): stats_all = lax.all_to_all(stats, axes, 0, 0, tiled=True)  3.33 us
  transfers between devices with their start and end apart: 26, of which 8 were waited for; matrix products, arithmetic and copies ran while one was open for 1% of the time, Pallas kernels for 21%

profile of v2, /device:TPU:0, one launch (start us, length us, event | category | flops | bytes accessed | tf_op | source)
XLA Modules:
  0.0 79.4 jit_solution(11307105095027301383)
XLA Ops:
  1.3 0.0 copy-start.11
  1.3 1.6 %pack.1 = bf16[1,144,512]{2,1,0:T(8,128)(2,1)} custom-call(bf16[128,512]{1,0:T(8,128)(2,1)} %own_hbm.2, s32[1,3,1,8]{3,2,1,0:T(1,128)} %bitcast.13, s32[1,1]{1,0:T(1,128)S(6)} %copy.14.count_hbm), custom_call_target="tpu_custom_call" | custom-call | tf_op jit(solution)/shard_map/pack/pallas_call | solution.py:444
  2.9 5.1 %collective-permute-start.2 = (bf16[1,144,512]{2,1,0:T(8,128)(2,1)}, bf16[1,144,512]{2,1,0:T(8,128)(2,1)S(1)}, u32[]{:S(2)}, u32[]{:S(2)}) collective-permute-start(bf16[1,144,512]{2,1,0:T(8,128)(2,1)} %pack.1), channel_id=1, source_target_pairs={{0,6},{1,7},{2,4},{3,5},{4,2},{5,3},{6,0},{7,1},{8,14},{9,15},{10,... | collective-permute-start | bytes 442376 | tf_op jit(solution)/shard_map/ppermute | solution.py:418
  8.1 0.0 collective-permute-start.1
  8.1 0.6 collective-permute-start
  8.7 1.7 %collective-permute-start.7 = (bf16[1,64,512]{2,1,0:T(8,128)(2,1)S(1)}, bf16[1,64,512]{2,1,0:T(8,128)(2,1)S(1)}, u32[]{:S(2)}, u32[]{:S(2)}) collective-permute-start(bf16[1,64,512]{2,1,0:T(8,128)(2,1)S(1)} %get-tuple-element.52), channel_id=1, source_target_pairs={{0,16},{1,17},{2,18},{3,19},{4,20},{5,21},{6,22},{7,23},{8,24},{9,... | collective-permute-start | bytes 196616 | tf_op jit(solution)/shard_map/ppermute | solution.py:418
  10.4 1.5 %collective-permute-start.6 = (bf16[1,64,512]{2,1,0:T(8,128)(2,1)S(1)}, bf16[1,64,512]{2,1,0:T(8,128)(2,1)S(1)}, u32[]{:S(2)}, u32[]{:S(2)}) collective-permute-start(bf16[1,64,512]{2,1,0:T(8,128)(2,1)S(1)} %get-tuple-element.53), channel_id=1, source_target_pairs={{0,8},{1,9},{2,10},{3,11},{4,12},{5,13},{6,14},{7,15},{8,0},{9,1},... | collective-permute-start | bytes 196616 | tf_op jit(solution)/shard_map/ppermute | solution.py:418
  12.0 1.1 %collective-permute-done.7 = bf16[1,64,512]{2,1,0:T(8,128)(2,1)S(1)} collective-permute-done((bf16[1,64,512]{2,1,0:T(8,128)(2,1)S(1)}, bf16[1,64,512]{2,1,0:T(8,128)(2,1)S(1)}, u32[]{:S(2)}, u32[]{:S(2)}) %collective-permute-start.7) | collective-permute-done | bytes 65568 | tf_op jit(solution)/shard_map/ppermute | solution.py:418
  13.0 2.6 %collective-permute-start.5 = (bf16[1,144,512]{2,1,0:T(8,128)(2,1)S(1)}, bf16[1,144,512]{2,1,0:T(8,128)(2,1)S(1)}, u32[]{:S(2)}, u32[]{:S(2)}) collective-permute-start(bf16[1,144,512]{2,1,0:T(8,128)(2,1)S(1)} %copy-done.19), channel_id=1, source_target_pairs={{0,24},{1,25},{2,26},{3,27},{4,28},{5,29},{6,30},{7,31},{8,16},{9,... | collective-permute-start | bytes 442376 | tf_op jit(solution)/shard_map/ppermute | solution.py:418
  15.6 0.0 collective-permute-done.6
  15.6 0.5 collective-permute-start.4
  16.1 0.0 collective-permute-done.2
  16.2 0.6 collective-permute-start.3
  16.8 0.1 copy-done.26
  16.8 3.9 %collective-permute-done.1 = bf16[1,144,512]{2,1,0:T(8,128)(2,1)S(1)} collective-permute-done((bf16[1,144,512]{2,1,0:T(8,128)(2,1)}, bf16[1,144,512]{2,1,0:T(8,128)(2,1)S(1)}, u32[]{:S(2)}, u32[]{:S(2)}) %collective-permute-start.1) | collective-permute-done | bytes 147488 | tf_op jit(solution)/shard_map/ppermute | solution.py:418
  20.8 0.9 %slice-done = bf16[1,128,512]{2,1,0:T(8,128)(2,1)S(1)} async-done(((bf16[1,144,512]{2,1,0:T(8,128)(2,1)}), bf16[1,128,512]{2,1,0:T(8,128)(2,1)S(1)}, s32[]{:S(2)}) %slice-start) | async-done | bytes 131096 | tf_op jit(solution)/shard_map/slice | solution.py:502
  21.7 0.0 collective-permute-done.5
  21.7 0.0 collective-permute-done.3
  21.7 2.5 %collective-permute-start.17 = (bf16[4,64,512]{2,1,0:T(8,128)(2,1)S(1)}, bf16[4,64,512]{2,1,0:T(8,128)(2,1)S(1)}, u32[]{:S(2)}, u32[]{:S(2)}) collective-permute-start(bf16[4,64,512]{2,1,0:T(8,128)(2,1)S(1)} %pad_maximum_fusion.3), channel_id=1, source_target_pairs={{0,2},{1,3},{2,0},{3,1},{4,6},{5,7},{6,4},{7,5},{8,10},{9,11},{10,... | collective-permute-start | bytes 786440 | tf_op jit(solution)/shard_map/ppermute | solution.py:418
  24.3 1.5 %collective-permute-start.16 = (bf16[4,64,512]{2,1,0:T(8,128)(2,1)S(1)}, bf16[4,64,512]{2,1,0:T(8,128)(2,1)S(1)}, u32[]{:S(2)}, u32[]{:S(2)}) collective-permute-start(bf16[4,64,512]{2,1,0:T(8,128)(2,1)S(1)} %pad_maximum_fusion.3), channel_id=1, source_target_pairs={{0,4},{1,5},{2,6},{3,7},{4,0},{5,1},{6,2},{7,3},{8,12},{9,13},{10,... | collective-permute-start | bytes 786440 | tf_op jit(solution)/shard_map/ppermute | solution.py:418
  25.7 1.3 %collective-permute-start.11 = (bf16[3,128,512]{2,1,0:T(8,128)(2,1)S(1)}, bf16[3,128,512]{2,1,0:T(8,128)(2,1)S(1)}, u32[]{:S(2)}, u32[]{:S(2)}) collective-permute-start(bf16[3,128,512]{2,1,0:T(8,128)(2,1)S(1)} %pad_maximum_fusion.2), channel_id=1, source_target_pairs={{0,16},{1,17},{2,18},{3,19},{4,20},{5,21},{6,22},{7,23},{8,24},{9,... | collective-permute-start | bytes 1179656 | tf_op jit(solution)/shard_map/ppermute | solution.py:418
  27.0 1.5 %collective-permute-start.10 = (bf16[3,128,512]{2,1,0:T(8,128)(2,1)S(1)}, bf16[3,128,512]{2,1,0:T(8,128)(2,1)S(1)}, u32[]{:S(2)}, u32[]{:S(2)}) collective-permute-start(bf16[3,128,512]{2,1,0:T(8,128)(2,1)S(1)} %pad_maximum_fusion.2), channel_id=1, source_target_pairs={{0,8},{1,9},{2,10},{3,11},{4,12},{5,13},{6,14},{7,15},{8,0},{9,1},... | collective-permute-start | bytes 1179656 | tf_op jit(solution)/shard_map/ppermute | solution.py:418
  28.5 0.7 collective-permute-start.8
  29.3 0.9 %copy-done.27 = bf16[1,144,512]{2,1,0:T(8,128)(2,1)S(1)} copy-done((bf16[1,144,512]{2,1,0:T(8,128)(2,1)S(1)}, bf16[1,144,512]{2,1,0:T(8,128)(2,1)}, u32[]{:S(2)}) %copy-start.27) | copy-done | bytes 147480
  30.3 3.6 %prepare.1 = (bf16[4,128,256]{2,1,0:T(8,128)(2,1)}, bf16[4,128,256]{2,1,0:T(8,128)(2,1)}, bf16[128,512]{1,0:T(8,128)(2,1)}, bf16[128,512]{1,0:T(8,128)(2,1)}, bf...) custom-call(bf16[128,512]{1,0:T(8,128)(2,1)} %own_hbm.2, bf16[128,512]{1,0:T(8,128)(2,1)} %cot_ref.1, ...), custom_call_target="tpu_custom_call" | custom-call | flops 400000000 | bytes 4000000 | tf_op jit(solution)/shard_map/prepare/pallas_call | solution.py:490
  33.9 1.3 %key_work.1.work_ref = s32[69]{0:T(128)S(1)} custom-call(s32[4,128]{1,0:T(4,128)S(1)} %bitcast.12), custom_call_target="tpu_custom_call" | custom-call | flops 200000000 | bytes 4000000 | tf_op jit(solution)/shard_map/key_work/pallas_call | solution.py:472
  35.2 1.7 %collective-permute-done.16 = bf16[4,64,512]{2,1,0:T(8,128)(2,1)S(1)} collective-permute-done((bf16[4,64,512]{2,1,0:T(8,128)(2,1)S(1)}, bf16[4,64,512]{2,1,0:T(8,128)(2,1)S(1)}, u32[]{:S(2)}, u32[]{:S(2)}) %collective-permute-start.16) | collective-permute-done | bytes 262176 | tf_op jit(solution)/shard_map/ppermute | solution.py:418
  36.9 0.7 collective-permute-start.18
  37.6 6.3 %collective-permute-done.8.refs_3_ = bf16[3,128,512]{2,1,0:T(8,128)(2,1)S(1)} collective-permute-done((bf16[3,128,512]{2,1,0:T(8,128)(2,1)S(1)}, bf16[3,128,512]{2,1,0:T(8,128)(2,1)S(1)}, u32[]{:S(2)}, u32[]{:S(2)}) %collective-permute-start.8) | collective-permute-done | bytes 393248 | tf_op jit(solution)/shard_map/ppermute | solution.py:418
  43.9 0.0 collective-permute-start.12
  43.9 0.0 collective-permute-done.17
  44.0 0.6 collective-permute-start.9
  44.5 0.0 collective-permute-done.11.refs_2_
  44.6 0.1 collective-permute-start.15
  44.7 0.0 collective-permute-done.10.refs_1_
  44.7 0.5 collective-permute-start.14
  45.2 1.3 %collective-permute-done.9 = bf16[4,16,128]{2,1,0:T(8,128)(2,1)S(1)} collective-permute-done((bf16[4,16,128]{2,1,0:T(8,128)(2,1)S(1)}, bf16[4,16,128]{2,1,0:T(8,128)(2,1)S(1)}, u32[]{:S(2)}, u32[]{:S(2)}) %collective-permute-start.9) | collective-permute-done | bytes 16416 | tf_op jit(solution)/shard_map/ppermute | solution.py:418
  46.4 0.1 collective-permute-start.13
  46.6 1.6 %query_work.1.work_ref = s32[133]{0:T(256)S(1)} custom-call(s32[8,128]{1,0:T(8,128)S(1)} %bitcast.11), custom_call_target="tpu_custom_call" | custom-call | flops 200000000 | bytes 4000000 | tf_op jit(solution)/shard_map/query_work/pallas_call | solution.py:472
  48.1 0.0 copy-start.14
  48.2 0.0 collective-permute-done.18
  48.2 0.0 copy-start.12
  48.2 0.1 pad_maximum_fusion.1.refs_12_
  48.3 0.0 copy-start.2
  48.3 0.0 copy-start.3
  48.3 0.1 pad_maximum_fusion.refs_8_
  48.4 1.8 %collective-permute-start.19 = (bf16[8,64,512]{2,1,0:T(8,128)(2,1)S(1)}, bf16[8,64,512]{2,1,0:T(8,128)(2,1)S(1)}, u32[]{:S(2)}, u32[]{:S(2)}) collective-permute-start(bf16[8,64,512]{2,1,0:T(8,128)(2,1)S(1)} %pad_maximum_fusion.refs_8_), channel_id=1, source_target_pairs={{0,16},{1,17},{2,18},{3,19},{4,20},{5,21},{6,22},{7,23},{8,24},{9,... | collective-permute-start | bytes 1572872 | tf_op jit(solution)/shard_map/ppermute | solution.py:418
  50.2 0.0 collective-permute-done.14.refs_6_
  50.2 1.3 %collective-permute-start.22 = (bf16[8,64,512]{2,1,0:T(8,128)(2,1)S(1)}, bf16[8,64,512]{2,1,0:T(8,128)(2,1)S(1)}, u32[]{:S(2)}, u32[]{:S(2)}) collective-permute-start(bf16[8,64,512]{2,1,0:T(8,128)(2,1)S(1)} %pad_maximum_fusion.1.refs_12_), channel_id=1, source_target_pairs={{0,8},{1,9},{2,10},{3,11},{4,12},{5,13},{6,14},{7,15},{8,0},{9,1},... | collective-permute-start | bytes 1572872 | tf_op jit(solution)/shard_map/ppermute | solution.py:418
  51.5 0.0 collective-permute-done.13.refs_5_
  51.5 0.0 collective-permute-done.12.refs_4_
  51.7 4.6 %forward.1 = (bf16[128,512]{1,0:T(8,128)(2,1)}, f32[32,16,128]{2,1,0:T(8,128)}) custom-call(s32[133]{0:T(256)S(1)} %query_work.1.work_ref, bf16[4,128,256]{2,1,0:T(8,128)(2,1)S(1)} %copy-done.13, bf16[128,512]{1,0:T(8,128)(2,1)S(1)} %copy-done.12, bf16[512,512]{1,0:T(8,128)(2,1)S(1)} %copy-done.2, bf16[512,512]{1,0:T(8,128)(2,1)S(1)} %copy-done.10, ...), custom_call_target="tpu_custom_call" | custom-call | flops 1000000000 | bytes 4000000 | tf_op jit(solution)/shard_map/forward/pallas_call | solution.py:542
  56.3 3.3 %all-to-all-start = ((f32[32,16,128]{2,1,0:T(8,128)}), f32[32,16,128]{2,1,0:T(8,128)S(1)}, u32[]{:S(2)}, u32[]{:S(2)}) async-start(f32[32,16,128]{2,1,0:T(8,128)} %get-tuple-element.34.stats_hbm), calls=%async_computation | async-start | bytes 524288 | tf_op jit(solution)/shard_map/all_to_all | solution.py:555
  59.7 0.3 collective-permute-start.20
  60.0 0.3 collective-permute-start.23
  60.2 5.5 %query_grad.1.part_hbm = f32[128,512]{1,0:T(8,128)} custom-call(s32[133]{0:T(256)} %copy-done.14, bf16[4,128,256]{2,1,0:T(8,128)(2,1)} %get-tuple-element.26.stack_ref.stack_hbm, bf16[4,128,256]{2,1,0:T(8,128)(2,1)} %get-tuple-element.33.cot_stack_hbm, f32[32,16,128]{2,1,0:T(8,128)} %get-tuple-element.34.stats_hbm, ...), custom_call_target="tpu_custom_call" | custom-call | flops 1000000000 | bytes 4000000 | tf_op jit(solution)/shard_map/query_grad/pallas_call | solution.py:557
  65.8 4.2 %all-to-all-done.stats_all_ref = f32[32,16,128]{2,1,0:T(8,128)S(1)} async-done(((f32[32,16,128]{2,1,0:T(8,128)}), f32[32,16,128]{2,1,0:T(8,128)S(1)}, u32[]{:S(2)}, u32[]{:S(2)}) %all-to-all-start) | async-done | bytes 262176 | tf_op jit(solution)/shard_map/all_to_all | solution.py:555
  70.0 0.4 collective-permute-start.21
  70.4 0.1 collective-permute-start.24
  70.6 1.4 %collective-permute-done.21.refs_11_ = bf16[8,64,512]{2,1,0:T(8,128)(2,1)S(1)} collective-permute-done((bf16[8,64,512]{2,1,0:T(8,128)(2,1)S(1)}, bf16[8,64,512]{2,1,0:T(8,128)(2,1)S(1)}, u32[]{:S(2)}, u32[]{:S(2)}) %collective-permute-start.21) | collective-permute-done | bytes 524320 | tf_op jit(solution)/shard_map/ppermute | solution.py:418
  72.0 0.7 collective-permute-done.24.refs_15_
  72.7 0.0 copy-done.24
  72.8 0.8 copy-done.25
  73.6 5.9 %key_grad.1 = bf16[128,512]{1,0:T(8,128)(2,1)} custom-call(s32[69]{0:T(128)} %copy-done.15, bf16[128,512]{1,0:T(8,128)(2,1)} %get-tuple-element.30.key_hbm, bf16[128,512]{1,0:T(8,128)(2,1)} %get-tuple-element.31.value_hbm, bf16[512,512]{1,0:T(8,128)(2,1)} %wq_hbm.3, bf16[512,512]{1,0:T(8,128)(2,1)} %get-tuple-element.32.wkt_hbm, ...), custom_call_target="tpu_custom_call" | custom-call | flops 1000000000 | bytes 4000000 | tf_op jit(solution)/shard_map/key_grad/pallas_call | solution.py:576
  (79 shorter events, 0.4 us)
Async XLA Ops:
  1.3 7.4 %copy-start.11 = (bf16[128,512]{1,0:T(8,128)(2,1)S(1)}, bf16[128,512]{1,0:T(8,128)(2,1)}, u32[]{:S(2)}) copy-start(bf16[128,512]{1,0:T(8,128)(2,1)} %cot_ref.1) | copy-start | bytes 393220
  2.9 9.0 %copy-start.19 = (bf16[1,144,512]{2,1,0:T(8,128)(2,1)S(1)}, bf16[1,144,512]{2,1,0:T(8,128)(2,1)}, u32[]{:S(2)}) copy-start(bf16[1,144,512]{2,1,0:T(8,128)(2,1)} %pack.1) | copy-start | bytes 442372
  2.9 13.2 %collective-permute-start.2 = (bf16[1,144,512]{2,1,0:T(8,128)(2,1)}, bf16[1,144,512]{2,1,0:T(8,128)(2,1)S(1)}, u32[]{:S(2)}, u32[]{:S(2)}) collective-permute-start(bf16[1,144,512]{2,1,0:T(8,128)(2,1)} %pack.1), channel_id=1, source_target_pairs={{0,6},{1,7},{2,4},{3,5},{4,2},{5,3},{6,0},{7,1},{8,14},{9,15},{10,... | collective-permute-start | bytes 442376 | tf_op jit(solution)/shard_map/ppermute | solution.py:418
  8.1 12.7 %collective-permute-start.1 = (bf16[1,144,512]{2,1,0:T(8,128)(2,1)}, bf16[1,144,512]{2,1,0:T(8,128)(2,1)S(1)}, u32[]{:S(2)}, u32[]{:S(2)}) collective-permute-start(bf16[1,144,512]{2,1,0:T(8,128)(2,1)} %pack.1), channel_id=1, source_target_pairs={{0,4},{1,5},{2,6},{3,7},{4,0},{5,1},{6,2},{7,3},{8,12},{9,13},{10,... | collective-permute-start | bytes 442376 | tf_op jit(solution)/shard_map/ppermute | solution.py:418
  8.1 12.7 %collective-permute-start = (bf16[1,144,512]{2,1,0:T(8,128)(2,1)}, bf16[1,144,512]{2,1,0:T(8,128)(2,1)S(1)}, u32[]{:S(2)}, u32[]{:S(2)}) collective-permute-start(bf16[1,144,512]{2,1,0:T(8,128)(2,1)} %pack.1), channel_id=1, source_target_pairs={{0,2},{1,3},{2,0},{3,1},{4,6},{5,7},{6,4},{7,5},{8,10},{9,11},{10,... | collective-permute-start | bytes 442376 | tf_op jit(solution)/shard_map/ppermute | solution.py:418
  8.7 4.3 %collective-permute-start.7 = (bf16[1,64,512]{2,1,0:T(8,128)(2,1)S(1)}, bf16[1,64,512]{2,1,0:T(8,128)(2,1)S(1)}, u32[]{:S(2)}, u32[]{:S(2)}) collective-permute-start(bf16[1,64,512]{2,1,0:T(8,128)(2,1)S(1)} %get-tuple-element.52), channel_id=1, source_target_pairs={{0,16},{1,17},{2,18},{3,19},{4,20},{5,21},{6,22},{7,23},{8,24},{9,... | collective-permute-start | bytes 196616 | tf_op jit(solution)/shard_map/ppermute | solution.py:418
  10.4 5.2 %collective-permute-start.6 = (bf16[1,64,512]{2,1,0:T(8,128)(2,1)S(1)}, bf16[1,64,512]{2,1,0:T(8,128)(2,1)S(1)}, u32[]{:S(2)}, u32[]{:S(2)}) collective-permute-start(bf16[1,64,512]{2,1,0:T(8,128)(2,1)S(1)} %get-tuple-element.53), channel_id=1, source_target_pairs={{0,8},{1,9},{2,10},{3,11},{4,12},{5,13},{6,14},{7,15},{8,0},{9,1},... | collective-permute-start | bytes 196616 | tf_op jit(solution)/shard_map/ppermute | solution.py:418
  13.0 8.7 %collective-permute-start.5 = (bf16[1,144,512]{2,1,0:T(8,128)(2,1)S(1)}, bf16[1,144,512]{2,1,0:T(8,128)(2,1)S(1)}, u32[]{:S(2)}, u32[]{:S(2)}) collective-permute-start(bf16[1,144,512]{2,1,0:T(8,128)(2,1)S(1)} %copy-done.19), channel_id=1, source_target_pairs={{0,24},{1,25},{2,26},{3,27},{4,28},{5,29},{6,30},{7,31},{8,16},{9,... | collective-permute-start | bytes 442376 | tf_op jit(solution)/shard_map/ppermute | solution.py:418
  15.6 6.1 %collective-permute-start.4 = (bf16[1,144,512]{2,1,0:T(8,128)(2,1)S(1)}, bf16[1,144,512]{2,1,0:T(8,128)(2,1)S(1)}, u32[]{:S(2)}, u32[]{:S(2)}) collective-permute-start(bf16[1,144,512]{2,1,0:T(8,128)(2,1)S(1)} %copy-done.19), channel_id=1, source_target_pairs={{0,16},{1,17},{2,18},{3,19},{4,20},{5,21},{6,22},{7,23},{8,24},{9,... | collective-permute-start | bytes 442376 | tf_op jit(solution)/shard_map/ppermute | solution.py:418
  16.1 0.7 copy-start.26
  16.2 5.6 %collective-permute-start.3 = (bf16[1,144,512]{2,1,0:T(8,128)(2,1)S(1)}, bf16[1,144,512]{2,1,0:T(8,128)(2,1)S(1)}, u32[]{:S(2)}, u32[]{:S(2)}) collective-permute-start(bf16[1,144,512]{2,1,0:T(8,128)(2,1)S(1)} %copy-done.19), channel_id=1, source_target_pairs={{0,8},{1,9},{2,10},{3,11},{4,12},{5,13},{6,14},{7,15},{8,0},{9,1},... | collective-permute-start | bytes 442376 | tf_op jit(solution)/shard_map/ppermute | solution.py:418
  20.8 0.9 %slice-start = ((bf16[1,144,512]{2,1,0:T(8,128)(2,1)}), bf16[1,128,512]{2,1,0:T(8,128)(2,1)S(1)}, s32[]{:S(2)}) async-start(bf16[1,144,512]{2,1,0:T(8,128)(2,1)} %copy-done.26), calls=%async_computation.1 | async-start | bytes 262144 | tf_op jit(solution)/shard_map/slice | solution.py:502
  21.7 22.2 %collective-permute-start.17 = (bf16[4,64,512]{2,1,0:T(8,128)(2,1)S(1)}, bf16[4,64,512]{2,1,0:T(8,128)(2,1)S(1)}, u32[]{:S(2)}, u32[]{:S(2)}) collective-permute-start(bf16[4,64,512]{2,1,0:T(8,128)(2,1)S(1)} %pad_maximum_fusion.3), channel_id=1, source_target_pairs={{0,2},{1,3},{2,0},{3,1},{4,6},{5,7},{6,4},{7,5},{8,10},{9,11},{10,... | collective-permute-start | bytes 786440 | tf_op jit(solution)/shard_map/ppermute | solution.py:418
  24.3 12.6 %collective-permute-start.16 = (bf16[4,64,512]{2,1,0:T(8,128)(2,1)S(1)}, bf16[4,64,512]{2,1,0:T(8,128)(2,1)S(1)}, u32[]{:S(2)}, u32[]{:S(2)}) collective-permute-start(bf16[4,64,512]{2,1,0:T(8,128)(2,1)S(1)} %pad_maximum_fusion.3), channel_id=1, source_target_pairs={{0,4},{1,5},{2,6},{3,7},{4,0},{5,1},{6,2},{7,3},{8,12},{9,13},{10,... | collective-permute-start | bytes 786440 | tf_op jit(solution)/shard_map/ppermute | solution.py:418
  25.7 18.8 %collective-permute-start.11 = (bf16[3,128,512]{2,1,0:T(8,128)(2,1)S(1)}, bf16[3,128,512]{2,1,0:T(8,128)(2,1)S(1)}, u32[]{:S(2)}, u32[]{:S(2)}) collective-permute-start(bf16[3,128,512]{2,1,0:T(8,128)(2,1)S(1)} %pad_maximum_fusion.2), channel_id=1, source_target_pairs={{0,16},{1,17},{2,18},{3,19},{4,20},{5,21},{6,22},{7,23},{8,24},{9,... | collective-permute-start | bytes 1179656 | tf_op jit(solution)/shard_map/ppermute | solution.py:418
  27.0 17.6 %collective-permute-start.10 = (bf16[3,128,512]{2,1,0:T(8,128)(2,1)S(1)}, bf16[3,128,512]{2,1,0:T(8,128)(2,1)S(1)}, u32[]{:S(2)}, u32[]{:S(2)}) collective-permute-start(bf16[3,128,512]{2,1,0:T(8,128)(2,1)S(1)} %pad_maximum_fusion.2), channel_id=1, source_target_pairs={{0,8},{1,9},{2,10},{3,11},{4,12},{5,13},{6,14},{7,15},{8,0},{9,1},... | collective-permute-start | bytes 1179656 | tf_op jit(solution)/shard_map/ppermute | solution.py:418
  28.5 15.4 %collective-permute-start.8 = (bf16[3,128,512]{2,1,0:T(8,128)(2,1)S(1)}, bf16[3,128,512]{2,1,0:T(8,128)(2,1)S(1)}, u32[]{:S(2)}, u32[]{:S(2)}) collective-permute-start(bf16[3,128,512]{2,1,0:T(8,128)(2,1)S(1)} %pad_maximum_fusion.2), channel_id=1, source_target_pairs={{0,24},{1,25},{2,26},{3,27},{4,28},{5,29},{6,30},{7,31},{8,16},{9,... | collective-permute-start | bytes 1179656 | tf_op jit(solution)/shard_map/ppermute | solution.py:418
  29.2 0.9 %copy-start.27 = (bf16[1,144,512]{2,1,0:T(8,128)(2,1)S(1)}, bf16[1,144,512]{2,1,0:T(8,128)(2,1)}, u32[]{:S(2)}) copy-start(bf16[1,144,512]{2,1,0:T(8,128)(2,1)} %copy-done.26) | copy-start | bytes 442372
  30.2 21.4 %copy-start = (bf16[7,128,512]{2,1,0:T(8,128)(2,1)}, bf16[7,128,512]{2,1,0:T(8,128)(2,1)S(1)}, u32[]{:S(2)}) copy-start(bf16[7,128,512]{2,1,0:T(8,128)(2,1)S(1)} %constant_dynamic-update-slice_fusion.refs_0_) | copy-start | bytes 2752516
  35.2 1.7 %copy-start.15 = (s32[69]{0:T(128)}, s32[69]{0:T(128)S(1)}, u32[]{:S(2)}) copy-start(s32[69]{0:T(128)S(1)} %key_work.1.work_ref) | copy-start | bytes 832
  36.9 11.3 %collective-permute-start.18 = (bf16[4,64,512]{2,1,0:T(8,128)(2,1)S(1)}, bf16[4,64,512]{2,1,0:T(8,128)(2,1)S(1)}, u32[]{:S(2)}, u32[]{:S(2)}) collective-permute-start(bf16[4,64,512]{2,1,0:T(8,128)(2,1)S(1)} %collective-permute-done.16), channel_id=1, source_target_pairs={{0,2},{1,3},{2,0},{3,1},{4,6},{5,7},{6,4},{7,5},{8,10},{9,11},{10,... | collective-permute-start | bytes 786440 | tf_op jit(solution)/shard_map/ppermute | solution.py:418
  43.9 7.7 %copy-start.6 = (bf16[3,128,512]{2,1,0:T(8,128)(2,1)}, bf16[3,128,512]{2,1,0:T(8,128)(2,1)S(1)}, u32[]{:S(2)}) copy-start(bf16[3,128,512]{2,1,0:T(8,128)(2,1)S(1)} %collective-permute-done.8.refs_3_) | copy-start | bytes 1179652
  43.9 7.6 %collective-permute-start.12 = (bf16[7,128,512]{2,1,0:T(8,128)(2,1)S(1)}, bf16[7,128,512]{2,1,0:T(8,128)(2,1)S(1)}, u32[]{:S(2)}, u32[]{:S(2)}) collective-permute-start(bf16[7,128,512]{2,1,0:T(8,128)(2,1)S(1)} %constant_dynamic-update-slice_fusion.refs_0_), channel_id=1, source_target_pairs={{0,1},{1,0},{2,3},{3,2},{4,5},{5,4},{6,7},{7,6},{8,9},{9,8},{10,11... | collective-permute-start | bytes 2752520 | tf_op jit(solution)/shard_map/ppermute | solution.py:418
  44.0 2.5 %collective-permute-start.9 = (bf16[4,16,128]{2,1,0:T(8,128)(2,1)S(1)}, bf16[4,16,128]{2,1,0:T(8,128)(2,1)S(1)}, u32[]{:S(2)}, u32[]{:S(2)}) collective-permute-start(bf16[4,16,128]{2,1,0:T(8,128)(2,1)S(1)} %pad_maximum_fusion.4), channel_id=1, source_target_pairs={{0,1},{1,0},{2,3},{3,2},{4,5},{5,4},{6,7},{7,6},{8,9},{9,8},{10,11... | collective-permute-start | bytes 49160 | tf_op jit(solution)/shard_map/ppermute | solution.py:418
  44.6 7.0 %copy-start.4 = (bf16[3,128,512]{2,1,0:T(8,128)(2,1)}, bf16[3,128,512]{2,1,0:T(8,128)(2,1)S(1)}, u32[]{:S(2)}) copy-start(bf16[3,128,512]{2,1,0:T(8,128)(2,1)S(1)} %collective-permute-done.11.refs_2_) | copy-start | bytes 1179652
  44.6 7.0 %collective-permute-start.15 = (bf16[3,128,512]{2,1,0:T(8,128)(2,1)S(1)}, bf16[3,128,512]{2,1,0:T(8,128)(2,1)S(1)}, u32[]{:S(2)}, u32[]{:S(2)}) collective-permute-start(bf16[3,128,512]{2,1,0:T(8,128)(2,1)S(1)} %collective-permute-done.8.refs_3_), channel_id=1, source_target_pairs={{0,1},{1,0},{2,3},{3,2},{4,5},{5,4},{6,7},{7,6},{8,9},{9,8},{10,11... | collective-permute-start | bytes 1179656 | tf_op jit(solution)/shard_map/ppermute | solution.py:418
  44.7 6.9 %copy-start.5 = (bf16[3,128,512]{2,1,0:T(8,128)(2,1)}, bf16[3,128,512]{2,1,0:T(8,128)(2,1)S(1)}, u32[]{:S(2)}) copy-start(bf16[3,128,512]{2,1,0:T(8,128)(2,1)S(1)} %collective-permute-done.10.refs_1_) | copy-start | bytes 1179652
  44.7 5.5 %collective-permute-start.14 = (bf16[3,128,512]{2,1,0:T(8,128)(2,1)S(1)}, bf16[3,128,512]{2,1,0:T(8,128)(2,1)S(1)}, u32[]{:S(2)}, u32[]{:S(2)}) collective-permute-start(bf16[3,128,512]{2,1,0:T(8,128)(2,1)S(1)} %collective-permute-done.11.refs_2_), channel_id=1, source_target_pairs={{0,1},{1,0},{2,3},{3,2},{4,5},{5,4},{6,7},{7,6},{8,9},{9,8},{10,11... | collective-permute-start | bytes 1179656 | tf_op jit(solution)/shard_map/ppermute | solution.py:418
  46.4 5.1 %collective-permute-start.13 = (bf16[3,128,512]{2,1,0:T(8,128)(2,1)S(1)}, bf16[3,128,512]{2,1,0:T(8,128)(2,1)S(1)}, u32[]{:S(2)}, u32[]{:S(2)}) collective-permute-start(bf16[3,128,512]{2,1,0:T(8,128)(2,1)S(1)} %collective-permute-done.10.refs_1_), channel_id=1, source_target_pairs={{0,1},{1,0},{2,3},{3,2},{4,5},{5,4},{6,7},{7,6},{8,9},{9,8},{10,11... | collective-permute-start | bytes 1179656 | tf_op jit(solution)/shard_map/ppermute | solution.py:418
  48.1 3.5 %copy-start.14 = (s32[133]{0:T(256)}, s32[133]{0:T(256)S(1)}, u32[]{:S(2)}) copy-start(s32[133]{0:T(256)S(1)} %query_work.1.work_ref) | copy-start | bytes 1600
  48.2 3.4 %copy-start.10 = (bf16[512,512]{1,0:T(8,128)(2,1)S(1)}, bf16[512,512]{1,0:T(8,128)(2,1)}, u32[]{:S(2)}) copy-start(bf16[512,512]{1,0:T(8,128)(2,1)} %get-tuple-element.27.wvt_ref.wvt_hbm) | copy-start | bytes 1572868
  48.2 3.4 %copy-start.12 = (bf16[128,512]{1,0:T(8,128)(2,1)S(1)}, bf16[128,512]{1,0:T(8,128)(2,1)}, u32[]{:S(2)}) copy-start(bf16[128,512]{1,0:T(8,128)(2,1)} %cot_ref.1) | copy-start | bytes 393220
  48.2 3.4 %copy-start.13 = (bf16[4,128,256]{2,1,0:T(8,128)(2,1)S(1)}, bf16[4,128,256]{2,1,0:T(8,128)(2,1)}, u32[]{:S(2)}) copy-start(bf16[4,128,256]{2,1,0:T(8,128)(2,1)} %get-tuple-element.26.stack_ref.stack_hbm) | copy-start | bytes 786436
  48.3 11.7 %copy-start.16 = (bf16[8,64,512]{2,1,0:T(8,128)(2,1)}, bf16[8,64,512]{2,1,0:T(8,128)(2,1)S(1)}, u32[]{:S(2)}) copy-start(bf16[8,64,512]{2,1,0:T(8,128)(2,1)S(1)} %pad_maximum_fusion.1.refs_12_) | copy-start | bytes 1572868
  48.3 3.3 %copy-start.2 = (bf16[512,512]{1,0:T(8,128)(2,1)S(1)}, bf16[512,512]{1,0:T(8,128)(2,1)}, u32[]{:S(2)}) copy-start(bf16[512,512]{1,0:T(8,128)(2,1)} %wk_hbm.3) | copy-start | bytes 1572868
  48.3 3.3 %copy-start.3 = (s32[240,128,4]{1,2,0:T(4,128)S(1)}, s32[240,128,4]{1,2,0:T(4,128)}, u32[]{:S(2)}) copy-start(s32[240,128,4]{1,2,0:T(4,128)} %param.15) | copy-start | bytes 1474564
  48.4 11.2 %copy-start.17 = (bf16[8,64,512]{2,1,0:T(8,128)(2,1)}, bf16[8,64,512]{2,1,0:T(8,128)(2,1)S(1)}, u32[]{:S(2)}) copy-start(bf16[8,64,512]{2,1,0:T(8,128)(2,1)S(1)} %pad_maximum_fusion.refs_8_) | copy-start | bytes 1572868
  48.4 17.4 %collective-permute-start.19 = (bf16[8,64,512]{2,1,0:T(8,128)(2,1)S(1)}, bf16[8,64,512]{2,1,0:T(8,128)(2,1)S(1)}, u32[]{:S(2)}, u32[]{:S(2)}) collective-permute-start(bf16[8,64,512]{2,1,0:T(8,128)(2,1)S(1)} %pad_maximum_fusion.refs_8_), channel_id=1, source_target_pairs={{0,16},{1,17},{2,18},{3,19},{4,20},{5,21},{6,22},{7,23},{8,24},{9,... | collective-permute-start | bytes 1572872 | tf_op jit(solution)/shard_map/ppermute | solution.py:418
  50.2 6.1 %copy-start.8 = (bf16[3,128,512]{2,1,0:T(8,128)(2,1)}, bf16[3,128,512]{2,1,0:T(8,128)(2,1)S(1)}, u32[]{:S(2)}) copy-start(bf16[3,128,512]{2,1,0:T(8,128)(2,1)S(1)} %collective-permute-done.14.refs_6_) | copy-start | bytes 1179652
  50.2 20.2 %collective-permute-start.22 = (bf16[8,64,512]{2,1,0:T(8,128)(2,1)S(1)}, bf16[8,64,512]{2,1,0:T(8,128)(2,1)S(1)}, u32[]{:S(2)}, u32[]{:S(2)}) collective-permute-start(bf16[8,64,512]{2,1,0:T(8,128)(2,1)S(1)} %pad_maximum_fusion.1.refs_12_), channel_id=1, source_target_pairs={{0,8},{1,9},{2,10},{3,11},{4,12},{5,13},{6,14},{7,15},{8,0},{9,1},... | collective-permute-start | bytes 1572872 | tf_op jit(solution)/shard_map/ppermute | solution.py:418
  51.5 4.8 %copy-start.9 = (bf16[3,128,512]{2,1,0:T(8,128)(2,1)}, bf16[3,128,512]{2,1,0:T(8,128)(2,1)S(1)}, u32[]{:S(2)}) copy-start(bf16[3,128,512]{2,1,0:T(8,128)(2,1)S(1)} %collective-permute-done.13.refs_5_) | copy-start | bytes 1179652
  51.5 4.8 %copy-start.7 = (bf16[3,128,512]{2,1,0:T(8,128)(2,1)}, bf16[3,128,512]{2,1,0:T(8,128)(2,1)S(1)}, u32[]{:S(2)}) copy-start(bf16[3,128,512]{2,1,0:T(8,128)(2,1)S(1)} %collective-permute-done.15.refs_7_) | copy-start | bytes 1179652
  51.6 4.7 %copy-start.1 = (bf16[7,128,512]{2,1,0:T(8,128)(2,1)}, bf16[7,128,512]{2,1,0:T(8,128)(2,1)S(1)}, u32[]{:S(2)}) copy-start(bf16[7,128,512]{2,1,0:T(8,128)(2,1)S(1)} %collective-permute-done.12.refs_4_) | copy-start | bytes 2752516
  56.3 13.7 %all-to-all-start = ((f32[32,16,128]{2,1,0:T(8,128)}), f32[32,16,128]{2,1,0:T(8,128)S(1)}, u32[]{:S(2)}, u32[]{:S(2)}) async-start(f32[32,16,128]{2,1,0:T(8,128)} %get-tuple-element.34.stats_hbm), calls=%async_computation | async-start | bytes 524288 | tf_op jit(solution)/shard_map/all_to_all | solution.py:555
  59.7 10.9 %collective-permute-start.20 = (bf16[8,64,512]{2,1,0:T(8,128)(2,1)S(1)}, bf16[8,64,512]{2,1,0:T(8,128)(2,1)S(1)}, u32[]{:S(2)}, u32[]{:S(2)}) collective-permute-start(bf16[8,64,512]{2,1,0:T(8,128)(2,1)S(1)} %pad_maximum_fusion.refs_8_), channel_id=1, source_target_pairs={{0,1},{1,0},{2,3},{3,2},{4,5},{5,4},{6,7},{7,6},{8,9},{9,8},{10,11... | collective-permute-start | bytes 1572872 | tf_op jit(solution)/shard_map/ppermute | solution.py:418
  60.0 10.6 %collective-permute-start.23 = (bf16[8,64,512]{2,1,0:T(8,128)(2,1)S(1)}, bf16[8,64,512]{2,1,0:T(8,128)(2,1)S(1)}, u32[]{:S(2)}, u32[]{:S(2)}) collective-permute-start(bf16[8,64,512]{2,1,0:T(8,128)(2,1)S(1)} %pad_maximum_fusion.1.refs_12_), channel_id=1, source_target_pairs={{0,1},{1,0},{2,3},{3,2},{4,5},{5,4},{6,7},{7,6},{8,9},{9,8},{10,11... | collective-permute-start | bytes 1572872 | tf_op jit(solution)/shard_map/ppermute | solution.py:418
  65.8 6.9 %copy-start.20 = (bf16[8,64,512]{2,1,0:T(8,128)(2,1)}, bf16[8,64,512]{2,1,0:T(8,128)(2,1)S(1)}, u32[]{:S(2)}) copy-start(bf16[8,64,512]{2,1,0:T(8,128)(2,1)S(1)} %collective-permute-done.19.refs_9_) | copy-start | bytes 1572868
  70.0 2.7 %copy-start.18 = (f32[32,16,128]{2,1,0:T(8,128)}, f32[32,16,128]{2,1,0:T(8,128)S(1)}, u32[]{:S(2)}) copy-start(f32[32,16,128]{2,1,0:T(8,128)S(1)} %all-to-all-done.stats_all_ref) | copy-start | bytes 786436
  70.0 1.9 %collective-permute-start.21 = (bf16[8,64,512]{2,1,0:T(8,128)(2,1)S(1)}, bf16[8,64,512]{2,1,0:T(8,128)(2,1)S(1)}, u32[]{:S(2)}, u32[]{:S(2)}) collective-permute-start(bf16[8,64,512]{2,1,0:T(8,128)(2,1)S(1)} %collective-permute-done.19.refs_9_), channel_id=1, source_target_pairs={{0,1},{1,0},{2,3},{3,2},{4,5},{5,4},{6,7},{7,6},{8,9},{9,8},{10,11... | collective-permute-start | bytes 1572872 | tf_op jit(solution)/shard_map/ppermute | solution.py:418
  70.4 2.3 %copy-start.21 = (bf16[8,64,512]{2,1,0:T(8,128)(2,1)}, bf16[8,64,512]{2,1,0:T(8,128)(2,1)S(1)}, u32[]{:S(2)}) copy-start(bf16[8,64,512]{2,1,0:T(8,128)(2,1)S(1)} %collective-permute-done.22.refs_13_) | copy-start | bytes 1572868
  70.4 2.3 %collective-permute-start.24 = (bf16[8,64,512]{2,1,0:T(8,128)(2,1)S(1)}, bf16[8,64,512]{2,1,0:T(8,128)(2,1)S(1)}, u32[]{:S(2)}, u32[]{:S(2)}) collective-permute-start(bf16[8,64,512]{2,1,0:T(8,128)(2,1)S(1)} %collective-permute-done.22.refs_13_), channel_id=1, source_target_pairs={{0,1},{1,0},{2,3},{3,2},{4,5},{5,4},{6,7},{7,6},{8,9},{9,8},{10,11... | collective-permute-start | bytes 1572872 | tf_op jit(solution)/shard_map/ppermute | solution.py:418
  70.6 2.2 %copy-start.22 = (bf16[8,64,512]{2,1,0:T(8,128)(2,1)}, bf16[8,64,512]{2,1,0:T(8,128)(2,1)S(1)}, u32[]{:S(2)}) copy-start(bf16[8,64,512]{2,1,0:T(8,128)(2,1)S(1)} %collective-permute-done.20.refs_10_) | copy-start | bytes 1572868
  70.6 2.2 %copy-start.23 = (bf16[8,64,512]{2,1,0:T(8,128)(2,1)}, bf16[8,64,512]{2,1,0:T(8,128)(2,1)S(1)}, u32[]{:S(2)}) copy-start(bf16[8,64,512]{2,1,0:T(8,128)(2,1)S(1)} %collective-permute-done.23.refs_14_) | copy-start | bytes 1572868
  72.0 0.8 %copy-start.24 = (bf16[8,64,512]{2,1,0:T(8,128)(2,1)}, bf16[8,64,512]{2,1,0:T(8,128)(2,1)S(1)}, u32[]{:S(2)}) copy-start(bf16[8,64,512]{2,1,0:T(8,128)(2,1)S(1)} %collective-permute-done.21.refs_11_) | copy-start | bytes 1572868
  72.8 0.8 %copy-start.25 = (bf16[8,64,512]{2,1,0:T(8,128)(2,1)}, bf16[8,64,512]{2,1,0:T(8,128)(2,1)S(1)}, u32[]{:S(2)}) copy-start(bf16[8,64,512]{2,1,0:T(8,128)(2,1)S(1)} %collective-permute-done.24.refs_15_) | copy-start | bytes 1572868

commit v3 on v0

--- a/solution.py
+++ b/solution.py
@@ -496,13 +496,13 @@
     )(after(features, columns), cotangent, w_query, w_key, w_value)
     query_stack, cot_stack, keys, values, w_query_t, w_key_t, w_value_t = prepared
 
-    line = jnp.concatenate([entry[:, :block] for entry in lined[1:]], 0)
+    line = jnp.concatenate(lined[1:], 0)[:, :block]
     line = after(line, columns, cot_other)
     there = to_readers(line)
     near = jnp.concatenate([entry[:, :block] for entry in columns] + [line], 0)
 
     pairs = [part for k in range(2) for part in (cot_parts[k], cot_other[k])]
-    pieces = [after(jnp.concatenate(pairs, 0), near)]
+    pieces = [after(jnp.concatenate(pairs, 0), line)]
     done_first = (key_work, prepared)
     mask = blks // 2
     while mask > 1:

time: 79.4 us -> 76.7 us (0.966)
  waiting for transfers between devices: 24.4 us -> 19.8 us
  Pallas kernels: 21.2 us -> 23.8 us
  local copies, waits for them, and re-layouts: 2.59 us -> 1.59 us
    ppermute x25, waiting for transfers between devices: 19.2 us -> 15.6 us  [swap(): return lax.ppermute(block, axes, [(i, i ^ mask) for i in range(count)])]
    pallas_call x1, Pallas kernels: 2.9 us -> 4.25 us  [local(): pl.pallas_call(functools.partial(forward_kernel, sizes), out_shape=(own,...]
    all_to_all x1, waiting for transfers between devices: 5.26 us -> 4.24 us  [local(): stats_all = lax.all_to_all(stats, axes, 0, 0, tiled=True)]
    pallas_call x1, Pallas kernels: 4.52 us -> 5.54 us  [local(): pl.pallas_call(functools.partial(query_grad_kernel, sizes), out_shape=sha...]
    slice x4 -> x0, local copies, waits for them, and re-layouts: 0.89 us -> none  [local(): line = jnp.concatenate([entry[:, :block] for entry in lined[1:]], 0)]
  transfers between devices with their start and end apart: 26 -> 26, of which waited for: 8 -> 11; matrix products, arithmetic and copies ran while one was open for 1% -> 1% of each run, Pallas kernels for 17% -> 21%
where the time goes in v3:
time: 76.7 us; the launch traced here: 76.9 us
  starting transfers between devices  29.6 us (39%)
  Pallas kernels  23.8 us (31%)
  waiting for transfers between devices  19.8 us (26%)
  between operations  1.81 us (2%)
  local copies, waits for them, and re-layouts  1.59 us (2%)
    ppermute x25, starting transfers between devices, swap(): return lax.ppermute(block, axes, [(i, i ^ mask) for i in range(count)])  26.5 us
    ppermute x25, waiting for transfers between devices, swap(): return lax.ppermute(block, axes, [(i, i ^ mask) for i in range(count)])  15.6 us
    pallas_call x1, Pallas kernels, local(): pl.pallas_call(functools.partial(key_grad_kernel, sizes, bits), out_shape...  5.8 us
    pallas_call x1, Pallas kernels, local(): pl.pallas_call(functools.partial(query_grad_kernel, sizes), out_shape=sha...  5.54 us
    pallas_call x1, Pallas kernels, local(): pl.pallas_call(functools.partial(forward_kernel, sizes), out_shape=(own,...  4.25 us
    all_to_all x1, waiting for transfers between devices, local(): stats_all = lax.all_to_all(stats, axes, 0, 0, tiled=True)  4.24 us
    pallas_call x1, Pallas kernels, local(): pl.pallas_call(prepare_kernel, out_shape=(stacks, stacks, own, own, squar...  3.54 us
    all_to_all x1, starting transfers between devices, local(): stats_all = lax.all_to_all(stats, axes, 0, 0, tiled=True)  3.16 us
  transfers between devices with their start and end apart: 26, of which 11 were waited for; matrix products, arithmetic and copies ran while one was open for 1% of the time, Pallas kernels for 21%

profile of v3, /device:TPU:0, one launch (start us, length us, event | category | flops | bytes accessed | tf_op | source)
XLA Modules:
  0.0 76.9 jit_solution(8819743015228037040)
XLA Ops:
  1.3 0.0 copy-start.11
  1.3 1.6 %pack.1 = bf16[1,144,512]{2,1,0:T(8,128)(2,1)} custom-call(bf16[128,512]{1,0:T(8,128)(2,1)} %own_hbm.2, s32[1,3,1,8]{3,2,1,0:T(1,128)} %bitcast.13, s32[1,1]{1,0:T(1,128)S(6)} %copy.14.count_hbm), custom_call_target="tpu_custom_call" | custom-call | tf_op jit(solution)/shard_map/pack/pallas_call | solution.py:441
  2.9 5.1 %collective-permute-start.2 = (bf16[1,144,512]{2,1,0:T(8,128)(2,1)}, bf16[1,144,512]{2,1,0:T(8,128)(2,1)S(1)}, u32[]{:S(2)}, u32[]{:S(2)}) collective-permute-start(bf16[1,144,512]{2,1,0:T(8,128)(2,1)} %pack.1), channel_id=1, source_target_pairs={{0,6},{1,7},{2,4},{3,5},{4,2},{5,3},{6,0},{7,1},{8,14},{9,15},{10,... | collective-permute-start | bytes 442376 | tf_op jit(solution)/shard_map/ppermute | solution.py:415
  8.1 0.0 collective-permute-start.1
  8.1 0.6 collective-permute-start
  8.7 1.7 %collective-permute-start.3 = (bf16[1,64,512]{2,1,0:T(8,128)(2,1)S(1)}, bf16[1,64,512]{2,1,0:T(8,128)(2,1)S(1)}, u32[]{:S(2)}, u32[]{:S(2)}) collective-permute-start(bf16[1,64,512]{2,1,0:T(8,128)(2,1)S(1)} %get-tuple-element.50), channel_id=1, source_target_pairs={{0,8},{1,9},{2,10},{3,11},{4,12},{5,13},{6,14},{7,15},{8,0},{9,1},... | collective-permute-start | bytes 196616 | tf_op jit(solution)/shard_map/ppermute | solution.py:415
  10.4 1.5 %collective-permute-start.4 = (bf16[1,64,512]{2,1,0:T(8,128)(2,1)S(1)}, bf16[1,64,512]{2,1,0:T(8,128)(2,1)S(1)}, u32[]{:S(2)}, u32[]{:S(2)}) collective-permute-start(bf16[1,64,512]{2,1,0:T(8,128)(2,1)S(1)} %get-tuple-element.51), channel_id=1, source_target_pairs={{0,16},{1,17},{2,18},{3,19},{4,20},{5,21},{6,22},{7,23},{8,24},{9,... | collective-permute-start | bytes 196616 | tf_op jit(solution)/shard_map/ppermute | solution.py:415
  12.0 1.1 %collective-permute-done.3 = bf16[1,64,512]{2,1,0:T(8,128)(2,1)S(1)} collective-permute-done((bf16[1,64,512]{2,1,0:T(8,128)(2,1)S(1)}, bf16[1,64,512]{2,1,0:T(8,128)(2,1)S(1)}, u32[]{:S(2)}, u32[]{:S(2)}) %collective-permute-start.3) | collective-permute-done | bytes 65568 | tf_op jit(solution)/shard_map/ppermute | solution.py:415
  13.0 2.6 %collective-permute-start.7 = (bf16[1,144,512]{2,1,0:T(8,128)(2,1)S(1)}, bf16[1,144,512]{2,1,0:T(8,128)(2,1)S(1)}, u32[]{:S(2)}, u32[]{:S(2)}) collective-permute-start(bf16[1,144,512]{2,1,0:T(8,128)(2,1)S(1)} %copy-done.19), channel_id=1, source_target_pairs={{0,24},{1,25},{2,26},{3,27},{4,28},{5,29},{6,30},{7,31},{8,16},{9,... | collective-permute-start | bytes 442376 | tf_op jit(solution)/shard_map/ppermute | solution.py:415
  15.6 0.0 collective-permute-done.4
  15.6 0.6 collective-permute-start.6
  16.2 0.0 collective-permute-done.2
  16.2 0.5 collective-permute-start.5
  16.8 4.0 %collective-permute-done.1 = bf16[1,144,512]{2,1,0:T(8,128)(2,1)S(1)} collective-permute-done((bf16[1,144,512]{2,1,0:T(8,128)(2,1)}, bf16[1,144,512]{2,1,0:T(8,128)(2,1)S(1)}, u32[]{:S(2)}, u32[]{:S(2)}) %collective-permute-start.1) | collective-permute-done | bytes 147488 | tf_op jit(solution)/shard_map/ppermute | solution.py:415
  20.7 0.0 collective-permute-done
  20.8 0.0 collective-permute-done.7
  20.8 0.7 collective-permute-done.6
  21.5 0.0 collective-permute-done.5
  21.5 4.0 %collective-permute-start.17 = (bf16[4,64,512]{2,1,0:T(8,128)(2,1)S(1)}, bf16[4,64,512]{2,1,0:T(8,128)(2,1)S(1)}, u32[]{:S(2)}, u32[]{:S(2)}) collective-permute-start(bf16[4,64,512]{2,1,0:T(8,128)(2,1)S(1)} %pad_maximum_fusion.4), channel_id=1, source_target_pairs={{0,4},{1,5},{2,6},{3,7},{4,0},{5,1},{6,2},{7,3},{8,12},{9,13},{10,... | collective-permute-start | bytes 786440 | tf_op jit(solution)/shard_map/ppermute | solution.py:415
  25.5 0.2 collective-permute-start.8
  25.7 2.2 %collective-permute-start.12 = (bf16[3,128,512]{2,1,0:T(8,128)(2,1)S(1)}, bf16[3,128,512]{2,1,0:T(8,128)(2,1)S(1)}, u32[]{:S(2)}, u32[]{:S(2)}) collective-permute-start(bf16[3,128,512]{2,1,0:T(8,128)(2,1)S(1)} %pad_maximum_fusion.2), channel_id=1, source_target_pairs={{0,24},{1,25},{2,26},{3,27},{4,28},{5,29},{6,30},{7,31},{8,16},{9,... | collective-permute-start | bytes 1179656 | tf_op jit(solution)/shard_map/ppermute | solution.py:415
  27.9 0.5 collective-permute-start.11
  28.4 0.8 collective-permute-start.10
  29.4 3.5 %prepare.1 = (bf16[4,128,256]{2,1,0:T(8,128)(2,1)}, bf16[4,128,256]{2,1,0:T(8,128)(2,1)}, bf16[128,512]{1,0:T(8,128)(2,1)}, bf16[128,512]{1,0:T(8,128)(2,1)}, bf...) custom-call(bf16[128,512]{1,0:T(8,128)(2,1)} %own_hbm.2, bf16[128,512]{1,0:T(8,128)(2,1)} %cot_ref.1, ...), custom_call_target="tpu_custom_call" | custom-call | flops 400000000 | bytes 4000000 | tf_op jit(solution)/shard_map/prepare/pallas_call | solution.py:487
  32.9 1.4 %key_work.1.work_ref = s32[69]{0:T(128)S(1)} custom-call(s32[4,128]{1,0:T(4,128)S(1)} %bitcast.12), custom_call_target="tpu_custom_call" | custom-call | flops 200000000 | bytes 4000000 | tf_op jit(solution)/shard_map/key_work/pallas_call | solution.py:469
  34.4 0.5 copy-done.15
  34.9 0.3 collective-permute-done.8
  35.2 0.0 collective-permute-done.17
  35.2 0.5 collective-permute-start.9
  35.7 2.0 %collective-permute-done.9 = bf16[4,16,128]{2,1,0:T(8,128)(2,1)S(1)} collective-permute-done((bf16[4,16,128]{2,1,0:T(8,128)(2,1)S(1)}, bf16[4,16,128]{2,1,0:T(8,128)(2,1)S(1)}, u32[]{:S(2)}, u32[]{:S(2)}) %collective-permute-start.9) | collective-permute-done | bytes 16416 | tf_op jit(solution)/shard_map/ppermute | solution.py:415
  37.7 1.4 %collective-permute-start.18 = (bf16[4,64,512]{2,1,0:T(8,128)(2,1)S(1)}, bf16[4,64,512]{2,1,0:T(8,128)(2,1)S(1)}, u32[]{:S(2)}, u32[]{:S(2)}) collective-permute-start(bf16[4,64,512]{2,1,0:T(8,128)(2,1)S(1)} %collective-permute-done.17), channel_id=1, source_target_pairs={{0,2},{1,3},{2,0},{3,1},{4,6},{5,7},{6,4},{7,5},{8,10},{9,11},{10,... | collective-permute-start | bytes 786440 | tf_op jit(solution)/shard_map/ppermute | solution.py:415
  39.2 1.6 %query_work.1.work_ref = s32[133]{0:T(256)S(1)} custom-call(s32[8,128]{1,0:T(8,128)S(1)} %bitcast.11), custom_call_target="tpu_custom_call" | custom-call | flops 200000000 | bytes 4000000 | tf_op jit(solution)/shard_map/query_work/pallas_call | solution.py:469
  40.8 0.0 copy-start.14
  40.8 0.1 collective-permute-start.16
  40.9 1.8 %collective-permute-done.11.refs_2_ = bf16[3,128,512]{2,1,0:T(8,128)(2,1)S(1)} collective-permute-done((bf16[3,128,512]{2,1,0:T(8,128)(2,1)S(1)}, bf16[3,128,512]{2,1,0:T(8,128)(2,1)S(1)}, u32[]{:S(2)}, u32[]{:S(2)}) %collective-permute-start.11) | collective-permute-done | bytes 393248 | tf_op jit(solution)/shard_map/ppermute | solution.py:415
  42.7 0.0 collective-permute-start.15
  42.7 0.7 collective-permute-done.10.refs_1_
  43.4 0.0 collective-permute-start.14
  43.4 2.7 %collective-permute-done.18 = bf16[4,64,512]{2,1,0:T(8,128)(2,1)S(1)} collective-permute-done((bf16[4,64,512]{2,1,0:T(8,128)(2,1)S(1)}, bf16[4,64,512]{2,1,0:T(8,128)(2,1)S(1)}, u32[]{:S(2)}, u32[]{:S(2)}) %collective-permute-start.18) | collective-permute-done | bytes 262176 | tf_op jit(solution)/shard_map/ppermute | solution.py:415
  46.1 0.0 copy-start.12
  46.1 0.1 pad_maximum_fusion.1.refs_12_
  46.2 0.0 copy-start.2
  46.2 0.0 copy-start.3
  46.2 0.1 pad_maximum_fusion.refs_8_
  46.3 1.5 %collective-permute-start.19 = (bf16[8,64,512]{2,1,0:T(8,128)(2,1)S(1)}, bf16[8,64,512]{2,1,0:T(8,128)(2,1)}, u32[]{:S(2)}, u32[]{:S(2)}) collective-permute-start(bf16[8,64,512]{2,1,0:T(8,128)(2,1)S(1)} %pad_maximum_fusion.refs_8_), channel_id=1, source_target_pairs={{0,16},{1,17},{2,18},{3,19},{4,20},{5,21},{6,22},{7,23},{8,24},{9,... | collective-permute-start | bytes 1572872 | tf_op jit(solution)/shard_map/ppermute | solution.py:415
  47.9 1.5 %collective-permute-start.22 = (bf16[8,64,512]{2,1,0:T(8,128)(2,1)S(1)}, bf16[8,64,512]{2,1,0:T(8,128)(2,1)}, u32[]{:S(2)}, u32[]{:S(2)}) collective-permute-start(bf16[8,64,512]{2,1,0:T(8,128)(2,1)S(1)} %pad_maximum_fusion.1.refs_12_), channel_id=1, source_target_pairs={{0,8},{1,9},{2,10},{3,11},{4,12},{5,13},{6,14},{7,15},{8,0},{9,1},... | collective-permute-start | bytes 1572872 | tf_op jit(solution)/shard_map/ppermute | solution.py:415
  49.4 0.0 collective-permute-done.15.refs_6_
  49.4 0.0 collective-permute-done.14.refs_5_
  49.5 4.3 %forward.1 = (bf16[128,512]{1,0:T(8,128)(2,1)}, f32[32,16,128]{2,1,0:T(8,128)}) custom-call(s32[133]{0:T(256)S(1)} %query_work.1.work_ref, bf16[4,128,256]{2,1,0:T(8,128)(2,1)S(1)} %copy-done.13, bf16[128,512]{1,0:T(8,128)(2,1)S(1)} %copy-done.12, bf16[512,512]{1,0:T(8,128)(2,1)S(1)} %copy-done.2, bf16[512,512]{1,0:T(8,128)(2,1)S(1)} %copy-done.10, ...), custom_call_target="tpu_custom_call" | custom-call | flops 1000000000 | bytes 4000000 | tf_op jit(solution)/shard_map/forward/pallas_call | solution.py:537
  53.8 3.2 %all-to-all-start = ((f32[32,16,128]{2,1,0:T(8,128)}), f32[32,16,128]{2,1,0:T(8,128)S(1)}, u32[]{:S(2)}, u32[]{:S(2)}) async-start(f32[32,16,128]{2,1,0:T(8,128)} %get-tuple-element.33.stats_hbm), calls=%async_computation | async-start | bytes 524288 | tf_op jit(solution)/shard_map/all_to_all | solution.py:548
  57.0 0.3 collective-permute-start.20
  57.3 0.3 collective-permute-start.23
  57.5 5.5 %query_grad.1.part_hbm = f32[128,512]{1,0:T(8,128)} custom-call(s32[133]{0:T(256)} %copy-done.14, bf16[4,128,256]{2,1,0:T(8,128)(2,1)} %get-tuple-element.26.stack_ref.stack_hbm, bf16[4,128,256]{2,1,0:T(8,128)(2,1)} %get-tuple-element.32.cot_stack_hbm, f32[32,16,128]{2,1,0:T(8,128)} %get-tuple-element.33.stats_hbm, ...), custom_call_target="tpu_custom_call" | custom-call | flops 1000000000 | bytes 4000000 | tf_op jit(solution)/shard_map/query_grad/pallas_call | solution.py:550
  63.1 4.2 %all-to-all-done.stats_all_ref = f32[32,16,128]{2,1,0:T(8,128)S(1)} async-done(((f32[32,16,128]{2,1,0:T(8,128)}), f32[32,16,128]{2,1,0:T(8,128)S(1)}, u32[]{:S(2)}, u32[]{:S(2)}) %all-to-all-start) | async-done | bytes 262176 | tf_op jit(solution)/shard_map/all_to_all | solution.py:548
  67.3 0.4 collective-permute-start.21
  67.7 0.0 collective-permute-done.22.refs_13_
  67.7 0.1 collective-permute-start.24
  67.9 0.0 collective-permute-done.20.refs_10_
  67.9 0.0 collective-permute-done.23.refs_14_
  67.9 1.6 %collective-permute-done.21.refs_11_ = bf16[8,64,512]{2,1,0:T(8,128)(2,1)S(1)} collective-permute-done((bf16[8,64,512]{2,1,0:T(8,128)(2,1)}, bf16[8,64,512]{2,1,0:T(8,128)(2,1)S(1)}, u32[]{:S(2)}, u32[]{:S(2)}) %collective-permute-start.21) | collective-permute-done | bytes 524320 | tf_op jit(solution)/shard_map/ppermute | solution.py:415
  69.5 0.7 collective-permute-done.24.refs_15_
  70.2 0.1 copy-done.22
  70.3 0.8 %copy-done.23 = bf16[8,64,512]{2,1,0:T(8,128)(2,1)} copy-done((bf16[8,64,512]{2,1,0:T(8,128)(2,1)}, bf16[8,64,512]{2,1,0:T(8,128)(2,1)S(1)}, u32[]{:S(2)}) %copy-start.23) | copy-done | bytes 524312
  71.1 5.8 %key_grad.1 = bf16[128,512]{1,0:T(8,128)(2,1)} custom-call(s32[69]{0:T(128)} %copy-done.15, bf16[128,512]{1,0:T(8,128)(2,1)} %get-tuple-element.29.key_hbm, bf16[128,512]{1,0:T(8,128)(2,1)} %get-tuple-element.30.value_hbm, bf16[512,512]{1,0:T(8,128)(2,1)} %wq_hbm.3, bf16[512,512]{1,0:T(8,128)(2,1)} %get-tuple-element.31.wkt_hbm, ...), custom_call_target="tpu_custom_call" | custom-call | flops 1000000000 | bytes 4000000 | tf_op jit(solution)/shard_map/key_grad/pallas_call | solution.py:569
  (67 shorter events, 0.3 us)
Async XLA Ops:
  1.3 7.4 %copy-start.11 = (bf16[128,512]{1,0:T(8,128)(2,1)S(1)}, bf16[128,512]{1,0:T(8,128)(2,1)}, u32[]{:S(2)}) copy-start(bf16[128,512]{1,0:T(8,128)(2,1)} %cot_ref.1) | copy-start | bytes 393220
  2.9 9.0 %copy-start.19 = (bf16[1,144,512]{2,1,0:T(8,128)(2,1)S(1)}, bf16[1,144,512]{2,1,0:T(8,128)(2,1)}, u32[]{:S(2)}) copy-start(bf16[1,144,512]{2,1,0:T(8,128)(2,1)} %pack.1) | copy-start | bytes 442372
  2.9 13.3 %collective-permute-start.2 = (bf16[1,144,512]{2,1,0:T(8,128)(2,1)}, bf16[1,144,512]{2,1,0:T(8,128)(2,1)S(1)}, u32[]{:S(2)}, u32[]{:S(2)}) collective-permute-start(bf16[1,144,512]{2,1,0:T(8,128)(2,1)} %pack.1), channel_id=1, source_target_pairs={{0,6},{1,7},{2,4},{3,5},{4,2},{5,3},{6,0},{7,1},{8,14},{9,15},{10,... | collective-permute-start | bytes 442376 | tf_op jit(solution)/shard_map/ppermute | solution.py:415
  8.1 12.7 %collective-permute-start.1 = (bf16[1,144,512]{2,1,0:T(8,128)(2,1)}, bf16[1,144,512]{2,1,0:T(8,128)(2,1)S(1)}, u32[]{:S(2)}, u32[]{:S(2)}) collective-permute-start(bf16[1,144,512]{2,1,0:T(8,128)(2,1)} %pack.1), channel_id=1, source_target_pairs={{0,4},{1,5},{2,6},{3,7},{4,0},{5,1},{6,2},{7,3},{8,12},{9,13},{10,... | collective-permute-start | bytes 442376 | tf_op jit(solution)/shard_map/ppermute | solution.py:415
  8.1 12.7 %collective-permute-start = (bf16[1,144,512]{2,1,0:T(8,128)(2,1)}, bf16[1,144,512]{2,1,0:T(8,128)(2,1)S(1)}, u32[]{:S(2)}, u32[]{:S(2)}) collective-permute-start(bf16[1,144,512]{2,1,0:T(8,128)(2,1)} %pack.1), channel_id=1, source_target_pairs={{0,2},{1,3},{2,0},{3,1},{4,6},{5,7},{6,4},{7,5},{8,10},{9,11},{10,... | collective-permute-start | bytes 442376 | tf_op jit(solution)/shard_map/ppermute | solution.py:415
  8.7 4.3 %collective-permute-start.3 = (bf16[1,64,512]{2,1,0:T(8,128)(2,1)S(1)}, bf16[1,64,512]{2,1,0:T(8,128)(2,1)S(1)}, u32[]{:S(2)}, u32[]{:S(2)}) collective-permute-start(bf16[1,64,512]{2,1,0:T(8,128)(2,1)S(1)} %get-tuple-element.50), channel_id=1, source_target_pairs={{0,8},{1,9},{2,10},{3,11},{4,12},{5,13},{6,14},{7,15},{8,0},{9,1},... | collective-permute-start | bytes 196616 | tf_op jit(solution)/shard_map/ppermute | solution.py:415
  10.4 5.2 %collective-permute-start.4 = (bf16[1,64,512]{2,1,0:T(8,128)(2,1)S(1)}, bf16[1,64,512]{2,1,0:T(8,128)(2,1)S(1)}, u32[]{:S(2)}, u32[]{:S(2)}) collective-permute-start(bf16[1,64,512]{2,1,0:T(8,128)(2,1)S(1)} %get-tuple-element.51), channel_id=1, source_target_pairs={{0,16},{1,17},{2,18},{3,19},{4,20},{5,21},{6,22},{7,23},{8,24},{9,... | collective-permute-start | bytes 196616 | tf_op jit(solution)/shard_map/ppermute | solution.py:415
  13.0 7.7 %collective-permute-start.7 = (bf16[1,144,512]{2,1,0:T(8,128)(2,1)S(1)}, bf16[1,144,512]{2,1,0:T(8,128)(2,1)S(1)}, u32[]{:S(2)}, u32[]{:S(2)}) collective-permute-start(bf16[1,144,512]{2,1,0:T(8,128)(2,1)S(1)} %copy-done.19), channel_id=1, source_target_pairs={{0,24},{1,25},{2,26},{3,27},{4,28},{5,29},{6,30},{7,31},{8,16},{9,... | collective-permute-start | bytes 442376 | tf_op jit(solution)/shard_map/ppermute | solution.py:415
  15.6 5.9 %collective-permute-start.6 = (bf16[1,144,512]{2,1,0:T(8,128)(2,1)S(1)}, bf16[1,144,512]{2,1,0:T(8,128)(2,1)S(1)}, u32[]{:S(2)}, u32[]{:S(2)}) collective-permute-start(bf16[1,144,512]{2,1,0:T(8,128)(2,1)S(1)} %copy-done.19), channel_id=1, source_target_pairs={{0,16},{1,17},{2,18},{3,19},{4,20},{5,21},{6,22},{7,23},{8,24},{9,... | collective-permute-start | bytes 442376 | tf_op jit(solution)/shard_map/ppermute | solution.py:415
  16.2 5.3 %collective-permute-start.5 = (bf16[1,144,512]{2,1,0:T(8,128)(2,1)S(1)}, bf16[1,144,512]{2,1,0:T(8,128)(2,1)S(1)}, u32[]{:S(2)}, u32[]{:S(2)}) collective-permute-start(bf16[1,144,512]{2,1,0:T(8,128)(2,1)S(1)} %copy-done.19), channel_id=1, source_target_pairs={{0,8},{1,9},{2,10},{3,11},{4,12},{5,13},{6,14},{7,15},{8,0},{9,1},... | collective-permute-start | bytes 442376 | tf_op jit(solution)/shard_map/ppermute | solution.py:415
  21.5 13.7 %collective-permute-start.17 = (bf16[4,64,512]{2,1,0:T(8,128)(2,1)S(1)}, bf16[4,64,512]{2,1,0:T(8,128)(2,1)S(1)}, u32[]{:S(2)}, u32[]{:S(2)}) collective-permute-start(bf16[4,64,512]{2,1,0:T(8,128)(2,1)S(1)} %pad_maximum_fusion.4), channel_id=1, source_target_pairs={{0,4},{1,5},{2,6},{3,7},{4,0},{5,1},{6,2},{7,3},{8,12},{9,13},{10,... | collective-permute-start | bytes 786440 | tf_op jit(solution)/shard_map/ppermute | solution.py:415
  25.5 9.7 %collective-permute-start.8 = (bf16[4,64,512]{2,1,0:T(8,128)(2,1)S(1)}, bf16[4,64,512]{2,1,0:T(8,128)(2,1)S(1)}, u32[]{:S(2)}, u32[]{:S(2)}) collective-permute-start(bf16[4,64,512]{2,1,0:T(8,128)(2,1)S(1)} %pad_maximum_fusion.4), channel_id=1, source_target_pairs={{0,2},{1,3},{2,0},{3,1},{4,6},{5,7},{6,4},{7,5},{8,10},{9,11},{10,... | collective-permute-start | bytes 786440 | tf_op jit(solution)/shard_map/ppermute | solution.py:415
  25.7 15.1 %collective-permute-start.12 = (bf16[3,128,512]{2,1,0:T(8,128)(2,1)S(1)}, bf16[3,128,512]{2,1,0:T(8,128)(2,1)S(1)}, u32[]{:S(2)}, u32[]{:S(2)}) collective-permute-start(bf16[3,128,512]{2,1,0:T(8,128)(2,1)S(1)} %pad_maximum_fusion.2), channel_id=1, source_target_pairs={{0,24},{1,25},{2,26},{3,27},{4,28},{5,29},{6,30},{7,31},{8,16},{9,... | collective-permute-start | bytes 1179656 | tf_op jit(solution)/shard_map/ppermute | solution.py:415
  27.9 14.8 %collective-permute-start.11 = (bf16[3,128,512]{2,1,0:T(8,128)(2,1)S(1)}, bf16[3,128,512]{2,1,0:T(8,128)(2,1)S(1)}, u32[]{:S(2)}, u32[]{:S(2)}) collective-permute-start(bf16[3,128,512]{2,1,0:T(8,128)(2,1)S(1)} %pad_maximum_fusion.2), channel_id=1, source_target_pairs={{0,16},{1,17},{2,18},{3,19},{4,20},{5,21},{6,22},{7,23},{8,24},{9,... | collective-permute-start | bytes 1179656 | tf_op jit(solution)/shard_map/ppermute | solution.py:415
  28.4 14.9 %collective-permute-start.10 = (bf16[3,128,512]{2,1,0:T(8,128)(2,1)S(1)}, bf16[3,128,512]{2,1,0:T(8,128)(2,1)S(1)}, u32[]{:S(2)}, u32[]{:S(2)}) collective-permute-start(bf16[3,128,512]{2,1,0:T(8,128)(2,1)S(1)} %pad_maximum_fusion.2), channel_id=1, source_target_pairs={{0,8},{1,9},{2,10},{3,11},{4,12},{5,13},{6,14},{7,15},{8,0},{9,1},... | collective-permute-start | bytes 1179656 | tf_op jit(solution)/shard_map/ppermute | solution.py:415
  29.3 20.1 %copy-start = (bf16[7,128,512]{2,1,0:T(8,128)(2,1)}, bf16[7,128,512]{2,1,0:T(8,128)(2,1)S(1)}, u32[]{:S(2)}) copy-start(bf16[7,128,512]{2,1,0:T(8,128)(2,1)S(1)} %constant_dynamic-update-slice_fusion.refs_0_) | copy-start | bytes 2752516
  34.4 0.5 copy-start.15
  35.2 14.2 %collective-permute-start.13 = (bf16[7,128,512]{2,1,0:T(8,128)(2,1)S(1)}, bf16[7,128,512]{2,1,0:T(8,128)(2,1)S(1)}, u32[]{:S(2)}, u32[]{:S(2)}) collective-permute-start(bf16[7,128,512]{2,1,0:T(8,128)(2,1)S(1)} %constant_dynamic-update-slice_fusion.refs_0_), channel_id=1, source_target_pairs={{0,1},{1,0},{2,3},{3,2},{4,5},{5,4},{6,7},{7,6},{8,9},{9,8},{10,11... | collective-permute-start | bytes 2752520 | tf_op jit(solution)/shard_map/ppermute | solution.py:415
  35.2 2.5 %collective-permute-start.9 = (bf16[4,16,128]{2,1,0:T(8,128)(2,1)S(1)}, bf16[4,16,128]{2,1,0:T(8,128)(2,1)S(1)}, u32[]{:S(2)}, u32[]{:S(2)}) collective-permute-start(bf16[4,16,128]{2,1,0:T(8,128)(2,1)S(1)} %pad_maximum_fusion.5), channel_id=1, source_target_pairs={{0,1},{1,0},{2,3},{3,2},{4,5},{5,4},{6,7},{7,6},{8,9},{9,8},{10,11... | collective-permute-start | bytes 49160 | tf_op jit(solution)/shard_map/ppermute | solution.py:415
  37.7 8.3 %collective-permute-start.18 = (bf16[4,64,512]{2,1,0:T(8,128)(2,1)S(1)}, bf16[4,64,512]{2,1,0:T(8,128)(2,1)S(1)}, u32[]{:S(2)}, u32[]{:S(2)}) collective-permute-start(bf16[4,64,512]{2,1,0:T(8,128)(2,1)S(1)} %collective-permute-done.17), channel_id=1, source_target_pairs={{0,2},{1,3},{2,0},{3,1},{4,6},{5,7},{6,4},{7,5},{8,10},{9,11},{10,... | collective-permute-start | bytes 786440 | tf_op jit(solution)/shard_map/ppermute | solution.py:415
  40.8 8.6 %copy-start.14 = (s32[133]{0:T(256)}, s32[133]{0:T(256)S(1)}, u32[]{:S(2)}) copy-start(s32[133]{0:T(256)S(1)} %query_work.1.work_ref) | copy-start | bytes 1600
  40.8 8.6 %copy-start.4 = (bf16[3,128,512]{2,1,0:T(8,128)(2,1)}, bf16[3,128,512]{2,1,0:T(8,128)(2,1)S(1)}, u32[]{:S(2)}) copy-start(bf16[3,128,512]{2,1,0:T(8,128)(2,1)S(1)} %collective-permute-done.12.refs_3_) | copy-start | bytes 1179652
  40.8 7.0 %collective-permute-start.16 = (bf16[3,128,512]{2,1,0:T(8,128)(2,1)S(1)}, bf16[3,128,512]{2,1,0:T(8,128)(2,1)S(1)}, u32[]{:S(2)}, u32[]{:S(2)}) collective-permute-start(bf16[3,128,512]{2,1,0:T(8,128)(2,1)S(1)} %collective-permute-done.12.refs_3_), channel_id=1, source_target_pairs={{0,1},{1,0},{2,3},{3,2},{4,5},{5,4},{6,7},{7,6},{8,9},{9,8},{10,11... | collective-permute-start | bytes 1179656 | tf_op jit(solution)/shard_map/ppermute | solution.py:415
  42.7 6.7 %copy-start.5 = (bf16[3,128,512]{2,1,0:T(8,128)(2,1)}, bf16[3,128,512]{2,1,0:T(8,128)(2,1)S(1)}, u32[]{:S(2)}) copy-start(bf16[3,128,512]{2,1,0:T(8,128)(2,1)S(1)} %collective-permute-done.11.refs_2_) | copy-start | bytes 1179652
  42.7 6.7 %collective-permute-start.15 = (bf16[3,128,512]{2,1,0:T(8,128)(2,1)S(1)}, bf16[3,128,512]{2,1,0:T(8,128)(2,1)S(1)}, u32[]{:S(2)}, u32[]{:S(2)}) collective-permute-start(bf16[3,128,512]{2,1,0:T(8,128)(2,1)S(1)} %collective-permute-done.11.refs_2_), channel_id=1, source_target_pairs={{0,1},{1,0},{2,3},{3,2},{4,5},{5,4},{6,7},{7,6},{8,9},{9,8},{10,11... | collective-permute-start | bytes 1179656 | tf_op jit(solution)/shard_map/ppermute | solution.py:415
  43.4 6.1 %copy-start.6 = (bf16[3,128,512]{2,1,0:T(8,128)(2,1)}, bf16[3,128,512]{2,1,0:T(8,128)(2,1)S(1)}, u32[]{:S(2)}) copy-start(bf16[3,128,512]{2,1,0:T(8,128)(2,1)S(1)} %collective-permute-done.10.refs_1_) | copy-start | bytes 1179652
  43.4 6.0 %collective-permute-start.14 = (bf16[3,128,512]{2,1,0:T(8,128)(2,1)S(1)}, bf16[3,128,512]{2,1,0:T(8,128)(2,1)S(1)}, u32[]{:S(2)}, u32[]{:S(2)}) collective-permute-start(bf16[3,128,512]{2,1,0:T(8,128)(2,1)S(1)} %collective-permute-done.10.refs_1_), channel_id=1, source_target_pairs={{0,1},{1,0},{2,3},{3,2},{4,5},{5,4},{6,7},{7,6},{8,9},{9,8},{10,11... | collective-permute-start | bytes 1179656 | tf_op jit(solution)/shard_map/ppermute | solution.py:415
  46.1 3.4 %copy-start.10 = (bf16[512,512]{1,0:T(8,128)(2,1)S(1)}, bf16[512,512]{1,0:T(8,128)(2,1)}, u32[]{:S(2)}) copy-start(bf16[512,512]{1,0:T(8,128)(2,1)} %get-tuple-element.27.wvt_ref.wvt_hbm) | copy-start | bytes 1572868
  46.1 3.4 %copy-start.12 = (bf16[128,512]{1,0:T(8,128)(2,1)S(1)}, bf16[128,512]{1,0:T(8,128)(2,1)}, u32[]{:S(2)}) copy-start(bf16[128,512]{1,0:T(8,128)(2,1)} %cot_ref.1) | copy-start | bytes 393220
  46.1 3.4 %copy-start.13 = (bf16[4,128,256]{2,1,0:T(8,128)(2,1)S(1)}, bf16[4,128,256]{2,1,0:T(8,128)(2,1)}, u32[]{:S(2)}) copy-start(bf16[4,128,256]{2,1,0:T(8,128)(2,1)} %get-tuple-element.26.stack_ref.stack_hbm) | copy-start | bytes 786436
  46.2 11.1 %copy-start.16 = (bf16[8,64,512]{2,1,0:T(8,128)(2,1)}, bf16[8,64,512]{2,1,0:T(8,128)(2,1)S(1)}, u32[]{:S(2)}) copy-start(bf16[8,64,512]{2,1,0:T(8,128)(2,1)S(1)} %pad_maximum_fusion.1.refs_12_) | copy-start | bytes 1572868
  46.2 3.3 %copy-start.2 = (bf16[512,512]{1,0:T(8,128)(2,1)S(1)}, bf16[512,512]{1,0:T(8,128)(2,1)}, u32[]{:S(2)}) copy-start(bf16[512,512]{1,0:T(8,128)(2,1)} %wk_hbm.3) | copy-start | bytes 1572868
  46.2 3.3 %copy-start.3 = (s32[240,128,4]{1,2,0:T(4,128)S(1)}, s32[240,128,4]{1,2,0:T(4,128)}, u32[]{:S(2)}) copy-start(s32[240,128,4]{1,2,0:T(4,128)} %param.15) | copy-start | bytes 1474564
  46.3 10.7 %copy-start.17 = (bf16[8,64,512]{2,1,0:T(8,128)(2,1)}, bf16[8,64,512]{2,1,0:T(8,128)(2,1)S(1)}, u32[]{:S(2)}) copy-start(bf16[8,64,512]{2,1,0:T(8,128)(2,1)S(1)} %pad_maximum_fusion.refs_8_) | copy-start | bytes 1572868
  46.3 16.8 %collective-permute-start.19 = (bf16[8,64,512]{2,1,0:T(8,128)(2,1)S(1)}, bf16[8,64,512]{2,1,0:T(8,128)(2,1)}, u32[]{:S(2)}, u32[]{:S(2)}) collective-permute-start(bf16[8,64,512]{2,1,0:T(8,128)(2,1)S(1)} %pad_maximum_fusion.refs_8_), channel_id=1, source_target_pairs={{0,16},{1,17},{2,18},{3,19},{4,20},{5,21},{6,22},{7,23},{8,24},{9,... | collective-permute-start | bytes 1572872 | tf_op jit(solution)/shard_map/ppermute | solution.py:415
  47.9 5.9 %copy-start.7 = (bf16[3,128,512]{2,1,0:T(8,128)(2,1)}, bf16[3,128,512]{2,1,0:T(8,128)(2,1)S(1)}, u32[]{:S(2)}) copy-start(bf16[3,128,512]{2,1,0:T(8,128)(2,1)S(1)} %collective-permute-done.16.refs_7_) | copy-start | bytes 1179652
  47.9 19.9 %collective-permute-start.22 = (bf16[8,64,512]{2,1,0:T(8,128)(2,1)S(1)}, bf16[8,64,512]{2,1,0:T(8,128)(2,1)}, u32[]{:S(2)}, u32[]{:S(2)}) collective-permute-start(bf16[8,64,512]{2,1,0:T(8,128)(2,1)S(1)} %pad_maximum_fusion.1.refs_12_), channel_id=1, source_target_pairs={{0,8},{1,9},{2,10},{3,11},{4,12},{5,13},{6,14},{7,15},{8,0},{9,1},... | collective-permute-start | bytes 1572872 | tf_op jit(solution)/shard_map/ppermute | solution.py:415
  49.4 4.4 %copy-start.8 = (bf16[3,128,512]{2,1,0:T(8,128)(2,1)}, bf16[3,128,512]{2,1,0:T(8,128)(2,1)S(1)}, u32[]{:S(2)}) copy-start(bf16[3,128,512]{2,1,0:T(8,128)(2,1)S(1)} %collective-permute-done.15.refs_6_) | copy-start | bytes 1179652
  49.4 4.4 %copy-start.9 = (bf16[3,128,512]{2,1,0:T(8,128)(2,1)}, bf16[3,128,512]{2,1,0:T(8,128)(2,1)S(1)}, u32[]{:S(2)}) copy-start(bf16[3,128,512]{2,1,0:T(8,128)(2,1)S(1)} %collective-permute-done.14.refs_5_) | copy-start | bytes 1179652
  49.4 4.4 %copy-start.1 = (bf16[7,128,512]{2,1,0:T(8,128)(2,1)}, bf16[7,128,512]{2,1,0:T(8,128)(2,1)S(1)}, u32[]{:S(2)}) copy-start(bf16[7,128,512]{2,1,0:T(8,128)(2,1)S(1)} %collective-permute-done.13.refs_4_) | copy-start | bytes 2752516
  53.8 13.6 %all-to-all-start = ((f32[32,16,128]{2,1,0:T(8,128)}), f32[32,16,128]{2,1,0:T(8,128)S(1)}, u32[]{:S(2)}, u32[]{:S(2)}) async-start(f32[32,16,128]{2,1,0:T(8,128)} %get-tuple-element.33.stats_hbm), calls=%async_computation | async-start | bytes 524288 | tf_op jit(solution)/shard_map/all_to_all | solution.py:548
  57.0 10.9 %collective-permute-start.20 = (bf16[8,64,512]{2,1,0:T(8,128)(2,1)S(1)}, bf16[8,64,512]{2,1,0:T(8,128)(2,1)S(1)}, u32[]{:S(2)}, u32[]{:S(2)}) collective-permute-start(bf16[8,64,512]{2,1,0:T(8,128)(2,1)S(1)} %pad_maximum_fusion.refs_8_), channel_id=1, source_target_pairs={{0,1},{1,0},{2,3},{3,2},{4,5},{5,4},{6,7},{7,6},{8,9},{9,8},{10,11... | collective-permute-start | bytes 1572872 | tf_op jit(solution)/shard_map/ppermute | solution.py:415
  57.3 10.6 %collective-permute-start.23 = (bf16[8,64,512]{2,1,0:T(8,128)(2,1)S(1)}, bf16[8,64,512]{2,1,0:T(8,128)(2,1)S(1)}, u32[]{:S(2)}, u32[]{:S(2)}) collective-permute-start(bf16[8,64,512]{2,1,0:T(8,128)(2,1)S(1)} %pad_maximum_fusion.1.refs_12_), channel_id=1, source_target_pairs={{0,1},{1,0},{2,3},{3,2},{4,5},{5,4},{6,7},{7,6},{8,9},{9,8},{10,11... | collective-permute-start | bytes 1572872 | tf_op jit(solution)/shard_map/ppermute | solution.py:415
  67.3 2.9 %copy-start.18 = (f32[32,16,128]{2,1,0:T(8,128)}, f32[32,16,128]{2,1,0:T(8,128)S(1)}, u32[]{:S(2)}) copy-start(f32[32,16,128]{2,1,0:T(8,128)S(1)} %all-to-all-done.stats_all_ref) | copy-start | bytes 786436
  67.3 2.1 %collective-permute-start.21 = (bf16[8,64,512]{2,1,0:T(8,128)(2,1)}, bf16[8,64,512]{2,1,0:T(8,128)(2,1)S(1)}, u32[]{:S(2)}, u32[]{:S(2)}) collective-permute-start(bf16[8,64,512]{2,1,0:T(8,128)(2,1)} %collective-permute-done.19.refs_9_), channel_id=1, source_target_pairs={{0,1},{1,0},{2,3},{3,2},{4,5},{5,4},{6,7},{7,6},{8,9},{9,8},{10,11... | collective-permute-start | bytes 1572872 | tf_op jit(solution)/shard_map/ppermute | solution.py:415
  67.7 2.5 %collective-permute-start.24 = (bf16[8,64,512]{2,1,0:T(8,128)(2,1)}, bf16[8,64,512]{2,1,0:T(8,128)(2,1)S(1)}, u32[]{:S(2)}, u32[]{:S(2)}) collective-permute-start(bf16[8,64,512]{2,1,0:T(8,128)(2,1)} %collective-permute-done.22.refs_13_), channel_id=1, source_target_pairs={{0,1},{1,0},{2,3},{3,2},{4,5},{5,4},{6,7},{7,6},{8,9},{9,8},{10,11... | collective-permute-start | bytes 1572872 | tf_op jit(solution)/shard_map/ppermute | solution.py:415
  67.9 2.4 %copy-start.20 = (bf16[8,64,512]{2,1,0:T(8,128)(2,1)}, bf16[8,64,512]{2,1,0:T(8,128)(2,1)S(1)}, u32[]{:S(2)}) copy-start(bf16[8,64,512]{2,1,0:T(8,128)(2,1)S(1)} %collective-permute-done.20.refs_10_) | copy-start | bytes 1572868
  67.9 2.4 %copy-start.21 = (bf16[8,64,512]{2,1,0:T(8,128)(2,1)}, bf16[8,64,512]{2,1,0:T(8,128)(2,1)S(1)}, u32[]{:S(2)}) copy-start(bf16[8,64,512]{2,1,0:T(8,128)(2,1)S(1)} %collective-permute-done.23.refs_14_) | copy-start | bytes 1572868
  69.5 0.8 %copy-start.22 = (bf16[8,64,512]{2,1,0:T(8,128)(2,1)}, bf16[8,64,512]{2,1,0:T(8,128)(2,1)S(1)}, u32[]{:S(2)}) copy-start(bf16[8,64,512]{2,1,0:T(8,128)(2,1)S(1)} %collective-permute-done.21.refs_11_) | copy-start | bytes 1572868
  70.3 0.8 %copy-start.23 = (bf16[8,64,512]{2,1,0:T(8,128)(2,1)}, bf16[8,64,512]{2,1,0:T(8,128)(2,1)S(1)}, u32[]{:S(2)}) copy-start(bf16[8,64,512]{2,1,0:T(8,128)(2,1)S(1)} %collective-permute-done.24.refs_15_) | copy-start | bytes 1572868

commit v4 on v3

--- a/solution.py
+++ b/solution.py
@@ -510,11 +510,12 @@
         mask //= 2
 
     line_lists = jnp.concatenate([entry[:, block:, :128] for entry in lined], 0)
-    line_lists = after(line_lists, pieces[lines // 2])
+    other_near = swap(after(near, pieces[lines // 2]), 1)
+    line_lists = after(line_lists, other_near)
     row_lists = jnp.concatenate([line_lists, swap(line_lists, 1)], 0)
     query_work = work(query_work_kernel, row_lists, blks, "query_work")
     here = [near] + there
-    rows_all = here + [swap(group, 1) for group in here]
+    rows_all = here + [other_near] + [swap(group, 1) for group in there]
 
     cots_here = []
     for k in range(2):

time: 76.7 us -> 76.6 us (level); the launches traced: 76.9 us -> 76 us
  starting transfers between devices: 29.6 us -> 28.5 us
  Pallas kernels: 23.8 us -> 24.9 us
    pallas_call x1, Pallas kernels: 4.25 us -> 5.6 us  [local(): pl.pallas_call(functools.partial(forward_kernel, sizes), out_shape=(own,...]
    pallas_call x1, Pallas kernels: 5.8 us -> 4.57 us  [local(): pl.pallas_call(functools.partial(key_grad_kernel, sizes, bits), out_shape...]
    all_to_all x1, waiting for transfers between devices: 4.24 us -> 3.07 us  [local(): stats_all = lax.all_to_all(stats, axes, 0, 0, tiled=True)]
    pallas_call x1, Pallas kernels: 5.54 us -> 6.69 us  [local(): pl.pallas_call(functools.partial(query_grad_kernel, sizes), out_shape=sha...]
  transfers between devices with their start and end apart: 26 -> 26, of which waited for: 11 -> 11; matrix products, arithmetic and copies ran while one was open for 1% -> 0% of each run, Pallas kernels for 21% -> 25%
where the time goes in v4:
time: 76.6 us; the launch traced here: 76 us
  starting transfers between devices  28.5 us (37%)
  Pallas kernels  24.9 us (33%)
  waiting for transfers between devices  19.1 us (25%)
  between operations  1.82 us (2%)
  local copies, waits for them, and re-layouts  1.53 us (2%)
    ppermute x25, starting transfers between devices, swap(): return lax.ppermute(block, axes, [(i, i ^ mask) for i in range(count)])  25.9 us
    ppermute x25, waiting for transfers between devices, swap(): return lax.ppermute(block, axes, [(i, i ^ mask) for i in range(count)])  16 us
    pallas_call x1, Pallas kernels, local(): pl.pallas_call(functools.partial(query_grad_kernel, sizes), out_shape=sha...  6.69 us
    pallas_call x1, Pallas kernels, local(): pl.pallas_call(functools.partial(forward_kernel, sizes), out_shape=(own,...  5.6 us
    pallas_call x1, Pallas kernels, local(): pl.pallas_call(functools.partial(key_grad_kernel, sizes, bits), out_shape...  4.57 us
    pallas_call x1, Pallas kernels, local(): pl.pallas_call(prepare_kernel, out_shape=(stacks, stacks, own, own, squar...  3.33 us
    all_to_all x1, waiting for transfers between devices, local(): stats_all = lax.all_to_all(stats, axes, 0, 0, tiled=True)  3.07 us
    pallas_call x2, Pallas kernels, work(): pl.pallas_call(functools.partial(kernel, sizes), out_shape=shape((2 * cou...  3.05 us
  transfers between devices with their start and end apart: 26, of which 11 were waited for; matrix products, arithmetic and copies ran while one was open for 0% of the time, Pallas kernels for 25%

profile of v4, /device:TPU:0, one launch (start us, length us, event | category | flops | bytes accessed | tf_op | source)
XLA Modules:
  0.0 76.0 jit_solution(1291061672766456059)
XLA Ops:
  1.3 0.0 copy-start.11
  1.3 1.6 %pack.1 = bf16[1,144,512]{2,1,0:T(8,128)(2,1)} custom-call(bf16[128,512]{1,0:T(8,128)(2,1)} %own_hbm.2, s32[1,3,1,8]{3,2,1,0:T(1,128)} %bitcast.13, s32[1,1]{1,0:T(1,128)S(6)} %copy.14.count_hbm), custom_call_target="tpu_custom_call" | custom-call | tf_op jit(solution)/shard_map/pack/pallas_call | solution.py:441
  2.9 5.1 %collective-permute-start.2 = (bf16[1,144,512]{2,1,0:T(8,128)(2,1)}, bf16[1,144,512]{2,1,0:T(8,128)(2,1)S(1)}, u32[]{:S(2)}, u32[]{:S(2)}) collective-permute-start(bf16[1,144,512]{2,1,0:T(8,128)(2,1)} %pack.1), channel_id=1, source_target_pairs={{0,6},{1,7},{2,4},{3,5},{4,2},{5,3},{6,0},{7,1},{8,14},{9,15},{10,... | collective-permute-start | bytes 442376 | tf_op jit(solution)/shard_map/ppermute | solution.py:415
  8.1 0.0 collective-permute-start.1
  8.1 0.6 collective-permute-start
  8.7 1.7 %collective-permute-start.7 = (bf16[1,64,512]{2,1,0:T(8,128)(2,1)S(1)}, bf16[1,64,512]{2,1,0:T(8,128)(2,1)S(1)}, u32[]{:S(2)}, u32[]{:S(2)}) collective-permute-start(bf16[1,64,512]{2,1,0:T(8,128)(2,1)S(1)} %get-tuple-element.52), channel_id=1, source_target_pairs={{0,16},{1,17},{2,18},{3,19},{4,20},{5,21},{6,22},{7,23},{8,24},{9,... | collective-permute-start | bytes 196616 | tf_op jit(solution)/shard_map/ppermute | solution.py:415
  10.4 1.5 %collective-permute-start.6 = (bf16[1,64,512]{2,1,0:T(8,128)(2,1)S(1)}, bf16[1,64,512]{2,1,0:T(8,128)(2,1)S(1)}, u32[]{:S(2)}, u32[]{:S(2)}) collective-permute-start(bf16[1,64,512]{2,1,0:T(8,128)(2,1)S(1)} %get-tuple-element.53), channel_id=1, source_target_pairs={{0,8},{1,9},{2,10},{3,11},{4,12},{5,13},{6,14},{7,15},{8,0},{9,1},... | collective-permute-start | bytes 196616 | tf_op jit(solution)/shard_map/ppermute | solution.py:415
  12.0 1.1 %collective-permute-done.7 = bf16[1,64,512]{2,1,0:T(8,128)(2,1)S(1)} collective-permute-done((bf16[1,64,512]{2,1,0:T(8,128)(2,1)S(1)}, bf16[1,64,512]{2,1,0:T(8,128)(2,1)S(1)}, u32[]{:S(2)}, u32[]{:S(2)}) %collective-permute-start.7) | collective-permute-done | bytes 65568 | tf_op jit(solution)/shard_map/ppermute | solution.py:415
  13.0 2.6 %collective-permute-start.5 = (bf16[1,144,512]{2,1,0:T(8,128)(2,1)S(1)}, bf16[1,144,512]{2,1,0:T(8,128)(2,1)S(1)}, u32[]{:S(2)}, u32[]{:S(2)}) collective-permute-start(bf16[1,144,512]{2,1,0:T(8,128)(2,1)S(1)} %copy-done.19), channel_id=1, source_target_pairs={{0,24},{1,25},{2,26},{3,27},{4,28},{5,29},{6,30},{7,31},{8,16},{9,... | collective-permute-start | bytes 442376 | tf_op jit(solution)/shard_map/ppermute | solution.py:415
  15.6 0.0 collective-permute-done.6
  15.6 0.5 collective-permute-start.4
  16.1 0.0 collective-permute-done.2
  16.1 0.6 collective-permute-start.3
  16.7 4.0 %collective-permute-done.1 = bf16[1,144,512]{2,1,0:T(8,128)(2,1)S(1)} collective-permute-done((bf16[1,144,512]{2,1,0:T(8,128)(2,1)}, bf16[1,144,512]{2,1,0:T(8,128)(2,1)S(1)}, u32[]{:S(2)}, u32[]{:S(2)}) %collective-permute-start.1) | collective-permute-done | bytes 147488 | tf_op jit(solution)/shard_map/ppermute | solution.py:415
  20.7 0.0 collective-permute-done
  20.8 0.0 collective-permute-done.5
  20.8 0.7 collective-permute-done.4
  21.5 0.0 collective-permute-done.3
  21.5 4.0 %collective-permute-start.17 = (bf16[4,64,512]{2,1,0:T(8,128)(2,1)S(1)}, bf16[4,64,512]{2,1,0:T(8,128)(2,1)S(1)}, u32[]{:S(2)}, u32[]{:S(2)}) collective-permute-start(bf16[4,64,512]{2,1,0:T(8,128)(2,1)S(1)} %pad_maximum_fusion.4), channel_id=1, source_target_pairs={{0,4},{1,5},{2,6},{3,7},{4,0},{5,1},{6,2},{7,3},{8,12},{9,13},{10,... | collective-permute-start | bytes 786440 | tf_op jit(solution)/shard_map/ppermute | solution.py:415
  25.6 0.2 collective-permute-start.8
  25.8 2.2 %collective-permute-start.13 = (bf16[3,128,512]{2,1,0:T(8,128)(2,1)S(1)}, bf16[3,128,512]{2,1,0:T(8,128)(2,1)S(1)}, u32[]{:S(2)}, u32[]{:S(2)}) collective-permute-start(bf16[3,128,512]{2,1,0:T(8,128)(2,1)S(1)} %pad_maximum_fusion.2), channel_id=1, source_target_pairs={{0,24},{1,25},{2,26},{3,27},{4,28},{5,29},{6,30},{7,31},{8,16},{9,... | collective-permute-start | bytes 1179656 | tf_op jit(solution)/shard_map/ppermute | solution.py:415
  28.0 0.5 collective-permute-start.12
  28.5 0.8 collective-permute-start.11
  29.4 3.3 %prepare.1 = (bf16[4,128,256]{2,1,0:T(8,128)(2,1)}, bf16[4,128,256]{2,1,0:T(8,128)(2,1)}, bf16[128,512]{1,0:T(8,128)(2,1)}, bf16[128,512]{1,0:T(8,128)(2,1)}, bf...) custom-call(bf16[128,512]{1,0:T(8,128)(2,1)} %own_hbm.2, bf16[128,512]{1,0:T(8,128)(2,1)} %cot_ref.1, ...), custom_call_target="tpu_custom_call" | custom-call | flops 400000000 | bytes 4000000 | tf_op jit(solution)/shard_map/prepare/pallas_call | solution.py:487
  32.7 1.4 %key_work.1.work_ref = s32[69]{0:T(128)S(1)} custom-call(s32[4,128]{1,0:T(4,128)S(1)} %bitcast.12), custom_call_target="tpu_custom_call" | custom-call | flops 200000000 | bytes 4000000 | tf_op jit(solution)/shard_map/key_work/pallas_call | solution.py:469
  34.1 0.5 copy-done.15
  34.6 0.6 collective-permute-done.8
  35.2 0.0 collective-permute-start.9
  35.3 0.0 collective-permute-done.17
  35.3 1.3 %collective-permute-start.18 = (bf16[4,64,512]{2,1,0:T(8,128)(2,1)S(1)}, bf16[4,64,512]{2,1,0:T(8,128)(2,1)S(1)}, u32[]{:S(2)}, u32[]{:S(2)}) collective-permute-start(bf16[4,64,512]{2,1,0:T(8,128)(2,1)S(1)} %collective-permute-done.17), channel_id=1, source_target_pairs={{0,2},{1,3},{2,0},{3,1},{4,6},{5,7},{6,4},{7,5},{8,10},{9,11},{10,... | collective-permute-start | bytes 786440 | tf_op jit(solution)/shard_map/ppermute | solution.py:415
  36.6 2.0 %collective-permute-done.13.refs_3_ = bf16[3,128,512]{2,1,0:T(8,128)(2,1)S(1)} collective-permute-done((bf16[3,128,512]{2,1,0:T(8,128)(2,1)S(1)}, bf16[3,128,512]{2,1,0:T(8,128)(2,1)S(1)}, u32[]{:S(2)}, u32[]{:S(2)}) %collective-permute-start.13) | collective-permute-done | bytes 393248 | tf_op jit(solution)/shard_map/ppermute | solution.py:415
  38.6 0.0 collective-permute-start.16
  38.6 4.1 %collective-permute-done.12.refs_2_ = bf16[3,128,512]{2,1,0:T(8,128)(2,1)S(1)} collective-permute-done((bf16[3,128,512]{2,1,0:T(8,128)(2,1)S(1)}, bf16[3,128,512]{2,1,0:T(8,128)(2,1)S(1)}, u32[]{:S(2)}, u32[]{:S(2)}) %collective-permute-start.12) | collective-permute-done | bytes 393248 | tf_op jit(solution)/shard_map/ppermute | solution.py:415
  42.7 0.7 collective-permute-done.11.refs_1_
  43.5 0.0 collective-permute-start.14
  43.5 0.6 collective-permute-done.18
  44.1 0.1 pad_maximum_fusion.1.refs_12_
  44.2 0.0 collective-permute-done.9.refs_4_
  44.2 0.1 collective-permute-start.10
  44.3 0.0 copy-start.3
  44.3 0.1 pad_maximum_fusion.refs_8_
  44.4 0.0 copy-start.2
  44.4 1.5 %collective-permute-start.19 = (bf16[8,64,512]{2,1,0:T(8,128)(2,1)S(1)}, bf16[8,64,512]{2,1,0:T(8,128)(2,1)S(1)}, u32[]{:S(2)}, u32[]{:S(2)}) collective-permute-start(bf16[8,64,512]{2,1,0:T(8,128)(2,1)S(1)} %pad_maximum_fusion.refs_8_), channel_id=1, source_target_pairs={{0,16},{1,17},{2,18},{3,19},{4,20},{5,21},{6,22},{7,23},{8,24},{9,... | collective-permute-start | bytes 1572872 | tf_op jit(solution)/shard_map/ppermute | solution.py:415
  45.9 0.0 collective-permute-done.10
  45.9 1.5 %collective-permute-start.22 = (bf16[8,64,512]{2,1,0:T(8,128)(2,1)S(1)}, bf16[8,64,512]{2,1,0:T(8,128)(2,1)S(1)}, u32[]{:S(2)}, u32[]{:S(2)}) collective-permute-start(bf16[8,64,512]{2,1,0:T(8,128)(2,1)S(1)} %pad_maximum_fusion.1.refs_12_), channel_id=1, source_target_pairs={{0,8},{1,9},{2,10},{3,11},{4,12},{5,13},{6,14},{7,15},{8,0},{9,1},... | collective-permute-start | bytes 1572872 | tf_op jit(solution)/shard_map/ppermute | solution.py:415
  47.4 1.7 %query_work.1.work_ref = s32[133]{0:T(256)S(1)} custom-call(s32[8,128]{1,0:T(8,128)S(1)} %bitcast.11), custom_call_target="tpu_custom_call" | custom-call | flops 200000000 | bytes 4000000 | tf_op jit(solution)/shard_map/query_work/pallas_call | solution.py:469
  49.1 0.0 copy-start.14
  49.1 0.0 collective-permute-done.16.refs_7_
  49.3 5.6 %forward.1 = (bf16[128,512]{1,0:T(8,128)(2,1)}, f32[32,16,128]{2,1,0:T(8,128)}) custom-call(s32[133]{0:T(256)S(1)} %query_work.1.work_ref, bf16[4,128,256]{2,1,0:T(8,128)(2,1)S(1)} %copy-done.13, bf16[128,512]{1,0:T(8,128)(2,1)S(1)} %copy-done.12, bf16[512,512]{1,0:T(8,128)(2,1)S(1)} %copy-done.2, bf16[512,512]{1,0:T(8,128)(2,1)S(1)} %copy-done.10, ...), custom_call_target="tpu_custom_call" | custom-call | flops 1000000000 | bytes 4000000 | tf_op jit(solution)/shard_map/forward/pallas_call | solution.py:538
  55.0 2.6 %all-to-all-start = ((f32[32,16,128]{2,1,0:T(8,128)}), f32[32,16,128]{2,1,0:T(8,128)S(1)}, u32[]{:S(2)}, u32[]{:S(2)}) async-start(f32[32,16,128]{2,1,0:T(8,128)} %get-tuple-element.35.stats_hbm), calls=%async_computation | async-start | bytes 524288 | tf_op jit(solution)/shard_map/all_to_all | solution.py:549
  57.6 0.2 collective-permute-start.20
  57.8 0.4 collective-permute-start.23
  58.2 6.7 %query_grad.1.part_hbm = f32[128,512]{1,0:T(8,128)} custom-call(s32[133]{0:T(256)} %copy-done.14, bf16[4,128,256]{2,1,0:T(8,128)(2,1)} %get-tuple-element.28.stack_ref.stack_hbm, bf16[4,128,256]{2,1,0:T(8,128)(2,1)} %get-tuple-element.34.cot_stack_hbm, f32[32,16,128]{2,1,0:T(8,128)} %get-tuple-element.35.stats_hbm, ...), custom_call_target="tpu_custom_call" | custom-call | flops 1000000000 | bytes 4000000 | tf_op jit(solution)/shard_map/query_grad/pallas_call | solution.py:551
  64.9 0.0 collective-permute-done.19.refs_9_
  64.9 3.1 %all-to-all-done.stats_all_ref = f32[32,16,128]{2,1,0:T(8,128)S(1)} async-done(((f32[32,16,128]{2,1,0:T(8,128)}), f32[32,16,128]{2,1,0:T(8,128)S(1)}, u32[]{:S(2)}, u32[]{:S(2)}) %all-to-all-start) | async-done | bytes 262176 | tf_op jit(solution)/shard_map/all_to_all | solution.py:549
  68.0 0.4 collective-permute-start.21
  68.3 0.1 collective-permute-start.24
  68.5 0.0 collective-permute-done.20.refs_10_
  68.5 0.0 collective-permute-done.23.refs_14_
  68.5 1.4 %collective-permute-done.21.refs_11_ = bf16[8,64,512]{2,1,0:T(8,128)(2,1)S(1)} collective-permute-done((bf16[8,64,512]{2,1,0:T(8,128)(2,1)S(1)}, bf16[8,64,512]{2,1,0:T(8,128)(2,1)S(1)}, u32[]{:S(2)}, u32[]{:S(2)}) %collective-permute-start.21) | collective-permute-done | bytes 524320 | tf_op jit(solution)/shard_map/ppermute | solution.py:415
  69.9 0.7 collective-permute-done.24.refs_15_
  70.7 0.0 copy-done.24
  70.7 0.8 %copy-done.25 = bf16[8,64,512]{2,1,0:T(8,128)(2,1)} copy-done((bf16[8,64,512]{2,1,0:T(8,128)(2,1)}, bf16[8,64,512]{2,1,0:T(8,128)(2,1)S(1)}, u32[]{:S(2)}) %copy-start.25) | copy-done | bytes 524312
  71.5 4.6 %key_grad.1 = bf16[128,512]{1,0:T(8,128)(2,1)} custom-call(s32[69]{0:T(128)} %copy-done.15, bf16[128,512]{1,0:T(8,128)(2,1)} %get-tuple-element.31.key_hbm, bf16[128,512]{1,0:T(8,128)(2,1)} %get-tuple-element.32.value_hbm, bf16[512,512]{1,0:T(8,128)(2,1)} %wq_hbm.3, bf16[512,512]{1,0:T(8,128)(2,1)} %get-tuple-element.33.wkt_hbm, ...), custom_call_target="tpu_custom_call" | custom-call | flops 1000000000 | bytes 4000000 | tf_op jit(solution)/shard_map/key_grad/pallas_call | solution.py:570
  (71 shorter events, 0.3 us)
Async XLA Ops:
  1.3 7.4 %copy-start.11 = (bf16[128,512]{1,0:T(8,128)(2,1)S(1)}, bf16[128,512]{1,0:T(8,128)(2,1)}, u32[]{:S(2)}) copy-start(bf16[128,512]{1,0:T(8,128)(2,1)} %cot_ref.1) | copy-start | bytes 393220
  2.9 9.0 %copy-start.19 = (bf16[1,144,512]{2,1,0:T(8,128)(2,1)S(1)}, bf16[1,144,512]{2,1,0:T(8,128)(2,1)}, u32[]{:S(2)}) copy-start(bf16[1,144,512]{2,1,0:T(8,128)(2,1)} %pack.1) | copy-start | bytes 442372
  2.9 13.2 %collective-permute-start.2 = (bf16[1,144,512]{2,1,0:T(8,128)(2,1)}, bf16[1,144,512]{2,1,0:T(8,128)(2,1)S(1)}, u32[]{:S(2)}, u32[]{:S(2)}) collective-permute-start(bf16[1,144,512]{2,1,0:T(8,128)(2,1)} %pack.1), channel_id=1, source_target_pairs={{0,6},{1,7},{2,4},{3,5},{4,2},{5,3},{6,0},{7,1},{8,14},{9,15},{10,... | collective-permute-start | bytes 442376 | tf_op jit(solution)/shard_map/ppermute | solution.py:415
  8.1 12.7 %collective-permute-start.1 = (bf16[1,144,512]{2,1,0:T(8,128)(2,1)}, bf16[1,144,512]{2,1,0:T(8,128)(2,1)S(1)}, u32[]{:S(2)}, u32[]{:S(2)}) collective-permute-start(bf16[1,144,512]{2,1,0:T(8,128)(2,1)} %pack.1), channel_id=1, source_target_pairs={{0,4},{1,5},{2,6},{3,7},{4,0},{5,1},{6,2},{7,3},{8,12},{9,13},{10,... | collective-permute-start | bytes 442376 | tf_op jit(solution)/shard_map/ppermute | solution.py:415
  8.1 12.7 %collective-permute-start = (bf16[1,144,512]{2,1,0:T(8,128)(2,1)}, bf16[1,144,512]{2,1,0:T(8,128)(2,1)S(1)}, u32[]{:S(2)}, u32[]{:S(2)}) collective-permute-start(bf16[1,144,512]{2,1,0:T(8,128)(2,1)} %pack.1), channel_id=1, source_target_pairs={{0,2},{1,3},{2,0},{3,1},{4,6},{5,7},{6,4},{7,5},{8,10},{9,11},{10,... | collective-permute-start | bytes 442376 | tf_op jit(solution)/shard_map/ppermute | solution.py:415
  8.7 4.3 %collective-permute-start.7 = (bf16[1,64,512]{2,1,0:T(8,128)(2,1)S(1)}, bf16[1,64,512]{2,1,0:T(8,128)(2,1)S(1)}, u32[]{:S(2)}, u32[]{:S(2)}) collective-permute-start(bf16[1,64,512]{2,1,0:T(8,128)(2,1)S(1)} %get-tuple-element.52), channel_id=1, source_target_pairs={{0,16},{1,17},{2,18},{3,19},{4,20},{5,21},{6,22},{7,23},{8,24},{9,... | collective-permute-start | bytes 196616 | tf_op jit(solution)/shard_map/ppermute | solution.py:415
  10.4 5.2 %collective-permute-start.6 = (bf16[1,64,512]{2,1,0:T(8,128)(2,1)S(1)}, bf16[1,64,512]{2,1,0:T(8,128)(2,1)S(1)}, u32[]{:S(2)}, u32[]{:S(2)}) collective-permute-start(bf16[1,64,512]{2,1,0:T(8,128)(2,1)S(1)} %get-tuple-element.53), channel_id=1, source_target_pairs={{0,8},{1,9},{2,10},{3,11},{4,12},{5,13},{6,14},{7,15},{8,0},{9,1},... | collective-permute-start | bytes 196616 | tf_op jit(solution)/shard_map/ppermute | solution.py:415
  13.0 7.7 %collective-permute-start.5 = (bf16[1,144,512]{2,1,0:T(8,128)(2,1)S(1)}, bf16[1,144,512]{2,1,0:T(8,128)(2,1)S(1)}, u32[]{:S(2)}, u32[]{:S(2)}) collective-permute-start(bf16[1,144,512]{2,1,0:T(8,128)(2,1)S(1)} %copy-done.19), channel_id=1, source_target_pairs={{0,24},{1,25},{2,26},{3,27},{4,28},{5,29},{6,30},{7,31},{8,16},{9,... | collective-permute-start | bytes 442376 | tf_op jit(solution)/shard_map/ppermute | solution.py:415
  15.6 5.9 %collective-permute-start.4 = (bf16[1,144,512]{2,1,0:T(8,128)(2,1)S(1)}, bf16[1,144,512]{2,1,0:T(8,128)(2,1)S(1)}, u32[]{:S(2)}, u32[]{:S(2)}) collective-permute-start(bf16[1,144,512]{2,1,0:T(8,128)(2,1)S(1)} %copy-done.19), channel_id=1, source_target_pairs={{0,16},{1,17},{2,18},{3,19},{4,20},{5,21},{6,22},{7,23},{8,24},{9,... | collective-permute-start | bytes 442376 | tf_op jit(solution)/shard_map/ppermute | solution.py:415
  16.1 5.4 %collective-permute-start.3 = (bf16[1,144,512]{2,1,0:T(8,128)(2,1)S(1)}, bf16[1,144,512]{2,1,0:T(8,128)(2,1)S(1)}, u32[]{:S(2)}, u32[]{:S(2)}) collective-permute-start(bf16[1,144,512]{2,1,0:T(8,128)(2,1)S(1)} %copy-done.19), channel_id=1, source_target_pairs={{0,8},{1,9},{2,10},{3,11},{4,12},{5,13},{6,14},{7,15},{8,0},{9,1},... | collective-permute-start | bytes 442376 | tf_op jit(solution)/shard_map/ppermute | solution.py:415
  21.5 13.7 %collective-permute-start.17 = (bf16[4,64,512]{2,1,0:T(8,128)(2,1)S(1)}, bf16[4,64,512]{2,1,0:T(8,128)(2,1)S(1)}, u32[]{:S(2)}, u32[]{:S(2)}) collective-permute-start(bf16[4,64,512]{2,1,0:T(8,128)(2,1)S(1)} %pad_maximum_fusion.4), channel_id=1, source_target_pairs={{0,4},{1,5},{2,6},{3,7},{4,0},{5,1},{6,2},{7,3},{8,12},{9,13},{10,... | collective-permute-start | bytes 786440 | tf_op jit(solution)/shard_map/ppermute | solution.py:415
  25.6 9.7 %collective-permute-start.8 = (bf16[4,64,512]{2,1,0:T(8,128)(2,1)S(1)}, bf16[4,64,512]{2,1,0:T(8,128)(2,1)S(1)}, u32[]{:S(2)}, u32[]{:S(2)}) collective-permute-start(bf16[4,64,512]{2,1,0:T(8,128)(2,1)S(1)} %pad_maximum_fusion.4), channel_id=1, source_target_pairs={{0,2},{1,3},{2,0},{3,1},{4,6},{5,7},{6,4},{7,5},{8,10},{9,11},{10,... | collective-permute-start | bytes 786440 | tf_op jit(solution)/shard_map/ppermute | solution.py:415
  25.8 12.8 %collective-permute-start.13 = (bf16[3,128,512]{2,1,0:T(8,128)(2,1)S(1)}, bf16[3,128,512]{2,1,0:T(8,128)(2,1)S(1)}, u32[]{:S(2)}, u32[]{:S(2)}) collective-permute-start(bf16[3,128,512]{2,1,0:T(8,128)(2,1)S(1)} %pad_maximum_fusion.2), channel_id=1, source_target_pairs={{0,24},{1,25},{2,26},{3,27},{4,28},{5,29},{6,30},{7,31},{8,16},{9,... | collective-permute-start | bytes 1179656 | tf_op jit(solution)/shard_map/ppermute | solution.py:415
  28.0 14.7 %collective-permute-start.12 = (bf16[3,128,512]{2,1,0:T(8,128)(2,1)S(1)}, bf16[3,128,512]{2,1,0:T(8,128)(2,1)S(1)}, u32[]{:S(2)}, u32[]{:S(2)}) collective-permute-start(bf16[3,128,512]{2,1,0:T(8,128)(2,1)S(1)} %pad_maximum_fusion.2), channel_id=1, source_target_pairs={{0,16},{1,17},{2,18},{3,19},{4,20},{5,21},{6,22},{7,23},{8,24},{9,... | collective-permute-start | bytes 1179656 | tf_op jit(solution)/shard_map/ppermute | solution.py:415
  28.5 14.9 %collective-permute-start.11 = (bf16[3,128,512]{2,1,0:T(8,128)(2,1)S(1)}, bf16[3,128,512]{2,1,0:T(8,128)(2,1)S(1)}, u32[]{:S(2)}, u32[]{:S(2)}) collective-permute-start(bf16[3,128,512]{2,1,0:T(8,128)(2,1)S(1)} %pad_maximum_fusion.2), channel_id=1, source_target_pairs={{0,8},{1,9},{2,10},{3,11},{4,12},{5,13},{6,14},{7,15},{8,0},{9,1},... | collective-permute-start | bytes 1179656 | tf_op jit(solution)/shard_map/ppermute | solution.py:415
  34.1 0.5 copy-start.15
  34.6 14.6 %copy-start = (bf16[7,128,512]{2,1,0:T(8,128)(2,1)}, bf16[7,128,512]{2,1,0:T(8,128)(2,1)S(1)}, u32[]{:S(2)}) copy-start(bf16[7,128,512]{2,1,0:T(8,128)(2,1)S(1)} %constant_dynamic-update-slice_fusion.refs_0_) | copy-start | bytes 2752516
  35.2 8.9 %collective-permute-start.9 = (bf16[7,128,512]{2,1,0:T(8,128)(2,1)S(1)}, bf16[7,128,512]{2,1,0:T(8,128)(2,1)S(1)}, u32[]{:S(2)}, u32[]{:S(2)}) collective-permute-start(bf16[7,128,512]{2,1,0:T(8,128)(2,1)S(1)} %constant_dynamic-update-slice_fusion.refs_0_), channel_id=1, source_target_pairs={{0,1},{1,0},{2,3},{3,2},{4,5},{5,4},{6,7},{7,6},{8,9},{9,8},{10,11... | collective-permute-start | bytes 2752520 | tf_op jit(solution)/shard_map/ppermute | solution.py:415
  35.3 8.8 %collective-permute-start.18 = (bf16[4,64,512]{2,1,0:T(8,128)(2,1)S(1)}, bf16[4,64,512]{2,1,0:T(8,128)(2,1)S(1)}, u32[]{:S(2)}, u32[]{:S(2)}) collective-permute-start(bf16[4,64,512]{2,1,0:T(8,128)(2,1)S(1)} %collective-permute-done.17), channel_id=1, source_target_pairs={{0,2},{1,3},{2,0},{3,1},{4,6},{5,7},{6,4},{7,5},{8,10},{9,11},{10,... | collective-permute-start | bytes 786440 | tf_op jit(solution)/shard_map/ppermute | solution.py:415
  38.6 10.6 %copy-start.4 = (bf16[3,128,512]{2,1,0:T(8,128)(2,1)}, bf16[3,128,512]{2,1,0:T(8,128)(2,1)S(1)}, u32[]{:S(2)}) copy-start(bf16[3,128,512]{2,1,0:T(8,128)(2,1)S(1)} %collective-permute-done.13.refs_3_) | copy-start | bytes 1179652
  38.6 10.6 %collective-permute-start.16 = (bf16[3,128,512]{2,1,0:T(8,128)(2,1)S(1)}, bf16[3,128,512]{2,1,0:T(8,128)(2,1)S(1)}, u32[]{:S(2)}, u32[]{:S(2)}) collective-permute-start(bf16[3,128,512]{2,1,0:T(8,128)(2,1)S(1)} %collective-permute-done.13.refs_3_), channel_id=1, source_target_pairs={{0,1},{1,0},{2,3},{3,2},{4,5},{5,4},{6,7},{7,6},{8,9},{9,8},{10,11... | collective-permute-start | bytes 1179656 | tf_op jit(solution)/shard_map/ppermute | solution.py:415
  42.7 6.5 %copy-start.5 = (bf16[3,128,512]{2,1,0:T(8,128)(2,1)}, bf16[3,128,512]{2,1,0:T(8,128)(2,1)S(1)}, u32[]{:S(2)}) copy-start(bf16[3,128,512]{2,1,0:T(8,128)(2,1)S(1)} %collective-permute-done.12.refs_2_) | copy-start | bytes 1179652
  42.7 6.4 %collective-permute-start.15 = (bf16[3,128,512]{2,1,0:T(8,128)(2,1)S(1)}, bf16[3,128,512]{2,1,0:T(8,128)(2,1)S(1)}, u32[]{:S(2)}, u32[]{:S(2)}) collective-permute-start(bf16[3,128,512]{2,1,0:T(8,128)(2,1)S(1)} %collective-permute-done.12.refs_2_), channel_id=1, source_target_pairs={{0,1},{1,0},{2,3},{3,2},{4,5},{5,4},{6,7},{7,6},{8,9},{9,8},{10,11... | collective-permute-start | bytes 1179656 | tf_op jit(solution)/shard_map/ppermute | solution.py:415
  43.5 5.8 %copy-start.6 = (bf16[3,128,512]{2,1,0:T(8,128)(2,1)}, bf16[3,128,512]{2,1,0:T(8,128)(2,1)S(1)}, u32[]{:S(2)}) copy-start(bf16[3,128,512]{2,1,0:T(8,128)(2,1)S(1)} %collective-permute-done.11.refs_1_) | copy-start | bytes 1179652
  43.5 5.7 %collective-permute-start.14 = (bf16[3,128,512]{2,1,0:T(8,128)(2,1)S(1)}, bf16[3,128,512]{2,1,0:T(8,128)(2,1)S(1)}, u32[]{:S(2)}, u32[]{:S(2)}) collective-permute-start(bf16[3,128,512]{2,1,0:T(8,128)(2,1)S(1)} %collective-permute-done.11.refs_1_), channel_id=1, source_target_pairs={{0,1},{1,0},{2,3},{3,2},{4,5},{5,4},{6,7},{7,6},{8,9},{9,8},{10,11... | collective-permute-start | bytes 1179656 | tf_op jit(solution)/shard_map/ppermute | solution.py:415
  44.1 5.2 %copy-start.13 = (bf16[4,128,256]{2,1,0:T(8,128)(2,1)S(1)}, bf16[4,128,256]{2,1,0:T(8,128)(2,1)}, u32[]{:S(2)}) copy-start(bf16[4,128,256]{2,1,0:T(8,128)(2,1)} %get-tuple-element.28.stack_ref.stack_hbm) | copy-start | bytes 786436
  44.2 13.6 %copy-start.16 = (bf16[8,64,512]{2,1,0:T(8,128)(2,1)}, bf16[8,64,512]{2,1,0:T(8,128)(2,1)S(1)}, u32[]{:S(2)}) copy-start(bf16[8,64,512]{2,1,0:T(8,128)(2,1)S(1)} %pad_maximum_fusion.1.refs_12_) | copy-start | bytes 1572868
  44.2 5.1 %copy-start.1 = (bf16[7,128,512]{2,1,0:T(8,128)(2,1)}, bf16[7,128,512]{2,1,0:T(8,128)(2,1)S(1)}, u32[]{:S(2)}) copy-start(bf16[7,128,512]{2,1,0:T(8,128)(2,1)S(1)} %collective-permute-done.9.refs_4_) | copy-start | bytes 2752516
  44.2 1.7 %collective-permute-start.10 = (bf16[4,16,128]{2,1,0:T(8,128)(2,1)S(1)}, bf16[4,16,128]{2,1,0:T(8,128)(2,1)S(1)}, u32[]{:S(2)}, u32[]{:S(2)}) collective-permute-start(bf16[4,16,128]{2,1,0:T(8,128)(2,1)S(1)} %pad_maximum_fusion.5), channel_id=1, source_target_pairs={{0,1},{1,0},{2,3},{3,2},{4,5},{5,4},{6,7},{7,6},{8,9},{9,8},{10,11... | collective-permute-start | bytes 49160 | tf_op jit(solution)/shard_map/ppermute | solution.py:415
  44.3 5.0 %copy-start.3 = (s32[240,128,4]{1,2,0:T(4,128)S(1)}, s32[240,128,4]{1,2,0:T(4,128)}, u32[]{:S(2)}) copy-start(s32[240,128,4]{1,2,0:T(4,128)} %param.15) | copy-start | bytes 1474564
  44.3 5.0 %copy-start.10 = (bf16[512,512]{1,0:T(8,128)(2,1)S(1)}, bf16[512,512]{1,0:T(8,128)(2,1)}, u32[]{:S(2)}) copy-start(bf16[512,512]{1,0:T(8,128)(2,1)} %get-tuple-element.29.wvt_ref.wvt_hbm) | copy-start | bytes 1572868
  44.4 13.2 %copy-start.17 = (bf16[8,64,512]{2,1,0:T(8,128)(2,1)}, bf16[8,64,512]{2,1,0:T(8,128)(2,1)S(1)}, u32[]{:S(2)}) copy-start(bf16[8,64,512]{2,1,0:T(8,128)(2,1)S(1)} %pad_maximum_fusion.refs_8_) | copy-start | bytes 1572868
  44.4 4.9 %copy-start.2 = (bf16[512,512]{1,0:T(8,128)(2,1)S(1)}, bf16[512,512]{1,0:T(8,128)(2,1)}, u32[]{:S(2)}) copy-start(bf16[512,512]{1,0:T(8,128)(2,1)} %wk_hbm.3) | copy-start | bytes 1572868
  44.4 20.5 %collective-permute-start.19 = (bf16[8,64,512]{2,1,0:T(8,128)(2,1)S(1)}, bf16[8,64,512]{2,1,0:T(8,128)(2,1)S(1)}, u32[]{:S(2)}, u32[]{:S(2)}) collective-permute-start(bf16[8,64,512]{2,1,0:T(8,128)(2,1)S(1)} %pad_maximum_fusion.refs_8_), channel_id=1, source_target_pairs={{0,16},{1,17},{2,18},{3,19},{4,20},{5,21},{6,22},{7,23},{8,24},{9,... | collective-permute-start | bytes 1572872 | tf_op jit(solution)/shard_map/ppermute | solution.py:415
  45.9 22.4 %collective-permute-start.22 = (bf16[8,64,512]{2,1,0:T(8,128)(2,1)S(1)}, bf16[8,64,512]{2,1,0:T(8,128)(2,1)S(1)}, u32[]{:S(2)}, u32[]{:S(2)}) collective-permute-start(bf16[8,64,512]{2,1,0:T(8,128)(2,1)S(1)} %pad_maximum_fusion.1.refs_12_), channel_id=1, source_target_pairs={{0,8},{1,9},{2,10},{3,11},{4,12},{5,13},{6,14},{7,15},{8,0},{9,1},... | collective-permute-start | bytes 1572872 | tf_op jit(solution)/shard_map/ppermute | solution.py:415
  47.4 1.9 %copy-start.12 = (bf16[128,512]{1,0:T(8,128)(2,1)S(1)}, bf16[128,512]{1,0:T(8,128)(2,1)}, u32[]{:S(2)}) copy-start(bf16[128,512]{1,0:T(8,128)(2,1)} %cot_ref.1) | copy-start | bytes 393220
  49.1 5.8 %copy-start.14 = (s32[133]{0:T(256)}, s32[133]{0:T(256)S(1)}, u32[]{:S(2)}) copy-start(s32[133]{0:T(256)S(1)} %query_work.1.work_ref) | copy-start | bytes 1600
  49.2 5.8 %copy-start.7 = (bf16[3,128,512]{2,1,0:T(8,128)(2,1)}, bf16[3,128,512]{2,1,0:T(8,128)(2,1)S(1)}, u32[]{:S(2)}) copy-start(bf16[3,128,512]{2,1,0:T(8,128)(2,1)S(1)} %collective-permute-done.16.refs_7_) | copy-start | bytes 1179652
  49.2 5.8 %copy-start.8 = (bf16[3,128,512]{2,1,0:T(8,128)(2,1)}, bf16[3,128,512]{2,1,0:T(8,128)(2,1)S(1)}, u32[]{:S(2)}) copy-start(bf16[3,128,512]{2,1,0:T(8,128)(2,1)S(1)} %collective-permute-done.15.refs_6_) | copy-start | bytes 1179652
  49.2 5.8 %copy-start.9 = (bf16[3,128,512]{2,1,0:T(8,128)(2,1)}, bf16[3,128,512]{2,1,0:T(8,128)(2,1)S(1)}, u32[]{:S(2)}) copy-start(bf16[3,128,512]{2,1,0:T(8,128)(2,1)S(1)} %collective-permute-done.14.refs_5_) | copy-start | bytes 1179652
  55.0 13.0 %all-to-all-start = ((f32[32,16,128]{2,1,0:T(8,128)}), f32[32,16,128]{2,1,0:T(8,128)S(1)}, u32[]{:S(2)}, u32[]{:S(2)}) async-start(f32[32,16,128]{2,1,0:T(8,128)} %get-tuple-element.35.stats_hbm), calls=%async_computation | async-start | bytes 524288 | tf_op jit(solution)/shard_map/all_to_all | solution.py:549
  57.6 10.9 %collective-permute-start.20 = (bf16[8,64,512]{2,1,0:T(8,128)(2,1)S(1)}, bf16[8,64,512]{2,1,0:T(8,128)(2,1)S(1)}, u32[]{:S(2)}, u32[]{:S(2)}) collective-permute-start(bf16[8,64,512]{2,1,0:T(8,128)(2,1)S(1)} %pad_maximum_fusion.refs_8_), channel_id=1, source_target_pairs={{0,1},{1,0},{2,3},{3,2},{4,5},{5,4},{6,7},{7,6},{8,9},{9,8},{10,11... | collective-permute-start | bytes 1572872 | tf_op jit(solution)/shard_map/ppermute | solution.py:415
  57.8 10.7 %collective-permute-start.23 = (bf16[8,64,512]{2,1,0:T(8,128)(2,1)S(1)}, bf16[8,64,512]{2,1,0:T(8,128)(2,1)S(1)}, u32[]{:S(2)}, u32[]{:S(2)}) collective-permute-start(bf16[8,64,512]{2,1,0:T(8,128)(2,1)S(1)} %pad_maximum_fusion.1.refs_12_), channel_id=1, source_target_pairs={{0,1},{1,0},{2,3},{3,2},{4,5},{5,4},{6,7},{7,6},{8,9},{9,8},{10,11... | collective-permute-start | bytes 1572872 | tf_op jit(solution)/shard_map/ppermute | solution.py:415
  64.9 5.8 %copy-start.20 = (bf16[8,64,512]{2,1,0:T(8,128)(2,1)}, bf16[8,64,512]{2,1,0:T(8,128)(2,1)S(1)}, u32[]{:S(2)}) copy-start(bf16[8,64,512]{2,1,0:T(8,128)(2,1)S(1)} %collective-permute-done.19.refs_9_) | copy-start | bytes 1572868
  68.0 2.7 %copy-start.18 = (f32[32,16,128]{2,1,0:T(8,128)}, f32[32,16,128]{2,1,0:T(8,128)S(1)}, u32[]{:S(2)}) copy-start(f32[32,16,128]{2,1,0:T(8,128)S(1)} %all-to-all-done.stats_all_ref) | copy-start | bytes 786436
  68.0 1.9 %collective-permute-start.21 = (bf16[8,64,512]{2,1,0:T(8,128)(2,1)S(1)}, bf16[8,64,512]{2,1,0:T(8,128)(2,1)S(1)}, u32[]{:S(2)}, u32[]{:S(2)}) collective-permute-start(bf16[8,64,512]{2,1,0:T(8,128)(2,1)S(1)} %collective-permute-done.19.refs_9_), channel_id=1, source_target_pairs={{0,1},{1,0},{2,3},{3,2},{4,5},{5,4},{6,7},{7,6},{8,9},{9,8},{10,11... | collective-permute-start | bytes 1572872 | tf_op jit(solution)/shard_map/ppermute | solution.py:415
  68.3 2.3 %copy-start.21 = (bf16[8,64,512]{2,1,0:T(8,128)(2,1)}, bf16[8,64,512]{2,1,0:T(8,128)(2,1)S(1)}, u32[]{:S(2)}) copy-start(bf16[8,64,512]{2,1,0:T(8,128)(2,1)S(1)} %collective-permute-done.22.refs_13_) | copy-start | bytes 1572868
  68.3 2.3 %collective-permute-start.24 = (bf16[8,64,512]{2,1,0:T(8,128)(2,1)S(1)}, bf16[8,64,512]{2,1,0:T(8,128)(2,1)S(1)}, u32[]{:S(2)}, u32[]{:S(2)}) collective-permute-start(bf16[8,64,512]{2,1,0:T(8,128)(2,1)S(1)} %collective-permute-done.22.refs_13_), channel_id=1, source_target_pairs={{0,1},{1,0},{2,3},{3,2},{4,5},{5,4},{6,7},{7,6},{8,9},{9,8},{10,11... | collective-permute-start | bytes 1572872 | tf_op jit(solution)/shard_map/ppermute | solution.py:415
  68.5 2.2 %copy-start.22 = (bf16[8,64,512]{2,1,0:T(8,128)(2,1)}, bf16[8,64,512]{2,1,0:T(8,128)(2,1)S(1)}, u32[]{:S(2)}) copy-start(bf16[8,64,512]{2,1,0:T(8,128)(2,1)S(1)} %collective-permute-done.20.refs_10_) | copy-start | bytes 1572868
  68.5 2.2 %copy-start.23 = (bf16[8,64,512]{2,1,0:T(8,128)(2,1)}, bf16[8,64,512]{2,1,0:T(8,128)(2,1)S(1)}, u32[]{:S(2)}) copy-start(bf16[8,64,512]{2,1,0:T(8,128)(2,1)S(1)} %collective-permute-done.23.refs_14_) | copy-start | bytes 1572868
  69.9 0.8 %copy-start.24 = (bf16[8,64,512]{2,1,0:T(8,128)(2,1)}, bf16[8,64,512]{2,1,0:T(8,128)(2,1)S(1)}, u32[]{:S(2)}) copy-start(bf16[8,64,512]{2,1,0:T(8,128)(2,1)S(1)} %collective-permute-done.21.refs_11_) | copy-start | bytes 1572868
  70.7 0.8 %copy-start.25 = (bf16[8,64,512]{2,1,0:T(8,128)(2,1)}, bf16[8,64,512]{2,1,0:T(8,128)(2,1)S(1)}, u32[]{:S(2)}) copy-start(bf16[8,64,512]{2,1,0:T(8,128)(2,1)S(1)} %collective-permute-done.24.refs_15_) | copy-start | bytes 1572868

commit v5 on v4

--- a/solution.py
+++ b/solution.py
@@ -511,7 +511,7 @@
 
     line_lists = jnp.concatenate([entry[:, block:, :128] for entry in lined], 0)
     other_near = swap(after(near, pieces[lines // 2]), 1)
-    line_lists = after(line_lists, other_near)
+    line_lists = after(line_lists, pieces[1])
     row_lists = jnp.concatenate([line_lists, swap(line_lists, 1)], 0)
     query_work = work(query_work_kernel, row_lists, blks, "query_work")
     here = [near] + there

time: 76.6 us -> 77.7 us (1.014)
  the two profiles are of different devices: /device:TPU:0 before, /device:TPU:1 now
where the time goes in v5:
time: 77.7 us; the launch traced here: 77.3 us
  starting transfers between devices  27 us (35%)
  Pallas kernels  23.9 us (31%)
  waiting for transfers between devices  22.8 us (29%)
  between operations  1.82 us (2%)
  local copies, waits for them, and re-layouts  1.59 us (2%)
    ppermute x25, starting transfers between devices, swap(): return lax.ppermute(block, axes, [(i, i ^ mask) for i in range(count)])  21.7 us
    ppermute x25, waiting for transfers between devices, swap(): return lax.ppermute(block, axes, [(i, i ^ mask) for i in range(count)])  18.3 us
    pallas_call x1, Pallas kernels, local(): pl.pallas_call(functools.partial(key_grad_kernel, sizes, bits), out_shape...  5.79 us
    pallas_call x1, Pallas kernels, local(): pl.pallas_call(functools.partial(query_grad_kernel, sizes), out_shape=sha...  5.54 us
    all_to_all x1, starting transfers between devices, local(): stats_all = lax.all_to_all(stats, axes, 0, 0, tiled=True)  5.29 us
    all_to_all x1, waiting for transfers between devices, local(): stats_all = lax.all_to_all(stats, axes, 0, 0, tiled=True)  4.51 us
    pallas_call x1, Pallas kernels, local(): pl.pallas_call(functools.partial(forward_kernel, sizes), out_shape=(own,...  4.25 us
    pallas_call x1, Pallas kernels, local(): pl.pallas_call(prepare_kernel, out_shape=(stacks, stacks, own, own, squar...  3.54 us
  transfers between devices with their start and end apart: 26, of which 9 were waited for; matrix products, arithmetic and copies ran while one was open for 1% of the time, Pallas kernels for 21%

profile of v5, /device:TPU:1, one launch (start us, length us, event | category | flops | bytes accessed | tf_op | source)
XLA Modules:
  0.0 77.3 jit_solution(9124530562464624208)
XLA Ops:
  1.3 0.0 copy-start.11
  1.3 1.6 %pack.1 = bf16[1,144,512]{2,1,0:T(8,128)(2,1)} custom-call(bf16[128,512]{1,0:T(8,128)(2,1)} %own_hbm.2, s32[1,3,1,8]{3,2,1,0:T(1,128)} %bitcast.13, s32[1,1]{1,0:T(1,128)S(6)} %copy.14.count_hbm), custom_call_target="tpu_custom_call" | custom-call | tf_op jit(solution)/shard_map/pack/pallas_call | solution.py:441
  2.9 4.2 %collective-permute-start.2 = (bf16[1,144,512]{2,1,0:T(8,128)(2,1)}, bf16[1,144,512]{2,1,0:T(8,128)(2,1)S(1)}, u32[]{:S(2)}, u32[]{:S(2)}) collective-permute-start(bf16[1,144,512]{2,1,0:T(8,128)(2,1)} %pack.1), channel_id=1, source_target_pairs={{0,6},{1,7},{2,4},{3,5},{4,2},{5,3},{6,0},{7,1},{8,14},{9,15},{10,... | collective-permute-start | bytes 442376 | tf_op jit(solution)/shard_map/ppermute | solution.py:415
  7.2 0.0 collective-permute-start.1
  7.2 0.4 collective-permute-start
  7.5 1.3 %collective-permute-start.3 = (bf16[1,64,512]{2,1,0:T(8,128)(2,1)S(1)}, bf16[1,64,512]{2,1,0:T(8,128)(2,1)S(1)}, u32[]{:S(2)}, u32[]{:S(2)}) collective-permute-start(bf16[1,64,512]{2,1,0:T(8,128)(2,1)S(1)} %get-tuple-element.52), channel_id=1, source_target_pairs={{0,8},{1,9},{2,10},{3,11},{4,12},{5,13},{6,14},{7,15},{8,0},{9,1},... | collective-permute-start | bytes 196616 | tf_op jit(solution)/shard_map/ppermute | solution.py:415
  8.8 1.2 %collective-permute-start.4 = (bf16[1,64,512]{2,1,0:T(8,128)(2,1)S(1)}, bf16[1,64,512]{2,1,0:T(8,128)(2,1)S(1)}, u32[]{:S(2)}, u32[]{:S(2)}) collective-permute-start(bf16[1,64,512]{2,1,0:T(8,128)(2,1)S(1)} %get-tuple-element.53), channel_id=1, source_target_pairs={{0,16},{1,17},{2,18},{3,19},{4,20},{5,21},{6,22},{7,23},{8,24},{9,... | collective-permute-start | bytes 196616 | tf_op jit(solution)/shard_map/ppermute | solution.py:415
  10.1 0.9 %collective-permute-done.3 = bf16[1,64,512]{2,1,0:T(8,128)(2,1)S(1)} collective-permute-done((bf16[1,64,512]{2,1,0:T(8,128)(2,1)S(1)}, bf16[1,64,512]{2,1,0:T(8,128)(2,1)S(1)}, u32[]{:S(2)}, u32[]{:S(2)}) %collective-permute-start.3) | collective-permute-done | bytes 65568 | tf_op jit(solution)/shard_map/ppermute | solution.py:415
  11.0 2.2 %collective-permute-start.7 = (bf16[1,144,512]{2,1,0:T(8,128)(2,1)S(1)}, bf16[1,144,512]{2,1,0:T(8,128)(2,1)S(1)}, u32[]{:S(2)}, u32[]{:S(2)}) collective-permute-start(bf16[1,144,512]{2,1,0:T(8,128)(2,1)S(1)} %copy-done.19), channel_id=1, source_target_pairs={{0,24},{1,25},{2,26},{3,27},{4,28},{5,29},{6,30},{7,31},{8,16},{9,... | collective-permute-start | bytes 442376 | tf_op jit(solution)/shard_map/ppermute | solution.py:415
  13.2 0.0 collective-permute-done.4
  13.2 0.3 collective-permute-start.6
  13.5 0.0 collective-permute-done.2
  13.5 0.3 collective-permute-start.5
  13.8 5.7 %collective-permute-done.1 = bf16[1,144,512]{2,1,0:T(8,128)(2,1)S(1)} collective-permute-done((bf16[1,144,512]{2,1,0:T(8,128)(2,1)}, bf16[1,144,512]{2,1,0:T(8,128)(2,1)S(1)}, u32[]{:S(2)}, u32[]{:S(2)}) %collective-permute-start.1) | collective-permute-done | bytes 147488 | tf_op jit(solution)/shard_map/ppermute | solution.py:415
  19.4 0.0 collective-permute-done
  19.5 0.0 collective-permute-done.7
  19.5 0.0 collective-permute-done.6
  19.5 2.0 %collective-permute-start.13 = (bf16[4,64,512]{2,1,0:T(8,128)(2,1)S(1)}, bf16[4,64,512]{2,1,0:T(8,128)(2,1)S(1)}, u32[]{:S(2)}, u32[]{:S(2)}) collective-permute-start(bf16[4,64,512]{2,1,0:T(8,128)(2,1)S(1)} %pad_maximum_fusion.4), channel_id=1, source_target_pairs={{0,2},{1,3},{2,0},{3,1},{4,6},{5,7},{6,4},{7,5},{8,10},{9,11},{10,... | collective-permute-start | bytes 786440 | tf_op jit(solution)/shard_map/ppermute | solution.py:415
  21.5 0.4 collective-permute-start.8
  21.9 2.2 %collective-permute-start.12 = (bf16[3,128,512]{2,1,0:T(8,128)(2,1)S(1)}, bf16[3,128,512]{2,1,0:T(8,128)(2,1)S(1)}, u32[]{:S(2)}, u32[]{:S(2)}) collective-permute-start(bf16[3,128,512]{2,1,0:T(8,128)(2,1)S(1)} %pad_maximum_fusion.2), channel_id=1, source_target_pairs={{0,24},{1,25},{2,26},{3,27},{4,28},{5,29},{6,30},{7,31},{8,16},{9,... | collective-permute-start | bytes 1179656 | tf_op jit(solution)/shard_map/ppermute | solution.py:415
  24.1 0.2 collective-permute-start.11
  24.3 0.6 collective-permute-start.10
  25.1 3.5 %prepare.1 = (bf16[4,128,256]{2,1,0:T(8,128)(2,1)}, bf16[4,128,256]{2,1,0:T(8,128)(2,1)}, bf16[128,512]{1,0:T(8,128)(2,1)}, bf16[128,512]{1,0:T(8,128)(2,1)}, bf...) custom-call(bf16[128,512]{1,0:T(8,128)(2,1)} %own_hbm.2, bf16[128,512]{1,0:T(8,128)(2,1)} %cot_ref.1, ...), custom_call_target="tpu_custom_call" | custom-call | flops 400000000 | bytes 4000000 | tf_op jit(solution)/shard_map/prepare/pallas_call | solution.py:487
  28.6 1.4 %key_work.1.work_ref = s32[69]{0:T(128)S(1)} custom-call(s32[4,128]{1,0:T(4,128)S(1)} %bitcast.12), custom_call_target="tpu_custom_call" | custom-call | flops 200000000 | bytes 4000000 | tf_op jit(solution)/shard_map/key_work/pallas_call | solution.py:469
  30.1 0.5 copy-done.15
  30.5 5.1 %collective-permute-done.8 = bf16[4,64,512]{2,1,0:T(8,128)(2,1)S(1)} collective-permute-done((bf16[4,64,512]{2,1,0:T(8,128)(2,1)S(1)}, bf16[4,64,512]{2,1,0:T(8,128)(2,1)S(1)}, u32[]{:S(2)}, u32[]{:S(2)}) %collective-permute-start.8) | collective-permute-done | bytes 262176 | tf_op jit(solution)/shard_map/ppermute | solution.py:415
  35.6 1.2 %collective-permute-start.9 = (bf16[4,16,128]{2,1,0:T(8,128)(2,1)S(1)}, bf16[4,16,128]{2,1,0:T(8,128)(2,1)S(1)}, u32[]{:S(2)}, u32[]{:S(2)}) collective-permute-start(bf16[4,16,128]{2,1,0:T(8,128)(2,1)S(1)} %pad_maximum_fusion.5), channel_id=1, source_target_pairs={{0,1},{1,0},{2,3},{3,2},{4,5},{5,4},{6,7},{7,6},{8,9},{9,8},{10,11... | collective-permute-start | bytes 49160 | tf_op jit(solution)/shard_map/ppermute | solution.py:415
  36.8 0.0 collective-permute-done.13
  36.8 0.0 collective-permute-start.14
  36.8 0.8 %collective-permute-done.9 = bf16[4,16,128]{2,1,0:T(8,128)(2,1)S(1)} collective-permute-done((bf16[4,16,128]{2,1,0:T(8,128)(2,1)S(1)}, bf16[4,16,128]{2,1,0:T(8,128)(2,1)S(1)}, u32[]{:S(2)}, u32[]{:S(2)}) %collective-permute-start.9) | collective-permute-done | bytes 16416 | tf_op jit(solution)/shard_map/ppermute | solution.py:415
  37.6 0.0 collective-permute-start.18
  37.7 1.7 %query_work.1.work_ref = s32[133]{0:T(256)S(1)} custom-call(s32[8,128]{1,0:T(8,128)S(1)} %bitcast.11), custom_call_target="tpu_custom_call" | custom-call | flops 200000000 | bytes 4000000 | tf_op jit(solution)/shard_map/query_work/pallas_call | solution.py:469
  39.4 0.0 copy-start.14
  39.4 0.0 collective-permute-done.12.refs_3_
  39.4 0.4 collective-permute-start.17
  39.9 1.6 %collective-permute-done.11.refs_2_ = bf16[3,128,512]{2,1,0:T(8,128)(2,1)S(1)} collective-permute-done((bf16[3,128,512]{2,1,0:T(8,128)(2,1)S(1)}, bf16[3,128,512]{2,1,0:T(8,128)(2,1)S(1)}, u32[]{:S(2)}, u32[]{:S(2)}) %collective-permute-start.11) | collective-permute-done | bytes 393248 | tf_op jit(solution)/shard_map/ppermute | solution.py:415
  41.5 1.3 %collective-permute-start.16 = (bf16[3,128,512]{2,1,0:T(8,128)(2,1)S(1)}, bf16[3,128,512]{2,1,0:T(8,128)(2,1)S(1)}, u32[]{:S(2)}, u32[]{:S(2)}) collective-permute-start(bf16[3,128,512]{2,1,0:T(8,128)(2,1)S(1)} %collective-permute-done.11.refs_2_), channel_id=1, source_target_pairs={{0,1},{1,0},{2,3},{3,2},{4,5},{5,4},{6,7},{7,6},{8,9},{9,8},{10,11... | collective-permute-start | bytes 1179656 | tf_op jit(solution)/shard_map/ppermute | solution.py:415
  42.8 0.7 collective-permute-start.15
  43.4 1.7 %collective-permute-done.18 = bf16[4,64,512]{2,1,0:T(8,128)(2,1)S(1)} collective-permute-done((bf16[4,64,512]{2,1,0:T(8,128)(2,1)S(1)}, bf16[4,64,512]{2,1,0:T(8,128)(2,1)S(1)}, u32[]{:S(2)}, u32[]{:S(2)}) %collective-permute-start.18) | collective-permute-done | bytes 262176 | tf_op jit(solution)/shard_map/ppermute | solution.py:415
  45.2 0.0 copy-start.12
  45.2 0.1 pad_maximum_fusion.1.refs_12_
  45.3 0.0 copy-start.2
  45.3 0.0 copy-start.3
  45.3 0.1 pad_maximum_fusion.refs_8_
  45.4 0.7 collective-permute-start.19
  46.1 0.0 collective-permute-done.17.refs_7_
  46.1 1.2 %collective-permute-start.22 = (bf16[8,64,512]{2,1,0:T(8,128)(2,1)S(1)}, bf16[8,64,512]{2,1,0:T(8,128)(2,1)}, u32[]{:S(2)}, u32[]{:S(2)}) collective-permute-start(bf16[8,64,512]{2,1,0:T(8,128)(2,1)S(1)} %pad_maximum_fusion.1.refs_12_), channel_id=1, source_target_pairs={{0,8},{1,9},{2,10},{3,11},{4,12},{5,13},{6,14},{7,15},{8,0},{9,1},... | collective-permute-start | bytes 1572872 | tf_op jit(solution)/shard_map/ppermute | solution.py:415
  47.4 0.0 collective-permute-done.14.refs_4_
  47.5 4.3 %forward.1 = (bf16[128,512]{1,0:T(8,128)(2,1)}, f32[32,16,128]{2,1,0:T(8,128)}) custom-call(s32[133]{0:T(256)S(1)} %query_work.1.work_ref, bf16[4,128,256]{2,1,0:T(8,128)(2,1)S(1)} %copy-done.13, bf16[128,512]{1,0:T(8,128)(2,1)S(1)} %copy-done.12, bf16[512,512]{1,0:T(8,128)(2,1)S(1)} %copy-done.2, bf16[512,512]{1,0:T(8,128)(2,1)S(1)} %copy-done.10, ...), custom_call_target="tpu_custom_call" | custom-call | flops 1000000000 | bytes 4000000 | tf_op jit(solution)/shard_map/forward/pallas_call | solution.py:538
  51.8 5.3 %all-to-all-start = ((f32[32,16,128]{2,1,0:T(8,128)}), f32[32,16,128]{2,1,0:T(8,128)S(1)}, u32[]{:S(2)}, u32[]{:S(2)}) async-start(f32[32,16,128]{2,1,0:T(8,128)} %get-tuple-element.35.stats_hbm), calls=%async_computation | async-start | bytes 524288 | tf_op jit(solution)/shard_map/all_to_all | solution.py:549
  57.1 0.5 collective-permute-start.20
  57.6 0.1 collective-permute-start.23
  57.7 5.5 %query_grad.1.part_hbm = f32[128,512]{1,0:T(8,128)} custom-call(s32[133]{0:T(256)} %copy-done.14, bf16[4,128,256]{2,1,0:T(8,128)(2,1)} %get-tuple-element.27.stack_ref.stack_hbm, bf16[4,128,256]{2,1,0:T(8,128)(2,1)} %get-tuple-element.34.cot_stack_hbm, f32[32,16,128]{2,1,0:T(8,128)} %get-tuple-element.35.stats_hbm, ...), custom_call_target="tpu_custom_call" | custom-call | flops 1000000000 | bytes 4000000 | tf_op jit(solution)/shard_map/query_grad/pallas_call | solution.py:551
  63.2 4.5 %all-to-all-done.stats_all_ref = f32[32,16,128]{2,1,0:T(8,128)S(1)} async-done(((f32[32,16,128]{2,1,0:T(8,128)}), f32[32,16,128]{2,1,0:T(8,128)S(1)}, u32[]{:S(2)}, u32[]{:S(2)}) %all-to-all-start) | async-done | bytes 262176 | tf_op jit(solution)/shard_map/all_to_all | solution.py:549
  67.7 0.1 collective-permute-start.21
  67.9 0.0 collective-permute-done.22.refs_13_
  67.9 0.4 collective-permute-start.24
  68.3 0.0 collective-permute-done.20.refs_10_
  68.3 0.0 collective-permute-done.23.refs_14_
  68.3 1.6 %collective-permute-done.21.refs_11_ = bf16[8,64,512]{2,1,0:T(8,128)(2,1)S(1)} collective-permute-done((bf16[8,64,512]{2,1,0:T(8,128)(2,1)}, bf16[8,64,512]{2,1,0:T(8,128)(2,1)S(1)}, u32[]{:S(2)}, u32[]{:S(2)}) %collective-permute-start.21) | collective-permute-done | bytes 524320 | tf_op jit(solution)/shard_map/ppermute | solution.py:415
  69.9 0.7 collective-permute-done.24.refs_15_
  70.6 0.1 copy-done.22
  70.7 0.8 %copy-done.23 = bf16[8,64,512]{2,1,0:T(8,128)(2,1)} copy-done((bf16[8,64,512]{2,1,0:T(8,128)(2,1)}, bf16[8,64,512]{2,1,0:T(8,128)(2,1)S(1)}, u32[]{:S(2)}) %copy-start.23) | copy-done | bytes 524312
  71.5 5.8 %key_grad.1 = bf16[128,512]{1,0:T(8,128)(2,1)} custom-call(s32[69]{0:T(128)} %copy-done.15, bf16[128,512]{1,0:T(8,128)(2,1)} %get-tuple-element.31.key_hbm, bf16[128,512]{1,0:T(8,128)(2,1)} %get-tuple-element.32.value_hbm, bf16[512,512]{1,0:T(8,128)(2,1)} %wq_hbm.3, bf16[512,512]{1,0:T(8,128)(2,1)} %get-tuple-element.33.wkt_hbm, ...), custom_call_target="tpu_custom_call" | custom-call | flops 1000000000 | bytes 4000000 | tf_op jit(solution)/shard_map/key_grad/pallas_call | solution.py:570
  (67 shorter events, 0.3 us)
Async XLA Ops:
  1.3 6.2 %copy-start.11 = (bf16[128,512]{1,0:T(8,128)(2,1)S(1)}, bf16[128,512]{1,0:T(8,128)(2,1)}, u32[]{:S(2)}) copy-start(bf16[128,512]{1,0:T(8,128)(2,1)} %cot_ref.1) | copy-start | bytes 393220
  2.9 7.1 %copy-start.19 = (bf16[1,144,512]{2,1,0:T(8,128)(2,1)S(1)}, bf16[1,144,512]{2,1,0:T(8,128)(2,1)}, u32[]{:S(2)}) copy-start(bf16[1,144,512]{2,1,0:T(8,128)(2,1)} %pack.1) | copy-start | bytes 442372
  2.9 10.5 %collective-permute-start.2 = (bf16[1,144,512]{2,1,0:T(8,128)(2,1)}, bf16[1,144,512]{2,1,0:T(8,128)(2,1)S(1)}, u32[]{:S(2)}, u32[]{:S(2)}) collective-permute-start(bf16[1,144,512]{2,1,0:T(8,128)(2,1)} %pack.1), channel_id=1, source_target_pairs={{0,6},{1,7},{2,4},{3,5},{4,2},{5,3},{6,0},{7,1},{8,14},{9,15},{10,... | collective-permute-start | bytes 442376 | tf_op jit(solution)/shard_map/ppermute | solution.py:415
  7.2 12.3 %collective-permute-start.1 = (bf16[1,144,512]{2,1,0:T(8,128)(2,1)}, bf16[1,144,512]{2,1,0:T(8,128)(2,1)S(1)}, u32[]{:S(2)}, u32[]{:S(2)}) collective-permute-start(bf16[1,144,512]{2,1,0:T(8,128)(2,1)} %pack.1), channel_id=1, source_target_pairs={{0,4},{1,5},{2,6},{3,7},{4,0},{5,1},{6,2},{7,3},{8,12},{9,13},{10,... | collective-permute-start | bytes 442376 | tf_op jit(solution)/shard_map/ppermute | solution.py:415
  7.2 12.3 %collective-permute-start = (bf16[1,144,512]{2,1,0:T(8,128)(2,1)}, bf16[1,144,512]{2,1,0:T(8,128)(2,1)S(1)}, u32[]{:S(2)}, u32[]{:S(2)}) collective-permute-start(bf16[1,144,512]{2,1,0:T(8,128)(2,1)} %pack.1), channel_id=1, source_target_pairs={{0,2},{1,3},{2,0},{3,1},{4,6},{5,7},{6,4},{7,5},{8,10},{9,11},{10,... | collective-permute-start | bytes 442376 | tf_op jit(solution)/shard_map/ppermute | solution.py:415
  7.5 3.5 %collective-permute-start.3 = (bf16[1,64,512]{2,1,0:T(8,128)(2,1)S(1)}, bf16[1,64,512]{2,1,0:T(8,128)(2,1)S(1)}, u32[]{:S(2)}, u32[]{:S(2)}) collective-permute-start(bf16[1,64,512]{2,1,0:T(8,128)(2,1)S(1)} %get-tuple-element.52), channel_id=1, source_target_pairs={{0,8},{1,9},{2,10},{3,11},{4,12},{5,13},{6,14},{7,15},{8,0},{9,1},... | collective-permute-start | bytes 196616 | tf_op jit(solution)/shard_map/ppermute | solution.py:415
  8.8 4.4 %collective-permute-start.4 = (bf16[1,64,512]{2,1,0:T(8,128)(2,1)S(1)}, bf16[1,64,512]{2,1,0:T(8,128)(2,1)S(1)}, u32[]{:S(2)}, u32[]{:S(2)}) collective-permute-start(bf16[1,64,512]{2,1,0:T(8,128)(2,1)S(1)} %get-tuple-element.53), channel_id=1, source_target_pairs={{0,16},{1,17},{2,18},{3,19},{4,20},{5,21},{6,22},{7,23},{8,24},{9,... | collective-permute-start | bytes 196616 | tf_op jit(solution)/shard_map/ppermute | solution.py:415
  11.0 8.5 %collective-permute-start.7 = (bf16[1,144,512]{2,1,0:T(8,128)(2,1)S(1)}, bf16[1,144,512]{2,1,0:T(8,128)(2,1)S(1)}, u32[]{:S(2)}, u32[]{:S(2)}) collective-permute-start(bf16[1,144,512]{2,1,0:T(8,128)(2,1)S(1)} %copy-done.19), channel_id=1, source_target_pairs={{0,24},{1,25},{2,26},{3,27},{4,28},{5,29},{6,30},{7,31},{8,16},{9,... | collective-permute-start | bytes 442376 | tf_op jit(solution)/shard_map/ppermute | solution.py:415
  13.2 6.3 %collective-permute-start.6 = (bf16[1,144,512]{2,1,0:T(8,128)(2,1)S(1)}, bf16[1,144,512]{2,1,0:T(8,128)(2,1)S(1)}, u32[]{:S(2)}, u32[]{:S(2)}) collective-permute-start(bf16[1,144,512]{2,1,0:T(8,128)(2,1)S(1)} %copy-done.19), channel_id=1, source_target_pairs={{0,16},{1,17},{2,18},{3,19},{4,20},{5,21},{6,22},{7,23},{8,24},{9,... | collective-permute-start | bytes 442376 | tf_op jit(solution)/shard_map/ppermute | solution.py:415
  13.5 6.0 %collective-permute-start.5 = (bf16[1,144,512]{2,1,0:T(8,128)(2,1)S(1)}, bf16[1,144,512]{2,1,0:T(8,128)(2,1)S(1)}, u32[]{:S(2)}, u32[]{:S(2)}) collective-permute-start(bf16[1,144,512]{2,1,0:T(8,128)(2,1)S(1)} %copy-done.19), channel_id=1, source_target_pairs={{0,8},{1,9},{2,10},{3,11},{4,12},{5,13},{6,14},{7,15},{8,0},{9,1},... | collective-permute-start | bytes 442376 | tf_op jit(solution)/shard_map/ppermute | solution.py:415
  19.5 17.3 %collective-permute-start.13 = (bf16[4,64,512]{2,1,0:T(8,128)(2,1)S(1)}, bf16[4,64,512]{2,1,0:T(8,128)(2,1)S(1)}, u32[]{:S(2)}, u32[]{:S(2)}) collective-permute-start(bf16[4,64,512]{2,1,0:T(8,128)(2,1)S(1)} %pad_maximum_fusion.4), channel_id=1, source_target_pairs={{0,2},{1,3},{2,0},{3,1},{4,6},{5,7},{6,4},{7,5},{8,10},{9,11},{10,... | collective-permute-start | bytes 786440 | tf_op jit(solution)/shard_map/ppermute | solution.py:415
  21.5 14.1 %collective-permute-start.8 = (bf16[4,64,512]{2,1,0:T(8,128)(2,1)S(1)}, bf16[4,64,512]{2,1,0:T(8,128)(2,1)S(1)}, u32[]{:S(2)}, u32[]{:S(2)}) collective-permute-start(bf16[4,64,512]{2,1,0:T(8,128)(2,1)S(1)} %pad_maximum_fusion.4), channel_id=1, source_target_pairs={{0,4},{1,5},{2,6},{3,7},{4,0},{5,1},{6,2},{7,3},{8,12},{9,13},{10,... | collective-permute-start | bytes 786440 | tf_op jit(solution)/shard_map/ppermute | solution.py:415
  21.9 17.5 %collective-permute-start.12 = (bf16[3,128,512]{2,1,0:T(8,128)(2,1)S(1)}, bf16[3,128,512]{2,1,0:T(8,128)(2,1)S(1)}, u32[]{:S(2)}, u32[]{:S(2)}) collective-permute-start(bf16[3,128,512]{2,1,0:T(8,128)(2,1)S(1)} %pad_maximum_fusion.2), channel_id=1, source_target_pairs={{0,24},{1,25},{2,26},{3,27},{4,28},{5,29},{6,30},{7,31},{8,16},{9,... | collective-permute-start | bytes 1179656 | tf_op jit(solution)/shard_map/ppermute | solution.py:415
  24.1 17.4 %collective-permute-start.11 = (bf16[3,128,512]{2,1,0:T(8,128)(2,1)S(1)}, bf16[3,128,512]{2,1,0:T(8,128)(2,1)S(1)}, u32[]{:S(2)}, u32[]{:S(2)}) collective-permute-start(bf16[3,128,512]{2,1,0:T(8,128)(2,1)S(1)} %pad_maximum_fusion.2), channel_id=1, source_target_pairs={{0,16},{1,17},{2,18},{3,19},{4,20},{5,21},{6,22},{7,23},{8,24},{9,... | collective-permute-start | bytes 1179656 | tf_op jit(solution)/shard_map/ppermute | solution.py:415
  24.3 18.5 %collective-permute-start.10 = (bf16[3,128,512]{2,1,0:T(8,128)(2,1)S(1)}, bf16[3,128,512]{2,1,0:T(8,128)(2,1)S(1)}, u32[]{:S(2)}, u32[]{:S(2)}) collective-permute-start(bf16[3,128,512]{2,1,0:T(8,128)(2,1)S(1)} %pad_maximum_fusion.2), channel_id=1, source_target_pairs={{0,8},{1,9},{2,10},{3,11},{4,12},{5,13},{6,14},{7,15},{8,0},{9,1},... | collective-permute-start | bytes 1179656 | tf_op jit(solution)/shard_map/ppermute | solution.py:415
  25.0 22.4 %copy-start = (bf16[7,128,512]{2,1,0:T(8,128)(2,1)}, bf16[7,128,512]{2,1,0:T(8,128)(2,1)S(1)}, u32[]{:S(2)}) copy-start(bf16[7,128,512]{2,1,0:T(8,128)(2,1)S(1)} %constant_dynamic-update-slice_fusion.refs_0_) | copy-start | bytes 2752516
  30.0 0.5 copy-start.15
  35.6 2.0 %collective-permute-start.9 = (bf16[4,16,128]{2,1,0:T(8,128)(2,1)S(1)}, bf16[4,16,128]{2,1,0:T(8,128)(2,1)S(1)}, u32[]{:S(2)}, u32[]{:S(2)}) collective-permute-start(bf16[4,16,128]{2,1,0:T(8,128)(2,1)S(1)} %pad_maximum_fusion.5), channel_id=1, source_target_pairs={{0,1},{1,0},{2,3},{3,2},{4,5},{5,4},{6,7},{7,6},{8,9},{9,8},{10,11... | collective-permute-start | bytes 49160 | tf_op jit(solution)/shard_map/ppermute | solution.py:415
  36.8 10.6 %collective-permute-start.14 = (bf16[7,128,512]{2,1,0:T(8,128)(2,1)S(1)}, bf16[7,128,512]{2,1,0:T(8,128)(2,1)S(1)}, u32[]{:S(2)}, u32[]{:S(2)}) collective-permute-start(bf16[7,128,512]{2,1,0:T(8,128)(2,1)S(1)} %constant_dynamic-update-slice_fusion.refs_0_), channel_id=1, source_target_pairs={{0,1},{1,0},{2,3},{3,2},{4,5},{5,4},{6,7},{7,6},{8,9},{9,8},{10,11... | collective-permute-start | bytes 2752520 | tf_op jit(solution)/shard_map/ppermute | solution.py:415
  37.6 7.5 %collective-permute-start.18 = (bf16[4,64,512]{2,1,0:T(8,128)(2,1)S(1)}, bf16[4,64,512]{2,1,0:T(8,128)(2,1)S(1)}, u32[]{:S(2)}, u32[]{:S(2)}) collective-permute-start(bf16[4,64,512]{2,1,0:T(8,128)(2,1)S(1)} %collective-permute-done.8), channel_id=1, source_target_pairs={{0,2},{1,3},{2,0},{3,1},{4,6},{5,7},{6,4},{7,5},{8,10},{9,11},{10,... | collective-permute-start | bytes 786440 | tf_op jit(solution)/shard_map/ppermute | solution.py:415
  39.4 8.0 %copy-start.14 = (s32[133]{0:T(256)}, s32[133]{0:T(256)S(1)}, u32[]{:S(2)}) copy-start(s32[133]{0:T(256)S(1)} %query_work.1.work_ref) | copy-start | bytes 1600
  39.4 8.0 %copy-start.4 = (bf16[3,128,512]{2,1,0:T(8,128)(2,1)}, bf16[3,128,512]{2,1,0:T(8,128)(2,1)S(1)}, u32[]{:S(2)}) copy-start(bf16[3,128,512]{2,1,0:T(8,128)(2,1)S(1)} %collective-permute-done.12.refs_3_) | copy-start | bytes 1179652
  39.4 6.7 %collective-permute-start.17 = (bf16[3,128,512]{2,1,0:T(8,128)(2,1)S(1)}, bf16[3,128,512]{2,1,0:T(8,128)(2,1)S(1)}, u32[]{:S(2)}, u32[]{:S(2)}) collective-permute-start(bf16[3,128,512]{2,1,0:T(8,128)(2,1)S(1)} %collective-permute-done.12.refs_3_), channel_id=1, source_target_pairs={{0,1},{1,0},{2,3},{3,2},{4,5},{5,4},{6,7},{7,6},{8,9},{9,8},{10,11... | collective-permute-start | bytes 1179656 | tf_op jit(solution)/shard_map/ppermute | solution.py:415
  41.5 5.9 %copy-start.5 = (bf16[3,128,512]{2,1,0:T(8,128)(2,1)}, bf16[3,128,512]{2,1,0:T(8,128)(2,1)S(1)}, u32[]{:S(2)}) copy-start(bf16[3,128,512]{2,1,0:T(8,128)(2,1)S(1)} %collective-permute-done.11.refs_2_) | copy-start | bytes 1179652
  41.5 5.9 %collective-permute-start.16 = (bf16[3,128,512]{2,1,0:T(8,128)(2,1)S(1)}, bf16[3,128,512]{2,1,0:T(8,128)(2,1)S(1)}, u32[]{:S(2)}, u32[]{:S(2)}) collective-permute-start(bf16[3,128,512]{2,1,0:T(8,128)(2,1)S(1)} %collective-permute-done.11.refs_2_), channel_id=1, source_target_pairs={{0,1},{1,0},{2,3},{3,2},{4,5},{5,4},{6,7},{7,6},{8,9},{9,8},{10,11... | collective-permute-start | bytes 1179656 | tf_op jit(solution)/shard_map/ppermute | solution.py:415
  42.8 4.7 %copy-start.6 = (bf16[3,128,512]{2,1,0:T(8,128)(2,1)}, bf16[3,128,512]{2,1,0:T(8,128)(2,1)S(1)}, u32[]{:S(2)}) copy-start(bf16[3,128,512]{2,1,0:T(8,128)(2,1)S(1)} %collective-permute-done.10.refs_1_) | copy-start | bytes 1179652
  42.8 4.6 %collective-permute-start.15 = (bf16[3,128,512]{2,1,0:T(8,128)(2,1)S(1)}, bf16[3,128,512]{2,1,0:T(8,128)(2,1)S(1)}, u32[]{:S(2)}, u32[]{:S(2)}) collective-permute-start(bf16[3,128,512]{2,1,0:T(8,128)(2,1)S(1)} %collective-permute-done.10.refs_1_), channel_id=1, source_target_pairs={{0,1},{1,0},{2,3},{3,2},{4,5},{5,4},{6,7},{7,6},{8,9},{9,8},{10,11... | collective-permute-start | bytes 1179656 | tf_op jit(solution)/shard_map/ppermute | solution.py:415
  45.2 2.2 %copy-start.10 = (bf16[512,512]{1,0:T(8,128)(2,1)S(1)}, bf16[512,512]{1,0:T(8,128)(2,1)}, u32[]{:S(2)}) copy-start(bf16[512,512]{1,0:T(8,128)(2,1)} %get-tuple-element.28.wvt_ref.wvt_hbm) | copy-start | bytes 1572868
  45.2 2.2 %copy-start.12 = (bf16[128,512]{1,0:T(8,128)(2,1)S(1)}, bf16[128,512]{1,0:T(8,128)(2,1)}, u32[]{:S(2)}) copy-start(bf16[128,512]{1,0:T(8,128)(2,1)} %cot_ref.1) | copy-start | bytes 393220
  45.2 2.2 %copy-start.13 = (bf16[4,128,256]{2,1,0:T(8,128)(2,1)S(1)}, bf16[4,128,256]{2,1,0:T(8,128)(2,1)}, u32[]{:S(2)}) copy-start(bf16[4,128,256]{2,1,0:T(8,128)(2,1)} %get-tuple-element.27.stack_ref.stack_hbm) | copy-start | bytes 786436
  45.3 12.3 %copy-start.16 = (bf16[8,64,512]{2,1,0:T(8,128)(2,1)}, bf16[8,64,512]{2,1,0:T(8,128)(2,1)S(1)}, u32[]{:S(2)}) copy-start(bf16[8,64,512]{2,1,0:T(8,128)(2,1)S(1)} %pad_maximum_fusion.1.refs_12_) | copy-start | bytes 1572868
  45.3 2.2 %copy-start.2 = (bf16[512,512]{1,0:T(8,128)(2,1)S(1)}, bf16[512,512]{1,0:T(8,128)(2,1)}, u32[]{:S(2)}) copy-start(bf16[512,512]{1,0:T(8,128)(2,1)} %wk_hbm.3) | copy-start | bytes 1572868
  45.3 2.2 %copy-start.3 = (s32[240,128,4]{1,2,0:T(4,128)S(1)}, s32[240,128,4]{1,2,0:T(4,128)}, u32[]{:S(2)}) copy-start(s32[240,128,4]{1,2,0:T(4,128)} %param.15) | copy-start | bytes 1474564
  45.4 11.7 %copy-start.17 = (bf16[8,64,512]{2,1,0:T(8,128)(2,1)}, bf16[8,64,512]{2,1,0:T(8,128)(2,1)S(1)}, u32[]{:S(2)}) copy-start(bf16[8,64,512]{2,1,0:T(8,128)(2,1)S(1)} %pad_maximum_fusion.refs_8_) | copy-start | bytes 1572868
  45.4 17.8 %collective-permute-start.19 = (bf16[8,64,512]{2,1,0:T(8,128)(2,1)S(1)}, bf16[8,64,512]{2,1,0:T(8,128)(2,1)}, u32[]{:S(2)}, u32[]{:S(2)}) collective-permute-start(bf16[8,64,512]{2,1,0:T(8,128)(2,1)S(1)} %pad_maximum_fusion.refs_8_), channel_id=1, source_target_pairs={{0,16},{1,17},{2,18},{3,19},{4,20},{5,21},{6,22},{7,23},{8,24},{9,... | collective-permute-start | bytes 1572872 | tf_op jit(solution)/shard_map/ppermute | solution.py:415
  46.1 5.6 %copy-start.7 = (bf16[3,128,512]{2,1,0:T(8,128)(2,1)}, bf16[3,128,512]{2,1,0:T(8,128)(2,1)S(1)}, u32[]{:S(2)}) copy-start(bf16[3,128,512]{2,1,0:T(8,128)(2,1)S(1)} %collective-permute-done.17.refs_7_) | copy-start | bytes 1179652
  46.1 21.7 %collective-permute-start.22 = (bf16[8,64,512]{2,1,0:T(8,128)(2,1)S(1)}, bf16[8,64,512]{2,1,0:T(8,128)(2,1)}, u32[]{:S(2)}, u32[]{:S(2)}) collective-permute-start(bf16[8,64,512]{2,1,0:T(8,128)(2,1)S(1)} %pad_maximum_fusion.1.refs_12_), channel_id=1, source_target_pairs={{0,8},{1,9},{2,10},{3,11},{4,12},{5,13},{6,14},{7,15},{8,0},{9,1},... | collective-permute-start | bytes 1572872 | tf_op jit(solution)/shard_map/ppermute | solution.py:415
  47.3 4.4 %copy-start.8 = (bf16[3,128,512]{2,1,0:T(8,128)(2,1)}, bf16[3,128,512]{2,1,0:T(8,128)(2,1)S(1)}, u32[]{:S(2)}) copy-start(bf16[3,128,512]{2,1,0:T(8,128)(2,1)S(1)} %collective-permute-done.16.refs_6_) | copy-start | bytes 1179652
  47.4 4.4 %copy-start.9 = (bf16[3,128,512]{2,1,0:T(8,128)(2,1)}, bf16[3,128,512]{2,1,0:T(8,128)(2,1)S(1)}, u32[]{:S(2)}) copy-start(bf16[3,128,512]{2,1,0:T(8,128)(2,1)S(1)} %collective-permute-done.15.refs_5_) | copy-start | bytes 1179652
  47.4 4.4 %copy-start.1 = (bf16[7,128,512]{2,1,0:T(8,128)(2,1)}, bf16[7,128,512]{2,1,0:T(8,128)(2,1)S(1)}, u32[]{:S(2)}) copy-start(bf16[7,128,512]{2,1,0:T(8,128)(2,1)S(1)} %collective-permute-done.14.refs_4_) | copy-start | bytes 2752516
  51.8 16.0 %all-to-all-start = ((f32[32,16,128]{2,1,0:T(8,128)}), f32[32,16,128]{2,1,0:T(8,128)S(1)}, u32[]{:S(2)}, u32[]{:S(2)}) async-start(f32[32,16,128]{2,1,0:T(8,128)} %get-tuple-element.35.stats_hbm), calls=%async_computation | async-start | bytes 524288 | tf_op jit(solution)/shard_map/all_to_all | solution.py:549
  57.1 11.2 %collective-permute-start.20 = (bf16[8,64,512]{2,1,0:T(8,128)(2,1)S(1)}, bf16[8,64,512]{2,1,0:T(8,128)(2,1)S(1)}, u32[]{:S(2)}, u32[]{:S(2)}) collective-permute-start(bf16[8,64,512]{2,1,0:T(8,128)(2,1)S(1)} %pad_maximum_fusion.refs_8_), channel_id=1, source_target_pairs={{0,1},{1,0},{2,3},{3,2},{4,5},{5,4},{6,7},{7,6},{8,9},{9,8},{10,11... | collective-permute-start | bytes 1572872 | tf_op jit(solution)/shard_map/ppermute | solution.py:415
  57.6 10.7 %collective-permute-start.23 = (bf16[8,64,512]{2,1,0:T(8,128)(2,1)S(1)}, bf16[8,64,512]{2,1,0:T(8,128)(2,1)S(1)}, u32[]{:S(2)}, u32[]{:S(2)}) collective-permute-start(bf16[8,64,512]{2,1,0:T(8,128)(2,1)S(1)} %pad_maximum_fusion.1.refs_12_), channel_id=1, source_target_pairs={{0,1},{1,0},{2,3},{3,2},{4,5},{5,4},{6,7},{7,6},{8,9},{9,8},{10,11... | collective-permute-start | bytes 1572872 | tf_op jit(solution)/shard_map/ppermute | solution.py:415
  67.7 2.9 %copy-start.18 = (f32[32,16,128]{2,1,0:T(8,128)}, f32[32,16,128]{2,1,0:T(8,128)S(1)}, u32[]{:S(2)}) copy-start(f32[32,16,128]{2,1,0:T(8,128)S(1)} %all-to-all-done.stats_all_ref) | copy-start | bytes 786436
  67.7 2.1 %collective-permute-start.21 = (bf16[8,64,512]{2,1,0:T(8,128)(2,1)}, bf16[8,64,512]{2,1,0:T(8,128)(2,1)S(1)}, u32[]{:S(2)}, u32[]{:S(2)}) collective-permute-start(bf16[8,64,512]{2,1,0:T(8,128)(2,1)} %collective-permute-done.19.refs_9_), channel_id=1, source_target_pairs={{0,1},{1,0},{2,3},{3,2},{4,5},{5,4},{6,7},{7,6},{8,9},{9,8},{10,11... | collective-permute-start | bytes 1572872 | tf_op jit(solution)/shard_map/ppermute | solution.py:415
  67.9 2.7 %collective-permute-start.24 = (bf16[8,64,512]{2,1,0:T(8,128)(2,1)}, bf16[8,64,512]{2,1,0:T(8,128)(2,1)S(1)}, u32[]{:S(2)}, u32[]{:S(2)}) collective-permute-start(bf16[8,64,512]{2,1,0:T(8,128)(2,1)} %collective-permute-done.22.refs_13_), channel_id=1, source_target_pairs={{0,1},{1,0},{2,3},{3,2},{4,5},{5,4},{6,7},{7,6},{8,9},{9,8},{10,11... | collective-permute-start | bytes 1572872 | tf_op jit(solution)/shard_map/ppermute | solution.py:415
  68.3 2.4 %copy-start.20 = (bf16[8,64,512]{2,1,0:T(8,128)(2,1)}, bf16[8,64,512]{2,1,0:T(8,128)(2,1)S(1)}, u32[]{:S(2)}) copy-start(bf16[8,64,512]{2,1,0:T(8,128)(2,1)S(1)} %collective-permute-done.20.refs_10_) | copy-start | bytes 1572868
  68.3 2.4 %copy-start.21 = (bf16[8,64,512]{2,1,0:T(8,128)(2,1)}, bf16[8,64,512]{2,1,0:T(8,128)(2,1)S(1)}, u32[]{:S(2)}) copy-start(bf16[8,64,512]{2,1,0:T(8,128)(2,1)S(1)} %collective-permute-done.23.refs_14_) | copy-start | bytes 1572868
  69.9 0.8 %copy-start.22 = (bf16[8,64,512]{2,1,0:T(8,128)(2,1)}, bf16[8,64,512]{2,1,0:T(8,128)(2,1)S(1)}, u32[]{:S(2)}) copy-start(bf16[8,64,512]{2,1,0:T(8,128)(2,1)S(1)} %collective-permute-done.21.refs_11_) | copy-start | bytes 1572868
  70.7 0.8 %copy-start.23 = (bf16[8,64,512]{2,1,0:T(8,128)(2,1)}, bf16[8,64,512]{2,1,0:T(8,128)(2,1)S(1)}, u32[]{:S(2)}) copy-start(bf16[8,64,512]{2,1,0:T(8,128)(2,1)S(1)} %collective-permute-done.24.refs_15_) | copy-start | bytes 1572868
